TPU v7x, 128 devices: a whole 4x4x4 slice. The times are simulated.
128 devices in a mesh: dp: 4 (over x), head: 2 (over z_hi), ctx: 16 (over z_lo, y, core).
Axes of the slice: x: 4, y: 4, z: 4 (z_hi: 2, z_lo: 2; z = z_hi * 2 + z_lo), core: 2. Of those that a mesh axis runs over, the one named last changes fastest.
Arguments:
- query_input: bfloat16 [4, 3072, 2560], P('dp', 'ctx', 'head'), may hold values from -2700 to 2700
- key_input: bfloat16 [4, 3072, 2560], P('dp', 'ctx', 'head'), may hold values from -2700 to 2700
- value_input: bfloat16 [4, 3072, 2560], P('dp', 'ctx', 'head'), may hold values from -6 to 6
- query_tangent: bfloat16 [4, 3072, 2560], P('dp', 'ctx', 'head'), may hold values from -2700 to 2700
- key_tangent: bfloat16 [4, 3072, 2560], P('dp', 'ctx', 'head'), may hold values from -2700 to 2700
- value_tangent: bfloat16 [4, 3072, 2560], P('dp', 'ctx', 'head'), may hold values from -6 to 6
- query_gain: float32 [2560], P('head'), may hold values from 0.8 to 2
- key_gain: float32 [2560], P('head'), may hold values from 0.8 to 2
- out_weight: bfloat16 [2560, 5120], P('head', 'dp'), may hold values from -0.125 to 0.125
- span_order: int32 [32], replicated, may hold values from 0 to 31, each once
Outputs:
- projected: bfloat16 [4, 3072, 5120], P('dp', 'ctx', 'head')
- projected_tangent: bfloat16 [4, 3072, 5120], P('dp', 'ctx', 'head')
Inputs may be any that keep to these rules, and one draw needn't show every extreme that they name: `span_order`: each span number appears once.
All inputs are finite; a program needn't handle non-finite values.
Results may differ from a plain program's by a relative error of at most 0.006.
The roundings to bfloat16 on the way count: a program that leaves them out, or rounds other values in their place, can miss the bound.
Values may be sent and summed in bfloat16 or wider, within the bound.
No kernel may reach another device: no remote copies, remote signals or barrier semaphores. Data moves between devices by JAX's collectives and lax.ppermute only.
A program may use at most 128 MiB of HBM per device.

v0:
```python
import math

import jax
import jax.numpy as jnp
from jax import lax
from jax.sharding import PartitionSpec as P

HEAD_DIM = 128
GRID_H = 8
GRID_W = 16
CAP = 30
HD = 2560


def rope_angles(positions):
    pair_count = HEAD_DIM // 2
    side_pairs = pair_count // 3
    time_pairs = pair_count - 2 * side_pairs
    frame_index = (positions // (GRID_H * GRID_W)).astype(jnp.float32)
    grid_row = (positions // GRID_W % GRID_H).astype(jnp.float32)
    grid_column = (positions % GRID_W).astype(jnp.float32)
    time_freq = 10000.0 ** (-jnp.arange(time_pairs, dtype=jnp.float32) / time_pairs)
    side_freq = 10000.0 ** (-jnp.arange(side_pairs, dtype=jnp.float32) / side_pairs)
    angle_table = jnp.concatenate(
        [
            frame_index[:, None] * time_freq[None, :],
            grid_row[:, None] * side_freq[None, :],
            grid_column[:, None] * side_freq[None, :],
        ],
        axis=1,
    )
    angle_table = jnp.repeat(angle_table, 2, axis=1)
    return (jnp.cos(angle_table), jnp.sin(angle_table))


def partner(features):
    parity = jnp.arange(features.shape[-1]) % 2 == 0
    return jnp.where(parity, -jnp.roll(features, -1, axis=-1), jnp.roll(features, 1, axis=-1))


def norm_rope(raw_rows, tangent_rows, square_sum, mixed_sum, gain_row, cosine_table, sine_table):
    inverse = lax.rsqrt(square_sum / HD + 1e-06)[..., None, None]
    mixing = (mixed_sum / HD)[..., None, None]
    head_gain = gain_row.reshape(-1, HEAD_DIM)
    normed = head_gain * raw_rows * inverse
    normed_tangent = head_gain * (
        tangent_rows * inverse - raw_rows * mixing * inverse * inverse * inverse
    )
    cosine_wide = cosine_table[:, None, :]
    sine_wide = sine_table[:, None, :]
    turned = normed * cosine_wide + partner(normed) * sine_wide
    turned_tangent = normed_tangent * cosine_wide + partner(normed_tangent) * sine_wide
    return (turned.astype(jnp.bfloat16), turned_tangent.astype(jnp.bfloat16))


def attend(
    running, queries, queries_tangent, key_rows, value_rows, key_rows_tangent, value_rows_tangent
):
    score_scale = 1.0 / math.sqrt(HEAD_DIM)
    scores = (
        jnp.einsum("qhd,khd->hqk", queries, key_rows, preferred_element_type=jnp.float32)
        * score_scale
    )
    scores_tangent = (
        jnp.einsum("qhd,khd->hqk", queries_tangent, key_rows, preferred_element_type=jnp.float32)
        + jnp.einsum("qhd,khd->hqk", queries, key_rows_tangent, preferred_element_type=jnp.float32)
    ) * score_scale
    squashed = jnp.tanh(scores / CAP)
    weights = jnp.exp(CAP * squashed)
    weights_tangent = weights * ((1.0 - squashed * squashed) * scores_tangent)
    weights_low = weights.astype(jnp.bfloat16)
    weights_low_tangent = weights_tangent.astype(jnp.bfloat16)
    norm_sum = running[0] + jnp.sum(weights, axis=-1)
    tangent_sum = running[1] + jnp.sum(weights_tangent, axis=-1)
    weighted = running[2] + jnp.einsum(
        "hqk,khd->qhd", weights_low, value_rows, preferred_element_type=jnp.float32
    )
    weighted_tangent = running[3] + (
        jnp.einsum(
            "hqk,khd->qhd", weights_low, value_rows_tangent, preferred_element_type=jnp.float32
        )
        + jnp.einsum(
            "hqk,khd->qhd", weights_low_tangent, value_rows, preferred_element_type=jnp.float32
        )
    )
    return (norm_sum, tangent_sum, weighted, weighted_tangent)


def pick_block(key_count):
    for candidate in (512, 384, 256, 192, 128):
        return candidate
    return key_count


def on_device(
    query_input,
    key_input,
    value_input,
    query_tangent,
    key_tangent,
    value_tangent,
    query_gain,
    key_gain,
    out_weight,
    span_order,
):
    row_count = query_input.shape[1]
    feature_count = query_input.shape[2]
    head_count = feature_count // HEAD_DIM
    span_rows = row_count // 2
    cycle_index = lax.axis_index("ctx")
    own_spans = lax.dynamic_slice_in_dim(span_order, 2 * cycle_index, 2)
    positions = (
        own_spans[:, None] * span_rows + jnp.arange(span_rows, dtype=jnp.int32)[None, :]
    ).reshape(-1)
    cosine_table, sine_table = rope_angles(positions)
    query_float = query_input[0].astype(jnp.float32)
    query_tangent_float = query_tangent[0].astype(jnp.float32)
    key_float = key_input[0].astype(jnp.float32)
    key_tangent_float = key_tangent[0].astype(jnp.float32)
    statistics = lax.psum(
        (
            jnp.sum(query_float * query_float, axis=-1),
            jnp.sum(query_float * query_tangent_float, axis=-1),
            jnp.sum(key_float * key_float, axis=-1),
            jnp.sum(key_float * key_tangent_float, axis=-1),
        ),
        "head",
    )
    head_shape = (row_count, head_count, HEAD_DIM)
    query_turned, query_turned_tangent = norm_rope(
        query_float.reshape(head_shape),
        query_tangent_float.reshape(head_shape),
        statistics[0],
        statistics[1],
        query_gain,
        cosine_table,
        sine_table,
    )
    key_turned, key_turned_tangent = norm_rope(
        key_float.reshape(head_shape),
        key_tangent_float.reshape(head_shape),
        statistics[2],
        statistics[3],
        key_gain,
        cosine_table,
        sine_table,
    )
    flat_shape = (1, row_count, feature_count)
    zero_sums = jnp.zeros((head_count, row_count), jnp.float32)
    zero_rows = jnp.zeros(head_shape, jnp.float32)
    pieces = (
        lax.all_gather(key_turned.reshape(flat_shape), "ctx", axis=1, tiled=True),
        lax.all_gather(value_input, "ctx", axis=1, tiled=True),
        lax.all_gather(key_turned_tangent.reshape(flat_shape), "ctx", axis=1, tiled=True),
        lax.all_gather(value_tangent, "ctx", axis=1, tiled=True),
    )
    key_count = pieces[0].shape[1]
    blocks = [member[0].reshape(key_count, head_count, HEAD_DIM) for member in pieces]
    block_rows = pick_block(key_count)

    def one_block(block_index, partial_state):
        sliced = [
            lax.dynamic_slice_in_dim(member, block_index * block_rows, block_rows, 0)
            for member in blocks
        ]
        return attend(
            partial_state,
            query_turned,
            query_turned_tangent,
            sliced[0],
            sliced[1],
            sliced[2],
            sliced[3],
        )

    totals = lax.fori_loop(
        0, key_count // block_rows, one_block, (zero_sums, zero_sums, zero_rows, zero_rows)
    )
    norm_sum, tangent_sum, weighted, weighted_tangent = totals
    denominator = norm_sum.T[:, :, None]
    attention = weighted / denominator
    attention_tangent = (
        weighted_tangent / denominator - (tangent_sum / norm_sum).T[:, :, None] * attention
    )
    stacked = jnp.concatenate(
        [
            attention.astype(jnp.bfloat16).reshape(row_count, feature_count),
            attention_tangent.astype(jnp.bfloat16).reshape(row_count, feature_count),
        ],
        axis=0,
    )
    partial_sums = jnp.dot(
        stacked,
        lax.all_gather(out_weight, "dp", axis=1, tiled=True),
        preferred_element_type=jnp.float32,
    )
    combined = lax.psum_scatter(partial_sums, "head", scatter_dimension=1, tiled=True).astype(
        jnp.bfloat16
    )
    return (combined[:row_count][None], combined[row_count:][None])


def solution(mesh):
    return jax.shard_map(
        on_device,
        mesh=mesh,
        in_specs=(
            P("dp", "ctx", "head"),
            P("dp", "ctx", "head"),
            P("dp", "ctx", "head"),
            P("dp", "ctx", "head"),
            P("dp", "ctx", "head"),
            P("dp", "ctx", "head"),
            P("head"),
            P("head"),
            P("head", "dp"),
            P(),
        ),
        out_specs=(P("dp", "ctx", "head"), P("dp", "ctx", "head")),
        check_vma=False,
    )
```

profile of v0, /device:TPU:1, one launch (start us, length us, event | category | flops | bytes accessed | tf_op | source)
XLA Modules:
  0.0 494.3 jit_solution(16365217484482907753)
XLA Ops:
  7.8 1.3 copy.26
  10.5 6.7 %all-reduce = (f32[192]{0:T(256)S(1)}, f32[192]{0:T(256)S(1)}, f32[192]{0:T(256)S(1)}, f32[192]{0:T(256)S(1)}) all-reduce(f32[192]{0:T(256)S(1)} %get-tuple-element.332, f32[192]{0:T(256)S(1)} %get-tuple-element.334, f32[192]{0:T(256)S(1)} %get-tuple-element.333, ...), channel_id=1, replica_groups=mesh['dp'=4,'head'=2,'ctx'=16] {'head'}, use_global_device_ids=true, to_apply=%region_1.2 | all-reduce | flops 768 | bytes 6144 | tf_op jit(solution)/shard_map/psum | solution.py:121
  19.1 1.3 fusion.63
  20.5 1.7 fusion.57
  24.2 0.9 broadcast_in_dim.62
  25.9 1.4 maximum_negate_fusion
  27.5 1.2 copy-done.3
  28.8 1.2 copy-done.2
  30.6 1.1 fusion.34
  31.7 1.0 copy.32
  32.8 1.0 copy.27
  36.7 1.3 copy.29
  38.1 1.8 subtract_multiply_fusion.1
  40.8 1.2 fusion.42
  42.6 43.3 %all-gather.8.cloned.1.call-done = bf16[1,3072,1280]{2,1,0:T(8,128)(2,1)} async-done(((bf16[1,192,1280]{2,1,0:T(8,128)(2,1)}), bf16[1,3072,1280]{2,1,0:T(8,128)(2,1)}) %all-gather.8.cloned.1.call-update) | async-done | bytes 7864336 | tf_op jit(solution)/shard_map/all_gather | solution.py:155
  85.9 10.6 %copy.33 = bf16[1,3072,1280]{1,2,0:T(8,128)(2,1)} copy(bf16[1,3072,1280]{2,1,0:T(8,128)(2,1)} %all-gather.8.cloned.1.call-done) | data formatting | bytes 15728640 | tf_op jit(solution)/shard_map/all_gather | solution.py:155
  96.5 42.2 %all-gather.6.cloned.1.call-done = bf16[1,3072,1280]{2,1,0:T(8,128)(2,1)} async-done(((bf16[1,192,1280]{2,1,0:T(8,128)(2,1)}), bf16[1,3072,1280]{2,1,0:T(8,128)(2,1)}) %all-gather.6.cloned.1.call-update) | async-done | bytes 7864336 | tf_op jit(solution)/shard_map/all_gather | solution.py:153
  138.8 10.6 %copy.28 = bf16[1,3072,1280]{1,2,0:T(8,128)(2,1)} copy(bf16[1,3072,1280]{2,1,0:T(8,128)(2,1)} %all-gather.6.cloned.1.call-done) | data formatting | bytes 15728640 | tf_op jit(solution)/shard_map/all_gather | solution.py:153
  149.4 41.6 %all-gather.10.cloned.1.call-done = bf16[1,3072,1280]{2,1,0:T(8,128)(2,1)} async-done(((bf16[1,192,1280]{2,1,0:T(8,128)(2,1)}), bf16[1,3072,1280]{2,1,0:T(8,128)(2,1)}) %all-gather.10.cloned.1.call-update) | async-done | bytes 7864336 | tf_op jit(solution)/shard_map/all_gather | solution.py:154
  191.0 10.7 %copy.34 = bf16[1,3072,1280]{1,2,0:T(8,128)(2,1)} copy(bf16[1,3072,1280]{2,1,0:T(8,128)(2,1)} %all-gather.10.cloned.1.call-done) | data formatting | bytes 15728640 | tf_op jit(solution)/shard_map/all_gather | solution.py:154
  201.7 41.5 %all-gather.12.cloned.1.call-done = bf16[1,3072,1280]{2,1,0:T(8,128)(2,1)} async-done(((bf16[1,192,1280]{2,1,0:T(8,128)(2,1)}), bf16[1,3072,1280]{2,1,0:T(8,128)(2,1)}) %all-gather.12.cloned.1.call-update) | async-done | bytes 7864336 | tf_op jit(solution)/shard_map/all_gather | solution.py:156
  243.1 10.6 %copy.35 = bf16[1,3072,1280]{1,2,0:T(8,128)(2,1)} copy(bf16[1,3072,1280]{2,1,0:T(8,128)(2,1)} %all-gather.12.cloned.1.call-done) | data formatting | bytes 15728640 | tf_op jit(solution)/shard_map/all_gather | solution.py:156
  253.8 116.2 %while.22 = (s32[]{:T(128)}, f32[10,192]{1,0:T(8,128)S(1)}, f32[10,192]{1,0:T(8,128)S(1)}, f32[192,10,128]{2,0,1:T(8,128)}, f32[192,10,128]{2,0,1:T(8,128)S(1)},...) while((s32[]{:T(128)}, f32[10,192]{1,0:T(8,128)S(1)}, ...), condition=%wide.region_11.12_spmd.clone, body=%wide.region_8.11_spmd.clone.sunk | while | flops 1529859840 | bytes 78213464 | solution.py:177
  253.8 3.0 bitcast_reduce_fusion.2
  256.8 3.1 fusion.91
  259.9 3.5 fusion.92
  263.4 3.5 fusion.94
  267.0 2.6 fusion.95
  269.8 3.5 fusion.93
  273.3 2.8 bitcast_reduce_fusion.2
  276.2 3.0 fusion.91
  279.2 3.3 fusion.92
  282.5 3.5 fusion.94
  286.0 2.6 fusion.95
  288.8 3.9 fusion.93
  292.6 2.8 bitcast_reduce_fusion.2
  295.5 3.0 fusion.91
  298.5 3.4 fusion.92
  301.9 3.4 fusion.94
  305.3 2.6 fusion.95
  308.2 3.9 fusion.93
  312.0 2.8 bitcast_reduce_fusion.2
  314.9 3.0 fusion.91
  317.9 3.4 fusion.92
  321.3 3.4 fusion.94
  324.7 2.7 fusion.95
  327.6 3.8 fusion.93
  331.5 2.8 bitcast_reduce_fusion.2
  334.3 3.0 fusion.91
  337.3 3.3 fusion.92
  340.7 3.4 fusion.94
  344.1 2.6 fusion.95
  346.9 3.8 fusion.93
  350.7 2.8 bitcast_reduce_fusion.2
  353.5 3.0 fusion.91
  356.5 3.3 fusion.92
  359.9 3.4 fusion.94
  363.3 2.6 fusion.95
  366.1 3.8 fusion.93
  370.0 1.7 fusion.47
  372.2 12.5 %fusion.43 = f32[384,5120]{1,0:T(8,128)} fusion(bf16[1280,5120]{1,0:T(8,128)(2,1)} %all-gather.14.cloned.1.call-done, bf16[192,1280]{0,1:T(8,128)(2,1)S(1)} %bitcast.105, bf16[192,1280]{0,1:T(8,128)(2,1)S(1)} %bitcast.104), kind=kOutput, calls=%fused_computation.65 | convolution fusion | flops 5035130880 | bytes 21954560 | tf_op jit(solution)/shard_map/dot_general | solution.py:193
  384.8 99.0 %reduce-scatter.2.cloned.1.call-done = f32[384,2560]{1,0:T(8,128)} async-done(((f32[384,5120]{1,0:T(8,128)}), f32[384,2560]{1,0:T(8,128)}) %reduce-scatter.2.cloned.1.call-update) | async-done | bytes 3932176 | tf_op jit(solution)/shard_map/reduce_scatter | solution.py:198
  483.8 2.3 convert_element_type.128
  486.1 1.4 slice_bitcast_fusion
  (135 shorter events, 13.8 us)
Async XLA Ops:
  7.2 1.9 copy-start.7
  7.2 78.7 %all-gather.8.cloned.1.call-start = ((), (), s32[]{:S(2)}) async-start(), calls=%async_computation.2 | async-start | bytes 8355840 | tf_op jit(solution)/shard_map/all_gather | solution.py:155
  9.1 1.0 copy-start.4
  9.1 1.2 copy-start.5
  9.3 9.0 %copy-start.10 = (f32[1280]{0:T(1024)S(1)}, f32[1280]{0:T(1024)}, u32[]{:S(2)}) copy-start(f32[1280]{0:T(1024)} %param.19) | copy-start | bytes 15364
  18.3 0.6 copy-start.12
  20.5 2.3 copy-start.18
  27.3 1.3 copy-start.3
  27.3 1.3 copy-start.11
  28.6 1.3 copy-start.2
  29.9 0.7 copy-start.13
  32.7 106.0 %all-gather.6.cloned.1.call-start = ((), (), s32[]{:S(2)}) async-start(), calls=%async_computation.1 | async-start | bytes 8355840 | tf_op jit(solution)/shard_map/all_gather | solution.py:153
  33.8 157.2 %all-gather.10.cloned.1.call-start = ((), (), s32[]{:S(2)}) async-start(), calls=%async_computation.3 | async-start | bytes 8355840 | tf_op jit(solution)/shard_map/all_gather | solution.py:154
  34.5 208.6 %all-gather.12.cloned.1.call-start = ((), (), s32[]{:S(2)}) async-start(), calls=%async_computation.4 | async-start | bytes 8355840 | tf_op jit(solution)/shard_map/all_gather | solution.py:156
  35.1 337.1 %all-gather.14.cloned.1.call-start = ((), (), s32[]{:S(2)}) async-start(), calls=%async_computation.5 | async-start | bytes 16384000 | tf_op jit(solution)/shard_map/all_gather | solution.py:195
  35.7 1.0 copy-start.6
  35.7 448.1 %reduce-scatter.2.cloned.1.call-start = ((), (), s32[]{:S(2)}) async-start(), calls=%async_computation.6 | async-start | bytes 11796480 | tf_op jit(solution)/shard_map/reduce_scatter | solution.py:198
  36.7 1.3 copy-start.14
  36.7 1.3 copy-start.15
  36.7 1.3 copy-start.16
  40.2 0.6 copy-start.17
  253.8 3.0 copy-start.8
  256.8 6.6 %copy-start = (f32[10,512,192]{1,2,0:T(8,128)}, f32[10,512,192]{1,2,0:T(8,128)S(1)}, u32[]{:S(2)}) copy-start(f32[10,512,192]{1,2,0:T(8,128)S(1)} %get-tuple-element.481) | copy-start | bytes 11796484 | tf_op jit(solution)/shard_map/while
  267.0 2.8 copy-start.1
  269.8 3.5 copy-start.9
  273.3 2.8 copy-start.8
  276.2 6.3 %copy-start = (f32[10,512,192]{1,2,0:T(8,128)}, f32[10,512,192]{1,2,0:T(8,128)S(1)}, u32[]{:S(2)}) copy-start(f32[10,512,192]{1,2,0:T(8,128)S(1)} %get-tuple-element.481) | copy-start | bytes 11796484 | tf_op jit(solution)/shard_map/while
  286.0 2.8 copy-start.1
  288.8 3.9 copy-start.9
  292.6 2.8 copy-start.8
  295.5 6.4 %copy-start = (f32[10,512,192]{1,2,0:T(8,128)}, f32[10,512,192]{1,2,0:T(8,128)S(1)}, u32[]{:S(2)}) copy-start(f32[10,512,192]{1,2,0:T(8,128)S(1)} %get-tuple-element.481) | copy-start | bytes 11796484 | tf_op jit(solution)/shard_map/while
  305.3 2.9 copy-start.1
  308.2 3.9 copy-start.9
  312.0 2.8 copy-start.8
  314.8 6.4 %copy-start = (f32[10,512,192]{1,2,0:T(8,128)}, f32[10,512,192]{1,2,0:T(8,128)S(1)}, u32[]{:S(2)}) copy-start(f32[10,512,192]{1,2,0:T(8,128)S(1)} %get-tuple-element.481) | copy-start | bytes 11796484 | tf_op jit(solution)/shard_map/while
  324.7 2.9 copy-start.1
  327.6 3.8 copy-start.9
  331.5 2.8 copy-start.8
  334.3 6.4 %copy-start = (f32[10,512,192]{1,2,0:T(8,128)}, f32[10,512,192]{1,2,0:T(8,128)S(1)}, u32[]{:S(2)}) copy-start(f32[10,512,192]{1,2,0:T(8,128)S(1)} %get-tuple-element.481) | copy-start | bytes 11796484 | tf_op jit(solution)/shard_map/while
  344.1 2.8 copy-start.1
  346.9 3.8 copy-start.9
  350.7 2.8 copy-start.8
  353.5 6.3 %copy-start = (f32[10,512,192]{1,2,0:T(8,128)}, f32[10,512,192]{1,2,0:T(8,128)S(1)}, u32[]{:S(2)}) copy-start(f32[10,512,192]{1,2,0:T(8,128)S(1)} %get-tuple-element.481) | copy-start | bytes 11796484 | tf_op jit(solution)/shard_map/while
  363.3 2.8 copy-start.1
  366.1 3.8 copy-start.9
Sparse Core Ops, SparseCore 0:
  32.8 53.0 all-gather.7
  88.2 50.5 all-gather.5
  140.5 50.5 all-gather.9
  192.6 50.5 all-gather.11
  244.7 123.3 all-gather.13
  384.9 98.8 reduce-scatter.1
where the time goes:
time: 497 us; the launch traced here: 494 us
  waiting for transfers between devices  269 us (54%)
  matrix products  127 us (26%)
  local copies, waits for them, and re-layouts  62 us (12%)
  between operations  14.4 us (3%)
  other arithmetic  14 us (3%)
  blocking collectives  6.74 us (1%)
    reduce_scatter x1, waiting for transfers between devices, on_device(): lax.psum_scatter(partial_sums, 'head', scatter_dimension=1, tiled=True)  99 us
    all_gather x1, waiting for transfers between devices, on_device(): lax.all_gather(key_turned_tangent.reshape(flat_shape), 'ctx', axis=1, til...  43.3 us
    all_gather x1, waiting for transfers between devices, on_device(): lax.all_gather(key_turned.reshape(flat_shape), 'ctx', axis=1, tiled=True)  42.2 us
    all_gather x1, waiting for transfers between devices, on_device(): lax.all_gather(value_input, 'ctx', axis=1, tiled=True)  41.6 us
    all_gather x1, waiting for transfers between devices, on_device(): lax.all_gather(value_tangent, 'ctx', axis=1, tiled=True)  41.5 us
    dot_general x6, matrix products, attend(): jnp.einsum('hqk,khd->qhd', weights_low, value_rows, preferred_element_typ...  22.7 us
    dot_general x6, matrix products, attend(): jnp.einsum('hqk,khd->qhd', weights_low, value_rows_tangent, preferred_ele...  20.7 us
    dot_general x6, matrix products, attend(): jnp.einsum('qhd,khd->hqk', queries, key_rows_tangent, preferred_element_t...  20.2 us
  transfers between devices with their start and end apart: 6, of which 5 were waited for; matrix products, arithmetic and copies ran while one was open for 34% of the time, Pallas kernels for 0%

commit v1 on v0

v1 whole, which is shorter than its diff:
```python
import functools
import math

import jax
import jax.numpy as jnp
from jax import lax
from jax.experimental import pallas as pl
from jax.experimental.pallas import tpu as pltpu
from jax.sharding import PartitionSpec as P

HEAD_DIM = 128
GRID_H = 8
GRID_W = 16
CAP = 30
HD = 2560
SPAN = 96
ROWS = 192
HEADS = 10
FEATURES = HEADS * HEAD_DIM
CHIPS = 8
PART = 48
SLOT = ROWS + PART
TILE_Q = 384
TILE_K = 512
SCALE = 1.0 / math.sqrt(HEAD_DIM)
BF16 = jnp.bfloat16
F32 = jnp.float32
MIB = 2**20
SMEM = pl.BlockSpec(memory_space=pltpu.SMEM)


def params(mib):
    return pltpu.CompilerParams(vmem_limit_bytes=mib * MIB)


def cost(flops, moved):
    return pl.CostEstimate(flops=flops, bytes_accessed=moved, transcendentals=0)


def shape(*dims, kind=BF16):
    return jax.ShapeDtypeStruct(dims, kind)


def whole(member):
    return pl.BlockSpec(member.shape, lambda step: (0,) * len(member.shape))


def call(kernel, name, outs, operands, scratch, mib, estimate, scalars=0):
    return pl.pallas_call(
        kernel,
        grid=(1,),
        out_shape=outs,
        in_specs=[SMEM] * scalars + [whole(member) for member in operands[scalars:]],
        out_specs=jax.tree.map(whole, outs),
        scratch_shapes=scratch,
        compiler_params=params(mib),
        cost_estimate=estimate,
        name=name,
    )(*operands)


def dot(left, right):
    return lax.dot_general(left, right, (((1,), (0,)), ((), ())), preferred_element_type=F32)


def dot_rows(left, right):
    return lax.dot_general(left, right, (((1,), (1,)), ((), ())), preferred_element_type=F32)


def head_columns(head):
    return pl.ds(pl.multiple_of(head * HEAD_DIM, HEAD_DIM), HEAD_DIM)


def rope_tables(own_spans):
    positions = (
        own_spans[:, None] * SPAN + jnp.arange(SPAN, dtype=jnp.int32)[None, :]
    ).reshape(-1)
    pairs = HEAD_DIM // 2
    side = pairs // 3
    time = pairs - 2 * side
    time_freq = 10000.0 ** (-jnp.arange(time, dtype=F32) / time)
    side_freq = 10000.0 ** (-jnp.arange(side, dtype=F32) / side)
    freq = jnp.concatenate([time_freq, side_freq, side_freq])
    freq = jnp.broadcast_to(freq[:, None], (pairs, 2)).reshape(1, HEAD_DIM)
    pair = (jnp.arange(HEAD_DIM, dtype=jnp.int32) // 2)[None, :]
    place = jnp.where(
        pair < time,
        (positions // (GRID_H * GRID_W))[:, None],
        jnp.where(
            pair < time + side,
            (positions // GRID_W % GRID_H)[:, None],
            (positions % GRID_W)[:, None],
        ),
    ).astype(F32)
    angle = place * freq
    return jnp.cos(angle), jnp.sin(angle)


def prepare_kernel(meta, q, qt, k, kt, v, vt, *outs):
    stats = outs[CHIPS]
    chip = meta[0]
    for slot in range(CHIPS):
        other = jnp.bitwise_xor(chip, slot)
        for place, head in ((0, other), (1, CHIPS + other // 4)):
            outs[slot][place, :, :HEAD_DIM] = v[:, head_columns(head)]
            outs[slot][place, :, HEAD_DIM:] = vt[:, head_columns(head)]
    lane = lax.broadcasted_iota(jnp.int32, (ROWS, HEAD_DIM), 1)
    total = jnp.zeros((ROWS, HEAD_DIM), F32)
    for place, (left, right) in enumerate(((q, q), (q, qt), (k, k), (k, kt))):
        product = left[...].astype(F32) * right[...].astype(F32)
        total = jnp.where(lane == place, jnp.sum(product, axis=1, keepdims=True), total)
    stats[...] = total


def prepare(meta, q, qt, k, kt, v, vt):
    return call(
        prepare_kernel,
        "prepare",
        [shape(2, ROWS, 256)] * CHIPS + [shape(ROWS, HEAD_DIM, kind=F32)],
        [meta, q, qt, k, kt, v, vt],
        [],
        60,
        cost(4 * ROWS * FEATURES, 6 * MIB),
        1,
    )


def norm_rope_kernel(meta, q, qt, k, kt, mine, theirs, q_gain, k_gain, cosine, sine, *rest):
    q_out, k_out = rest[:CHIPS], rest[CHIPS : 2 * CHIPS]
    q_extra, k_extra = rest[2 * CHIPS :]
    chip = meta[0]
    stats = mine[...] + theirs[...]
    cos = cosine[...]
    even = lax.broadcasted_iota(jnp.int32, (ROWS, HEAD_DIM), 1) % 2 == 0
    sin_next = jnp.where(even, -sine[...], 0.0)
    sin_last = jnp.where(even, 0.0, sine[...])

    def rotated(x):
        after = pltpu.roll(x, HEAD_DIM - 1, 1)
        before = pltpu.roll(x, 1, 1)
        return (x * cos + (after * sin_next + before * sin_last)).astype(BF16)

    def of_head(raw_ref, tangent_ref, gain_ref, inverse, mixing, head):
        columns = head_columns(head)
        raw = raw_ref[:, columns].astype(F32)
        tangent = tangent_ref[:, columns].astype(F32)
        gain = gain_ref[:, columns]
        normed = gain * raw * inverse
        normed_tangent = gain * (
            tangent * inverse - raw * mixing * inverse * inverse * inverse
        )
        return rotated(normed), rotated(normed_tangent)

    wide = (ROWS, HEAD_DIM)
    for first, raw_ref, tangent_ref, gain_ref, outs, extra in (
        (0, q, qt, q_gain, q_out, q_extra),
        (2, k, kt, k_gain, k_out, k_extra),
    ):
        inverse = jnp.broadcast_to(lax.rsqrt(stats[:, first : first + 1] / HD + 1e-06), wide)
        mixing = jnp.broadcast_to(stats[:, first + 1 : first + 2] / HD, wide)
        for shared in range(2):
            turned, turned_tangent = of_head(
                raw_ref, tangent_ref, gain_ref, inverse, mixing, CHIPS + shared
            )
            extra[shared, :, :HEAD_DIM] = turned
            extra[shared, :, HEAD_DIM:] = turned_tangent
        for slot in range(CHIPS):
            other = jnp.bitwise_xor(chip, slot)
            turned, turned_tangent = of_head(
                raw_ref, tangent_ref, gain_ref, inverse, mixing, other
            )
            if first == 0:
                outs[slot][:ROWS, :HEAD_DIM] = turned
                outs[slot][:ROWS, HEAD_DIM:] = turned_tangent
                start = pl.multiple_of(other % 4 * PART, 16)
                outs[slot][ROWS:] = extra[other // 4, pl.ds(start, PART)]
            else:
                outs[slot][0, :, :HEAD_DIM] = turned
                outs[slot][0, :, HEAD_DIM:] = turned_tangent
                outs[slot][1] = extra[other // 4]


def norm_rope(*operands):
    return call(
        norm_rope_kernel,
        "norm_rope",
        [shape(SLOT, 256)] * CHIPS + [shape(2, ROWS, 256)] * CHIPS,
        operands,
        [pltpu.VMEM((2, ROWS, 256), BF16)] * 2,
        60,
        cost(40 * ROWS * FEATURES, 5 * MIB),
        1,
    )


def attend_kernel(first, last, chunks, *refs):
    q_in = refs[:CHIPS]
    k_in = refs[CHIPS : CHIPS + chunks]
    v_in = refs[CHIPS + chunks : CHIPS + 2 * chunks]
    rest = refs[CHIPS + 2 * chunks :]
    before = None
    if not first:
        before, rest = rest[0], rest[1:]
    if last:
        outs, rest = rest[:CHIPS], rest[CHIPS:]
    else:
        state, rest = rest[0], rest[1:]
    queries, keys, values = rest[:3]
    for slot in range(CHIPS):
        queries[slot * ROWS : (slot + 1) * ROWS] = q_in[slot][:ROWS]
        low = CHIPS * ROWS + slot * PART
        queries[low : low + PART] = q_in[slot][ROWS:]
    for chunk in range(chunks):
        rows = slice(chunk * ROWS, (chunk + 1) * ROWS)
        for place in range(2):
            keys[place, rows] = k_in[chunk][place]
            values[place, rows] = v_in[chunk][place]
    tiles = CHIPS * SLOT // TILE_Q
    steps = chunks * ROWS // TILE_K

    def one_tile(tile, carry):
        place = tile // (tiles - 1)
        both = queries[pl.ds(pl.multiple_of(tile * TILE_Q, TILE_Q), TILE_Q)]
        plain = both[:, :HEAD_DIM]
        crossed = jnp.concatenate([both[:, HEAD_DIM:], plain], axis=1)
        if first:
            weighted = jnp.zeros((TILE_Q, 256), F32)
            weighted_tangent = jnp.zeros((TILE_Q, HEAD_DIM), F32)
        else:
            weighted = before[tile, :, :256]
            weighted_tangent = before[tile, :, 256:384]
        norm_lanes = jnp.zeros((TILE_Q, HEAD_DIM), F32)
        tangent_lanes = jnp.zeros((TILE_Q, HEAD_DIM), F32)
        for step in range(steps):
            rows = slice(step * TILE_K, (step + 1) * TILE_K)
            key_rows = keys[place, rows]
            value_rows = values[place, rows]
            scores = dot_rows(plain, key_rows[:, :HEAD_DIM])
            scores_tangent = dot_rows(crossed, key_rows)
            squashed = jnp.tanh(scores * (SCALE / CAP))
            weights = jnp.exp2(squashed * (CAP * math.log2(math.e)))
            weights_tangent = weights * ((1.0 - squashed * squashed) * scores_tangent)
            for low in range(0, TILE_K, HEAD_DIM):
                norm_lanes = norm_lanes + weights[:, low : low + HEAD_DIM]
                tangent_lanes = tangent_lanes + weights_tangent[:, low : low + HEAD_DIM]
            weighted = weighted + dot(weights.astype(BF16), value_rows)
            weighted_tangent = weighted_tangent + dot(
                weights_tangent.astype(BF16), value_rows[:, :HEAD_DIM]
            )
        norm_sum = jnp.sum(norm_lanes, axis=1, keepdims=True)
        tangent_sum = jnp.sum(tangent_lanes, axis=1, keepdims=True)
        if not first:
            norm_sum = norm_sum + before[tile, :, 384:385]
            tangent_sum = tangent_sum + before[tile, :, 448:449]
        if last:
            inverse = 1.0 / norm_sum
            attention = weighted[:, :HEAD_DIM] * inverse
            attention_tangent = (
                weighted[:, HEAD_DIM:] + weighted_tangent * SCALE
            ) * inverse - (tangent_sum * SCALE * inverse) * attention
            outcome = jnp.concatenate([attention, attention_tangent], axis=1)
            rest[3][pl.ds(pl.multiple_of(tile * TILE_Q, TILE_Q), TILE_Q)] = outcome.astype(BF16)
        else:
            state[tile, :, :256] = weighted
            state[tile, :, 256:384] = weighted_tangent
            state[tile, :, 384:448] = jnp.broadcast_to(norm_sum, (TILE_Q, 64))
            state[tile, :, 448:] = jnp.broadcast_to(tangent_sum, (TILE_Q, 64))
        return carry

    lax.fori_loop(0, tiles, one_tile, 0)
    if last:
        for slot in range(CHIPS):
            outs[slot][:ROWS] = rest[3][slot * ROWS : (slot + 1) * ROWS]
            low = CHIPS * ROWS + slot * PART
            outs[slot][ROWS:] = rest[3][low : low + PART]


def attend(queries, keys, values, before=None, last=False):
    chunks = len(keys)
    tiles = CHIPS * SLOT // TILE_Q
    first = before is None
    operands = list(queries) + list(keys) + list(values) + ([] if first else [before])
    outs = [shape(SLOT, 256)] * CHIPS if last else shape(tiles, TILE_Q, 512, kind=F32)
    scratch = [
        pltpu.VMEM((CHIPS * SLOT, 256), BF16),
        pltpu.VMEM((2, chunks * ROWS, 256), BF16),
        pltpu.VMEM((2, chunks * ROWS, 256), BF16),
    ]
    if last:
        scratch.append(pltpu.VMEM((CHIPS * SLOT, 256), BF16))
    return call(
        functools.partial(attend_kernel, first, last, chunks),
        "attend",
        outs,
        operands,
        scratch,
        60,
        cost(8 * 256 * CHIPS * SLOT * chunks * ROWS, 10 * MIB),
    )


def project_kernel(meta, *refs):
    parts = refs[:CHIPS]
    mine, theirs, out, left, right = refs[CHIPS:]
    chip = meta[0]
    core = meta[1]

    @pl.when(pl.program_id(0) == 0)
    def _():
        for slot in range(CHIPS):
            other = jnp.bitwise_xor(chip, slot)
            left[other, :ROWS] = parts[slot][:ROWS, :HEAD_DIM]
            left[other, ROWS:] = parts[slot][:ROWS, HEAD_DIM:]
            shared = CHIPS + other // 4
            start = pl.multiple_of(other % 4 * PART, 16)
            left[shared, pl.ds(start, PART)] = parts[slot][ROWS:, :HEAD_DIM]
            left[shared, pl.ds(ROWS + start, PART)] = parts[slot][ROWS:, HEAD_DIM:]

    half = FEATURES // 2
    right[pl.ds(pl.multiple_of(core * half, half), half)] = mine[0]
    right[pl.ds(pl.multiple_of((1 - core) * half, half), half)] = theirs[0]
    rows = jnp.concatenate([left[head] for head in range(HEADS)], axis=1)
    for low in range(0, FEATURES, 256):
        out[:, low : low + 256] = dot(rows, right[:, low : low + 256]).astype(out.dtype)


def project(meta, parts, mine, theirs, kind):
    half = FEATURES // 2

    def of_block(step, meta):
        return (2 * meta[2] + step, 0, 0)

    whole = pl.BlockSpec((SLOT, 256), lambda step, meta: (0, 0))
    return pl.pallas_call(
        project_kernel,
        out_shape=shape(2 * ROWS, 2 * FEATURES, kind=kind),
        grid_spec=pltpu.PrefetchScalarGridSpec(
            num_scalar_prefetch=1,
            grid=(2,),
            in_specs=[whole] * CHIPS
            + [pl.BlockSpec((1, half, FEATURES), of_block)] * 2,
            out_specs=pl.BlockSpec((2 * ROWS, FEATURES), lambda step, meta: (0, step)),
            scratch_shapes=[
                pltpu.VMEM((HEADS, 2 * ROWS, HEAD_DIM), BF16),
                pltpu.VMEM((FEATURES, FEATURES), BF16),
            ],
        ),
        compiler_params=params(60),
        cost_estimate=cost(2 * 2 * ROWS * FEATURES * 2 * FEATURES, 10 * MIB),
        name="project",
    )(meta, *parts, mine, theirs)


def to_chip(array, slot):
    if slot == 0:
        return array
    return lax.ppermute(array, "ctx", [(place, place ^ (2 * slot)) for place in range(16)])


def to_core(array):
    return lax.ppermute(array, "ctx", [(place, place ^ 1) for place in range(16)])


def to_group(array):
    return lax.ppermute(array, "head", [(0, 1), (1, 0)])


def on_device(
    query_input,
    key_input,
    value_input,
    query_tangent,
    key_tangent,
    value_tangent,
    query_gain,
    key_gain,
    out_weight,
    span_order,
):
    place = lax.axis_index("ctx")
    group = lax.axis_index("head")
    chip, core = place // 2, place % 2
    meta = jnp.stack([chip, core, group]).astype(jnp.int32)
    half = FEATURES // 2
    own_half = lax.dynamic_slice_in_dim(out_weight, core * half, half, 0)
    weight_mine = lax.all_gather(own_half, "dp", axis=0)

    raw = [
        member[0]
        for member in (
            query_input,
            query_tangent,
            key_input,
            key_tangent,
            value_input,
            value_tangent,
        )
    ]
    *value_slots, stats = prepare(meta, *raw)
    stats_peer = to_group(stats)
    order = (0, 1, 3, 4, 2, 5, 7, 6)
    cosine, sine = rope_tables(lax.dynamic_slice_in_dim(span_order, 2 * place, 2))
    slots = norm_rope(
        meta,
        *raw[:4],
        stats,
        stats_peer,
        query_gain[None],
        key_gain[None],
        cosine,
        sine,
    )
    value_slots[5:], slots = lax.optimization_barrier((value_slots[5:], slots))
    values = [to_chip(value_slots[slot], slot) for slot in order]
    queries = [to_chip(slots[slot], slot) for slot in range(CHIPS)]
    keys = [to_chip(slots[CHIPS + slot], slot) for slot in order]
    values = values + [to_core(member) for member in values]
    keys = keys + [to_core(member) for member in keys]
    early = [0, 1, 2, 3, 8, 9, 10, 11]
    late = [4, 5, 6, 7, 12, 13, 14, 15]
    state = attend(queries, [keys[i] for i in early], [values[i] for i in early])
    results = attend(
        queries, [keys[i] for i in late], [values[i] for i in late], state, last=True
    )
    weight_mine, results = lax.optimization_barrier((weight_mine, results))
    weight_theirs = to_core(weight_mine)
    parts = [to_chip(results[slot], slot) for slot in range(CHIPS)]
    for_peer = project(
        meta.at[2].set(1 - group), parts, weight_mine, weight_theirs, BF16
    )
    from_peer = to_group(for_peer)
    own = project(meta, parts, weight_mine, weight_theirs, F32)
    total = (own + from_peer.astype(F32)).astype(BF16)
    return (total[:ROWS][None], total[ROWS:][None])


def solution(mesh):
    return jax.shard_map(
        on_device,
        mesh=mesh,
        in_specs=(
            P("dp", "ctx", "head"),
            P("dp", "ctx", "head"),
            P("dp", "ctx", "head"),
            P("dp", "ctx", "head"),
            P("dp", "ctx", "head"),
            P("dp", "ctx", "head"),
            P("head"),
            P("head"),
            P("head", "dp"),
            P(),
        ),
        out_specs=(P("dp", "ctx", "head"), P("dp", "ctx", "head")),
        check_vma=False,
    )
```

time: 497 us -> 211 us (0.42)
  waiting for transfers between devices: 269 us -> 75 us
  matrix products: 127 us -> 0 us
  Pallas kernels: 0 us -> 54.5 us
  local copies, waits for them, and re-layouts: 62 us -> 7.61 us
  starting transfers between devices: 0.24 us -> 51.9 us
  other arithmetic: 14 us -> 4.75 us
  blocking collectives: 6.74 us -> 0 us
    all_gather x5 -> x1, waiting for transfers between devices: 169 us -> 0.02 us  [on_device(): weight_mine = lax.all_gather(own_half, 'dp', axis=0)]
    dot_general x37 -> x0, matrix products: 127 us -> none  [the longest x6 22.7 us: attend(): jnp.einsum('hqk,khd->qhd', weights_low, value_rows, preferred_element_typ...]
    reduce_scatter x1 -> x0, waiting for transfers between devices: 99 us -> none  [on_device(): lax.psum_scatter(partial_sums, 'head', scatter_dimension=1, tiled=True)]
    ppermute x0 -> x47, waiting for transfers between devices: none -> 74.9 us  [the longest x2 42.1 us: to_group(): return lax.ppermute(array, 'head', [(0, 1), (1, 0)])]
    pallas_call x0 -> x6, Pallas kernels: none -> 54.5 us  [the longest x4 39.3 us: call(): pl.pallas_call(kernel, grid=(1,), out_shape=outs, in_specs=[SMEM] * scala...]
    ppermute x0 -> x47, starting transfers between devices: none -> 51.9 us  [the longest x28 36.7 us: to_chip(): lax.ppermute(array, 'ctx', [(place, place ^ 2 * slot) for place in range(...]
    all_gather x4 -> x0, local copies, waits for them, and re-layouts: 42.5 us -> none  [the longest x1 10.7 us: on_device(): lax.all_gather(value_input, 'ctx', axis=1, tiled=True)]
    psum x1 -> x0, blocking collectives: 6.74 us -> none  [on_device(): lax.psum((jnp.sum(query_float * query_float, axis=-1), jnp.sum(query_floa...]
  transfers between devices with their start and end apart: 6 -> 48, of which waited for: 5 -> 13; matrix products, arithmetic and copies ran while one was open for 34% -> 2% of each run, Pallas kernels for 0% -> 19%
where the time goes in v1:
time: 211 us; the launch traced here: 208 us
  waiting for transfers between devices  75 us (36%)
  Pallas kernels  54.5 us (26%)
  starting transfers between devices  51.9 us (25%)
  between operations  14.4 us (7%)
  local copies, waits for them, and re-layouts  7.61 us (4%)
  other arithmetic  4.75 us (2%)
    ppermute x2, waiting for transfers between devices, to_group(): return lax.ppermute(array, 'head', [(0, 1), (1, 0)])  42.1 us
    pallas_call x4, Pallas kernels, call(): pl.pallas_call(kernel, grid=(1,), out_shape=outs, in_specs=[SMEM] * scala...  39.3 us
    ppermute x28, starting transfers between devices, to_chip(): lax.ppermute(array, 'ctx', [(place, place ^ 2 * slot) for place in range(...  36.7 us
    ppermute x28, waiting for transfers between devices, to_chip(): lax.ppermute(array, 'ctx', [(place, place ^ 2 * slot) for place in range(...  32.6 us
    pallas_call x2, Pallas kernels, project(): pl.pallas_call(project_kernel, out_shape=shape(2 * ROWS, 2 * FEATURES, ki...  15.2 us
    ppermute x17, starting transfers between devices, to_core(): lax.ppermute(array, 'ctx', [(place, place ^ 1) for place in range(16)])  9.39 us
    ppermute x2, starting transfers between devices, to_group(): return lax.ppermute(array, 'head', [(0, 1), (1, 0)])  5.73 us
  transfers between devices with their start and end apart: 48, of which 13 were waited for; matrix products, arithmetic and copies ran while one was open for 2% of the time, Pallas kernels for 19%

profile of v1, /device:TPU:1, one launch (start us, length us, event | category | flops | bytes accessed | tf_op | source)
XLA Modules:
  0.0 208.1 jit_solution(2897813648440885318)
XLA Ops:
  7.2 1.9 copy-done
  9.1 1.4 constant_dynamic-slice_fusion
  10.5 0.6 pad_add_fusion.meta
  11.1 3.4 %prepare.1 = (bf16[2,192,256]{2,1,0:T(8,128)(2,1)}, bf16[2,192,256]{2,1,0:T(8,128)(2,1)}, bf16[2,192,256]{2,1,0:T(8,128)(2,1)}, bf16[2,192,256]{2,1,0:T(8,128)(2...) custom-call(s32[3]{0:T(128)} %pad_add_fusion.meta, ...), custom_call_target="tpu_custom_call" | custom-call | flops 983040 | bytes 6291456 | tf_op jit(solution)/shard_map/prepare/pallas_call | solution.py:49
  14.5 4.4 %collective-permute-start = (f32[192,128]{1,0:T(8,128)}, f32[192,128]{1,0:T(8,128)S(1)}, u32[]{:S(2)}, u32[]{:S(2)}) collective-permute-start(f32[192,128]{1,0:T(8,128)} %get-tuple-element.78.mine), channel_id=1, source_target_pairs={{0,16},{16,0},{1,17},{17,1},{2,18},{18,2},{3,19},{19,3},{4,20},{20... | collective-permute-start | bytes 294920 | tf_op jit(solution)/shard_map/ppermute | solution.py:365
  18.9 2.9 %collective-permute-start.16 = (bf16[2,192,256]{2,1,0:T(8,128)(2,1)}, bf16[2,192,256]{2,1,0:T(8,128)(2,1)}, u32[]{:S(2)}, u32[]{:S(2)}) collective-permute-start(bf16[2,192,256]{2,1,0:T(8,128)(2,1)} %get-tuple-element.107), channel_id=1, source_target_pairs={{0,4},{1,5},{2,6},{3,7},{4,0},{5,1},{6,2},{7,3},{8,12},{9,13},{10,... | collective-permute-start | bytes 589832 | tf_op jit(solution)/shard_map/ppermute | solution.py:357
  21.8 0.4 collective-permute-start.31
  22.2 0.4 collective-permute-start.32
  22.6 0.7 collective-permute-start.33
  24.0 1.9 collective-permute-start.34
  25.8 1.2 fusion
  27.0 0.6 broadcast_in_dim.64.q_gain
  27.6 0.6 broadcast_in_dim.65.k_gain
  28.2 5.4 %norm_rope.1 = (bf16[240,256]{1,0:T(8,128)(2,1)}, bf16[240,256]{1,0:T(8,128)(2,1)}, bf16[240,256]{1,0:T(8,128)(2,1)}, bf16[240,256]{1,0:T(8,128)(2,1)}, bf16[240...) custom-call(s32[3]{0:T(128)} %pad_add_fusion.meta, ...), custom_call_target="tpu_custom_call" | custom-call | flops 9830400 | bytes 5242880 | tf_op jit(solution)/shard_map/norm_rope/pallas_call | solution.py:49
  33.6 1.3 collective-permute-start.1
  34.9 2.6 %collective-permute-start.2 = (bf16[240,256]{1,0:T(8,128)(2,1)}, bf16[240,256]{1,0:T(8,128)(2,1)S(1)}, u32[]{:S(2)}, u32[]{:S(2)}) collective-permute-start(bf16[240,256]{1,0:T(8,128)(2,1)} %get-tuple-element.97), channel_id=1, source_target_pairs={{0,4},{1,5},{2,6},{3,7},{4,0},{5,1},{6,2},{7,3},{8,12},{9,13},{10,... | collective-permute-start | bytes 368648 | tf_op jit(solution)/shard_map/ppermute | solution.py:357
  37.6 0.9 collective-permute-start.4
  38.5 0.3 collective-permute-start.5
  38.9 4.2 %collective-permute-start.6 = (bf16[240,256]{1,0:T(8,128)(2,1)}, bf16[240,256]{1,0:T(8,128)(2,1)S(1)}, u32[]{:S(2)}, u32[]{:S(2)}) collective-permute-start(bf16[240,256]{1,0:T(8,128)(2,1)} %get-tuple-element.101), channel_id=1, source_target_pairs={{0,12},{1,13},{2,14},{3,15},{4,8},{5,9},{6,10},{7,11},{8,4},{9,5},... | collective-permute-start | bytes 368648 | tf_op jit(solution)/shard_map/ppermute | solution.py:357
  43.1 0.7 collective-permute-done.2.refs_2_
  43.8 0.7 collective-permute-start.7
  44.5 2.7 %collective-permute-done.3.refs_3_ = bf16[240,256]{1,0:T(8,128)(2,1)S(1)} collective-permute-done((bf16[240,256]{1,0:T(8,128)(2,1)}, bf16[240,256]{1,0:T(8,128)(2,1)S(1)}, u32[]{:S(2)}, u32[]{:S(2)}) %collective-permute-start.3) | collective-permute-done | bytes 122912 | tf_op jit(solution)/shard_map/ppermute | solution.py:357
  47.2 0.7 collective-permute-start.9
  48.0 3.4 %collective-permute-start.10 = (bf16[2,192,256]{2,1,0:T(8,128)(2,1)}, bf16[2,192,256]{2,1,0:T(8,128)(2,1)S(1)}, u32[]{:S(2)}, u32[]{:S(2)}) collective-permute-start(bf16[2,192,256]{2,1,0:T(8,128)(2,1)} %get-tuple-element.105), channel_id=1, source_target_pairs={{0,14},{1,15},{2,12},{3,13},{4,10},{5,11},{6,8},{7,9},{8,6},{9,7},... | collective-permute-start | bytes 589832 | tf_op jit(solution)/shard_map/ppermute | solution.py:357
  51.4 0.7 collective-permute-start.11
  52.1 3.6 %collective-permute-done.7.refs_7_ = bf16[240,256]{1,0:T(8,128)(2,1)S(1)} collective-permute-done((bf16[240,256]{1,0:T(8,128)(2,1)}, bf16[240,256]{1,0:T(8,128)(2,1)S(1)}, u32[]{:S(2)}, u32[]{:S(2)}) %collective-permute-start.7) | collective-permute-done | bytes 122912 | tf_op jit(solution)/shard_map/ppermute | solution.py:357
  55.6 2.6 %collective-permute-start.17 = (bf16[2,192,256]{2,1,0:T(8,128)(2,1)}, bf16[2,192,256]{2,1,0:T(8,128)(2,1)}, u32[]{:S(2)}, u32[]{:S(2)}) collective-permute-start(bf16[2,192,256]{2,1,0:T(8,128)(2,1)} %get-tuple-element.108), channel_id=1, source_target_pairs={{0,10},{1,11},{2,8},{3,9},{4,14},{5,15},{6,12},{7,13},{8,2},{9,3},... | collective-permute-start | bytes 589832 | tf_op jit(solution)/shard_map/ppermute | solution.py:357
  58.3 2.1 collective-permute-start.19
  60.3 9.1 %collective-permute-done.10.refs_10_ = bf16[2,192,256]{2,1,0:T(8,128)(2,1)S(1)} collective-permute-done((bf16[2,192,256]{2,1,0:T(8,128)(2,1)}, bf16[2,192,256]{2,1,0:T(8,128)(2,1)S(1)}, u32[]{:S(2)}, u32[]{:S(2)}) %collective-permute-start.10) | collective-permute-done | bytes 196640 | tf_op jit(solution)/shard_map/ppermute | solution.py:357
  69.6 2.6 %collective-permute-done.17.refs_17_ = bf16[2,192,256]{2,1,0:T(8,128)(2,1)} collective-permute-done((bf16[2,192,256]{2,1,0:T(8,128)(2,1)}, bf16[2,192,256]{2,1,0:T(8,128)(2,1)}, u32[]{:S(2)}, u32[]{:S(2)}) %collective-permute-start.17) | collective-permute-done | bytes 196640 | tf_op jit(solution)/shard_map/ppermute | solution.py:357
  72.1 0.5 collective-permute-start.26
  72.6 6.4 %collective-permute-done.18.refs_18_ = bf16[2,192,256]{2,1,0:T(8,128)(2,1)} collective-permute-done((bf16[2,192,256]{2,1,0:T(8,128)(2,1)}, bf16[2,192,256]{2,1,0:T(8,128)(2,1)}, u32[]{:S(2)}, u32[]{:S(2)}) %collective-permute-start.18) | collective-permute-done | bytes 196640 | tf_op jit(solution)/shard_map/ppermute | solution.py:357
  79.0 1.1 collective-permute-start.27
  80.3 1.6 collective-permute-done.24.refs_9_
  81.9 1.4 collective-permute-start.35
  83.5 1.5 collective-permute-start.37
  85.1 0.4 collective-permute-start.13
  85.6 0.4 collective-permute-start.29
  86.0 0.2 collective-permute-done.37.refs_23_
  86.3 0.4 collective-permute-start.30
  86.8 0.4 collective-permute-start.15
  87.5 0.4 collective-permute-start.22
  88.2 0.7 copy-done.23
  88.8 0.4 collective-permute-start.23
  89.2 13.5 %attend.2.refs_24_ = f32[5,384,512]{2,1,0:T(8,128)} custom-call(bf16[240,256]{1,0:T(8,128)(2,1)} %get-tuple-element.95.refs_0_, bf16[240,256]{1,0:T(8,128)(2,1)} %copy-done.24, bf16[240,256]{1,0:T(8,128)(2,1)} %copy-done.25, bf16[240,256]{1,0:T(8,128)(2,1)} %copy-done.26, bf16[240,256]{1,0:T(8,128)(2,1)} %copy-done.27, bf16[240,256]{1,0:T(8,128)(2,1)} %copy-done.28, ...), custom_call_target="tpu_custom_call" | custom-call | flops 6039797760 | bytes 10485760 | tf_op jit(solution)/shard_map/attend/pallas_call | solution.py:49
  102.7 17.1 %attend.3 = (bf16[240,256]{1,0:T(8,128)(2,1)}, bf16[240,256]{1,0:T(8,128)(2,1)}, bf16[240,256]{1,0:T(8,128)(2,1)}, bf16[240,256]{1,0:T(8,128)(2,1)}, bf16[240,25...) custom-call(bf16[240,256]{1,0:T(8,128)(2,1)} %get-tuple-element.95.refs_0_, ...), custom_call_target="tpu_custom_call" | custom-call | flops 6039797760 | bytes 10485760 | tf_op jit(solution)/shard_map/attend/pallas_call | solution.py:49
  119.9 0.2 collective-permute-start.45
  120.1 1.4 collective-permute-start.38
  121.5 1.0 collective-permute-start.39
  122.6 1.4 collective-permute-start.40
  124.0 1.2 collective-permute-start.41
  125.2 2.0 collective-permute-start.42
  127.2 1.4 collective-permute-done.39.refs_2_
  128.7 2.7 %collective-permute-start.43 = (bf16[240,256]{1,0:T(8,128)(2,1)}, bf16[240,256]{1,0:T(8,128)(2,1)}, u32[]{:S(2)}, u32[]{:S(2)}) collective-permute-start(bf16[240,256]{1,0:T(8,128)(2,1)} %get-tuple-element.133), channel_id=1, source_target_pairs={{0,12},{1,13},{2,14},{3,15},{4,8},{5,9},{6,10},{7,11},{8,4},{9,5},... | collective-permute-start | bytes 368648 | tf_op jit(solution)/shard_map/ppermute | solution.py:357
  131.4 2.4 %collective-permute-start.44 = (bf16[240,256]{1,0:T(8,128)(2,1)}, bf16[240,256]{1,0:T(8,128)(2,1)}, u32[]{:S(2)}, u32[]{:S(2)}) collective-permute-start(bf16[240,256]{1,0:T(8,128)(2,1)} %get-tuple-element.134), channel_id=1, source_target_pairs={{0,14},{1,15},{2,12},{3,13},{4,10},{5,11},{6,8},{7,9},{8,6},{9,7},... | collective-permute-start | bytes 368648 | tf_op jit(solution)/shard_map/ppermute | solution.py:357
  133.8 1.3 collective-permute-done.43.refs_6_
  135.1 2.9 %collective-permute-done.44.refs_7_ = bf16[240,256]{1,0:T(8,128)(2,1)} collective-permute-done((bf16[240,256]{1,0:T(8,128)(2,1)}, bf16[240,256]{1,0:T(8,128)(2,1)}, u32[]{:S(2)}, u32[]{:S(2)}) %collective-permute-start.44) | collective-permute-done | bytes 122912 | tf_op jit(solution)/shard_map/ppermute | solution.py:357
  138.1 7.7 %project.2 = f32[384,2560]{1,0:T(8,128)} custom-call(s32[3]{0:T(128)} %pad_add_fusion.meta, bf16[240,256]{1,0:T(8,128)(2,1)} %get-tuple-element.127.refs_0_, bf16[240,256]{1,0:T(8,128)(2,1)} %copy-done.1, bf16[240,256]{1,0:T(8,128)(2,1)} %copy-done.2, bf16[240,256]{1,0:T(8,128)(2,1)} %collective-permute-done.40.refs_3_, ...), custom_call_target="tpu_custom_call" | custom-call | flops 2516582400 | bytes 10485760 | tf_op jit(solution)/shard_map/project/pallas_call | solution.py:334
  145.8 0.5 copy-done.5
  146.3 7.4 %project.3 = bf16[384,2560]{1,0:T(8,128)(2,1)} custom-call(s32[3]{0:T(128)} %copy-done.5, bf16[240,256]{1,0:T(8,128)(2,1)} %get-tuple-element.127.refs_0_, bf16[240,256]{1,0:T(8,128)(2,1)} %copy-done.1, bf16[240,256]{1,0:T(8,128)(2,1)} %copy-done.2, bf16[240,256]{1,0:T(8,128)(2,1)} %collective-permute-done.40.refs_3_, ...), custom_call_target="tpu_custom_call" | custom-call | flops 2516582400 | bytes 10485760 | tf_op jit(solution)/shard_map/project/pallas_call | solution.py:334
  153.8 1.3 collective-permute-start.46
  155.1 42.1 %collective-permute-done.46 = bf16[384,2560]{1,0:T(8,128)(2,1)S(1)} collective-permute-done((bf16[384,2560]{1,0:T(8,128)(2,1)}, bf16[384,2560]{1,0:T(8,128)(2,1)S(1)}, u32[]{:S(2)}, u32[]{:S(2)}) %collective-permute-start.46) | collective-permute-done | bytes 1966112 | tf_op jit(solution)/shard_map/ppermute | solution.py:365
  197.1 2.7 %add_convert_fusion = bf16[384,2560]{1,0:T(8,128)(2,1)S(1)} fusion(f32[384,2560]{1,0:T(8,128)} %project.2, bf16[384,2560]{1,0:T(8,128)(2,1)S(1)} %collective-permute-done.46), kind=kLoop, calls=%fused_computation | loop fusion | flops 2949120 | bytes 7864320 | tf_op jit(solution)/shard_map/convert_element_type | solution.py:433
  199.9 1.4 slice_bitcast_fusion
  (121 shorter events, 2.1 us)
Async XLA Ops:
  7.2 112.7 %all-gather.3.cloned.1.call-start = ((), (), s32[]{:S(2)}) async-start(), calls=%async_computation | async-start | bytes 8192000 | tf_op jit(solution)/shard_map/all_gather | solution.py:386
  9.1 14.2 %copy-start.31 = (s32[32]{0:T(128)S(1)}, s32[32]{0:T(128)}, u32[]{:S(2)}) copy-start(s32[32]{0:T(128)} %param.21) | copy-start | bytes 388
  10.5 16.5 %copy-start.6 = (f32[1280]{0:T(1024)S(1)}, f32[1280]{0:T(1024)}, u32[]{:S(2)}) copy-start(f32[1280]{0:T(1024)} %param.18) | copy-start | bytes 15364
  10.5 17.1 %copy-start.7 = (f32[1280]{0:T(1024)S(1)}, f32[1280]{0:T(1024)}, u32[]{:S(2)}) copy-start(f32[1280]{0:T(1024)} %param.19) | copy-start | bytes 15364
  14.5 9.5 %collective-permute-start = (f32[192,128]{1,0:T(8,128)}, f32[192,128]{1,0:T(8,128)S(1)}, u32[]{:S(2)}, u32[]{:S(2)}) collective-permute-start(f32[192,128]{1,0:T(8,128)} %get-tuple-element.78.mine), channel_id=1, source_target_pairs={{0,16},{16,0},{1,17},{17,1},{2,18},{18,2},{3,19},{19,3},{4,20},{20... | collective-permute-start | bytes 294920 | tf_op jit(solution)/shard_map/ppermute | solution.py:365
  18.9 14.7 %collective-permute-start.16 = (bf16[2,192,256]{2,1,0:T(8,128)(2,1)}, bf16[2,192,256]{2,1,0:T(8,128)(2,1)}, u32[]{:S(2)}, u32[]{:S(2)}) collective-permute-start(bf16[2,192,256]{2,1,0:T(8,128)(2,1)} %get-tuple-element.107), channel_id=1, source_target_pairs={{0,4},{1,5},{2,6},{3,7},{4,0},{5,1},{6,2},{7,3},{8,12},{9,13},{10,... | collective-permute-start | bytes 589832 | tf_op jit(solution)/shard_map/ppermute | solution.py:357
  21.8 13.1 %collective-permute-start.31 = (bf16[2,192,256]{2,1,0:T(8,128)(2,1)}, bf16[2,192,256]{2,1,0:T(8,128)(2,1)}, u32[]{:S(2)}, u32[]{:S(2)}) collective-permute-start(bf16[2,192,256]{2,1,0:T(8,128)(2,1)} %get-tuple-element.116), channel_id=1, source_target_pairs={{0,2},{1,3},{2,0},{3,1},{4,6},{5,7},{6,4},{7,5},{8,10},{9,11},{10,... | collective-permute-start | bytes 589832 | tf_op jit(solution)/shard_map/ppermute | solution.py:357
  22.2 15.3 %collective-permute-start.32 = (bf16[2,192,256]{2,1,0:T(8,128)(2,1)}, bf16[2,192,256]{2,1,0:T(8,128)(2,1)}, u32[]{:S(2)}, u32[]{:S(2)}) collective-permute-start(bf16[2,192,256]{2,1,0:T(8,128)(2,1)} %get-tuple-element.117), channel_id=1, source_target_pairs={{0,6},{1,7},{2,4},{3,5},{4,2},{5,3},{6,0},{7,1},{8,14},{9,15},{10,... | collective-permute-start | bytes 589832 | tf_op jit(solution)/shard_map/ppermute | solution.py:357
  22.6 15.0 %collective-permute-start.33 = (bf16[2,192,256]{2,1,0:T(8,128)(2,1)}, bf16[2,192,256]{2,1,0:T(8,128)(2,1)}, u32[]{:S(2)}, u32[]{:S(2)}) collective-permute-start(bf16[2,192,256]{2,1,0:T(8,128)(2,1)} %get-tuple-element.118), channel_id=1, source_target_pairs={{0,8},{1,9},{2,10},{3,11},{4,12},{5,13},{6,14},{7,15},{8,0},{9,1},... | collective-permute-start | bytes 589832 | tf_op jit(solution)/shard_map/ppermute | solution.py:357
  24.0 14.5 %collective-permute-start.34 = (bf16[2,192,256]{2,1,0:T(8,128)(2,1)}, bf16[2,192,256]{2,1,0:T(8,128)(2,1)S(1)}, u32[]{:S(2)}, u32[]{:S(2)}) collective-permute-start(bf16[2,192,256]{2,1,0:T(8,128)(2,1)} %get-tuple-element.115.refs_16_), channel_id=1, source_target_pairs={{0,1},{1,0},{2,3},{3,2},{4,5},{5,4},{6,7},{7,6},{8,9},{9,8},{10,11... | collective-permute-start | bytes 589832 | tf_op jit(solution)/shard_map/ppermute | solution.py:361
  33.6 5.3 %collective-permute-start.1 = (bf16[240,256]{1,0:T(8,128)(2,1)}, bf16[240,256]{1,0:T(8,128)(2,1)S(1)}, u32[]{:S(2)}, u32[]{:S(2)}) collective-permute-start(bf16[240,256]{1,0:T(8,128)(2,1)} %get-tuple-element.96), channel_id=1, source_target_pairs={{0,2},{1,3},{2,0},{3,1},{4,6},{5,7},{6,4},{7,5},{8,10},{9,11},{10,... | collective-permute-start | bytes 368648 | tf_op jit(solution)/shard_map/ppermute | solution.py:357
  34.9 8.9 %collective-permute-start.2 = (bf16[240,256]{1,0:T(8,128)(2,1)}, bf16[240,256]{1,0:T(8,128)(2,1)S(1)}, u32[]{:S(2)}, u32[]{:S(2)}) collective-permute-start(bf16[240,256]{1,0:T(8,128)(2,1)} %get-tuple-element.97), channel_id=1, source_target_pairs={{0,4},{1,5},{2,6},{3,7},{4,0},{5,1},{6,2},{7,3},{8,12},{9,13},{10,... | collective-permute-start | bytes 368648 | tf_op jit(solution)/shard_map/ppermute | solution.py:357
  37.5 9.7 %collective-permute-start.3 = (bf16[240,256]{1,0:T(8,128)(2,1)}, bf16[240,256]{1,0:T(8,128)(2,1)S(1)}, u32[]{:S(2)}, u32[]{:S(2)}) collective-permute-start(bf16[240,256]{1,0:T(8,128)(2,1)} %get-tuple-element.98), channel_id=1, source_target_pairs={{0,6},{1,7},{2,4},{3,5},{4,2},{5,3},{6,0},{7,1},{8,14},{9,15},{10,... | collective-permute-start | bytes 368648 | tf_op jit(solution)/shard_map/ppermute | solution.py:357
  37.6 9.7 %collective-permute-start.4 = (bf16[240,256]{1,0:T(8,128)(2,1)}, bf16[240,256]{1,0:T(8,128)(2,1)S(1)}, u32[]{:S(2)}, u32[]{:S(2)}) collective-permute-start(bf16[240,256]{1,0:T(8,128)(2,1)} %get-tuple-element.99), channel_id=1, source_target_pairs={{0,8},{1,9},{2,10},{3,11},{4,12},{5,13},{6,14},{7,15},{8,0},{9,1},... | collective-permute-start | bytes 368648 | tf_op jit(solution)/shard_map/ppermute | solution.py:357
  38.4 50.8 %copy-start.8 = (bf16[2,192,256]{2,1,0:T(8,128)(2,1)}, bf16[2,192,256]{2,1,0:T(8,128)(2,1)S(1)}, u32[]{:S(2)}) copy-start(bf16[2,192,256]{2,1,0:T(8,128)(2,1)S(1)} %collective-permute-done.34.refs_20_) | copy-start | bytes 589828
  38.5 9.5 %collective-permute-start.5 = (bf16[240,256]{1,0:T(8,128)(2,1)}, bf16[240,256]{1,0:T(8,128)(2,1)S(1)}, u32[]{:S(2)}, u32[]{:S(2)}) collective-permute-start(bf16[240,256]{1,0:T(8,128)(2,1)} %get-tuple-element.100), channel_id=1, source_target_pairs={{0,10},{1,11},{2,8},{3,9},{4,14},{5,15},{6,12},{7,13},{8,2},{9,3},... | collective-permute-start | bytes 368648 | tf_op jit(solution)/shard_map/ppermute | solution.py:357
  38.9 41.3 %copy-start.24 = (bf16[240,256]{1,0:T(8,128)(2,1)}, bf16[240,256]{1,0:T(8,128)(2,1)S(1)}, u32[]{:S(2)}) copy-start(bf16[240,256]{1,0:T(8,128)(2,1)S(1)} %collective-permute-done.1.refs_1_) | copy-start | bytes 368644
  38.9 12.5 %collective-permute-start.6 = (bf16[240,256]{1,0:T(8,128)(2,1)}, bf16[240,256]{1,0:T(8,128)(2,1)S(1)}, u32[]{:S(2)}, u32[]{:S(2)}) collective-permute-start(bf16[240,256]{1,0:T(8,128)(2,1)} %get-tuple-element.101), channel_id=1, source_target_pairs={{0,12},{1,13},{2,14},{3,15},{4,8},{5,9},{6,10},{7,11},{8,4},{9,5},... | collective-permute-start | bytes 368648 | tf_op jit(solution)/shard_map/ppermute | solution.py:357
  43.8 16.5 %copy-start.25 = (bf16[240,256]{1,0:T(8,128)(2,1)}, bf16[240,256]{1,0:T(8,128)(2,1)S(1)}, u32[]{:S(2)}) copy-start(bf16[240,256]{1,0:T(8,128)(2,1)S(1)} %collective-permute-done.2.refs_2_) | copy-start | bytes 368644
  43.8 11.8 %collective-permute-start.7 = (bf16[240,256]{1,0:T(8,128)(2,1)}, bf16[240,256]{1,0:T(8,128)(2,1)S(1)}, u32[]{:S(2)}, u32[]{:S(2)}) collective-permute-start(bf16[240,256]{1,0:T(8,128)(2,1)} %get-tuple-element.102), channel_id=1, source_target_pairs={{0,14},{1,15},{2,12},{3,13},{4,10},{5,11},{6,8},{7,9},{8,6},{9,7},... | collective-permute-start | bytes 368648 | tf_op jit(solution)/shard_map/ppermute | solution.py:357
  47.2 13.1 %copy-start.26 = (bf16[240,256]{1,0:T(8,128)(2,1)}, bf16[240,256]{1,0:T(8,128)(2,1)S(1)}, u32[]{:S(2)}) copy-start(bf16[240,256]{1,0:T(8,128)(2,1)S(1)} %collective-permute-done.3.refs_3_) | copy-start | bytes 368644
  47.2 11.0 %collective-permute-start.8 = (bf16[2,192,256]{2,1,0:T(8,128)(2,1)}, bf16[2,192,256]{2,1,0:T(8,128)(2,1)S(1)}, u32[]{:S(2)}, u32[]{:S(2)}) collective-permute-start(bf16[2,192,256]{2,1,0:T(8,128)(2,1)} %get-tuple-element.103), channel_id=1, source_target_pairs={{0,4},{1,5},{2,6},{3,7},{4,0},{5,1},{6,2},{7,3},{8,12},{9,13},{10,... | collective-permute-start | bytes 589832 | tf_op jit(solution)/shard_map/ppermute | solution.py:357
  47.2 13.1 %copy-start.27 = (bf16[240,256]{1,0:T(8,128)(2,1)}, bf16[240,256]{1,0:T(8,128)(2,1)S(1)}, u32[]{:S(2)}) copy-start(bf16[240,256]{1,0:T(8,128)(2,1)S(1)} %collective-permute-done.4.refs_4_) | copy-start | bytes 368644
  47.2 11.0 %collective-permute-start.9 = (bf16[2,192,256]{2,1,0:T(8,128)(2,1)}, bf16[2,192,256]{2,1,0:T(8,128)(2,1)S(1)}, u32[]{:S(2)}, u32[]{:S(2)}) collective-permute-start(bf16[2,192,256]{2,1,0:T(8,128)(2,1)} %get-tuple-element.104), channel_id=1, source_target_pairs={{0,10},{1,11},{2,8},{3,9},{4,14},{5,15},{6,12},{7,13},{8,2},{9,3},... | collective-permute-start | bytes 589832 | tf_op jit(solution)/shard_map/ppermute | solution.py:357
  48.0 21.5 %copy-start.28 = (bf16[240,256]{1,0:T(8,128)(2,1)}, bf16[240,256]{1,0:T(8,128)(2,1)S(1)}, u32[]{:S(2)}) copy-start(bf16[240,256]{1,0:T(8,128)(2,1)S(1)} %collective-permute-done.5.refs_5_) | copy-start | bytes 368644
  48.0 21.5 %collective-permute-start.10 = (bf16[2,192,256]{2,1,0:T(8,128)(2,1)}, bf16[2,192,256]{2,1,0:T(8,128)(2,1)S(1)}, u32[]{:S(2)}, u32[]{:S(2)}) collective-permute-start(bf16[2,192,256]{2,1,0:T(8,128)(2,1)} %get-tuple-element.105), channel_id=1, source_target_pairs={{0,14},{1,15},{2,12},{3,13},{4,10},{5,11},{6,8},{7,9},{8,6},{9,7},... | collective-permute-start | bytes 589832 | tf_op jit(solution)/shard_map/ppermute | solution.py:357
  51.4 33.6 %copy-start.29 = (bf16[240,256]{1,0:T(8,128)(2,1)}, bf16[240,256]{1,0:T(8,128)(2,1)S(1)}, u32[]{:S(2)}) copy-start(bf16[240,256]{1,0:T(8,128)(2,1)S(1)} %collective-permute-done.6.refs_6_) | copy-start | bytes 368644
  51.4 18.1 %collective-permute-start.11 = (bf16[2,192,256]{2,1,0:T(8,128)(2,1)}, bf16[2,192,256]{2,1,0:T(8,128)(2,1)}, u32[]{:S(2)}, u32[]{:S(2)}) collective-permute-start(bf16[2,192,256]{2,1,0:T(8,128)(2,1)} %get-tuple-element.106), channel_id=1, source_target_pairs={{0,12},{1,13},{2,14},{3,15},{4,8},{5,9},{6,10},{7,11},{8,4},{9,5},... | collective-permute-start | bytes 589832 | tf_op jit(solution)/shard_map/ppermute | solution.py:357
  55.6 13.9 %copy-start.30 = (bf16[240,256]{1,0:T(8,128)(2,1)}, bf16[240,256]{1,0:T(8,128)(2,1)S(1)}, u32[]{:S(2)}) copy-start(bf16[240,256]{1,0:T(8,128)(2,1)S(1)} %collective-permute-done.7.refs_7_) | copy-start | bytes 368644
  55.6 16.5 %collective-permute-start.17 = (bf16[2,192,256]{2,1,0:T(8,128)(2,1)}, bf16[2,192,256]{2,1,0:T(8,128)(2,1)}, u32[]{:S(2)}, u32[]{:S(2)}) collective-permute-start(bf16[2,192,256]{2,1,0:T(8,128)(2,1)} %get-tuple-element.108), channel_id=1, source_target_pairs={{0,10},{1,11},{2,8},{3,9},{4,14},{5,15},{6,12},{7,13},{8,2},{9,3},... | collective-permute-start | bytes 589832 | tf_op jit(solution)/shard_map/ppermute | solution.py:357
  58.2 44.4 %copy-start.9 = (bf16[2,192,256]{2,1,0:T(8,128)(2,1)}, bf16[2,192,256]{2,1,0:T(8,128)(2,1)S(1)}, u32[]{:S(2)}) copy-start(bf16[2,192,256]{2,1,0:T(8,128)(2,1)S(1)} %collective-permute-done.8.refs_8_) | copy-start | bytes 589828
  58.2 20.8 %collective-permute-start.18 = (bf16[2,192,256]{2,1,0:T(8,128)(2,1)}, bf16[2,192,256]{2,1,0:T(8,128)(2,1)}, u32[]{:S(2)}, u32[]{:S(2)}) collective-permute-start(bf16[2,192,256]{2,1,0:T(8,128)(2,1)} %get-tuple-element.109), channel_id=1, source_target_pairs={{0,14},{1,15},{2,12},{3,13},{4,10},{5,11},{6,8},{7,9},{8,6},{9,7},... | collective-permute-start | bytes 589832 | tf_op jit(solution)/shard_map/ppermute | solution.py:357
  58.2 44.4 %copy-start.10 = (bf16[2,192,256]{2,1,0:T(8,128)(2,1)}, bf16[2,192,256]{2,1,0:T(8,128)(2,1)S(1)}, u32[]{:S(2)}) copy-start(bf16[2,192,256]{2,1,0:T(8,128)(2,1)S(1)} %collective-permute-done.9.refs_9_) | copy-start | bytes 589828
  58.3 21.9 %collective-permute-start.19 = (bf16[2,192,256]{2,1,0:T(8,128)(2,1)}, bf16[2,192,256]{2,1,0:T(8,128)(2,1)}, u32[]{:S(2)}, u32[]{:S(2)}) collective-permute-start(bf16[2,192,256]{2,1,0:T(8,128)(2,1)} %get-tuple-element.110), channel_id=1, source_target_pairs={{0,12},{1,13},{2,14},{3,15},{4,8},{5,9},{6,10},{7,11},{8,4},{9,5},... | collective-permute-start | bytes 589832 | tf_op jit(solution)/shard_map/ppermute | solution.py:357
  69.4 33.2 %copy-start.11 = (bf16[2,192,256]{2,1,0:T(8,128)(2,1)}, bf16[2,192,256]{2,1,0:T(8,128)(2,1)S(1)}, u32[]{:S(2)}) copy-start(bf16[2,192,256]{2,1,0:T(8,128)(2,1)S(1)} %collective-permute-done.10.refs_10_) | copy-start | bytes 589828
  69.4 12.5 %collective-permute-start.24 = (bf16[2,192,256]{2,1,0:T(8,128)(2,1)}, bf16[2,192,256]{2,1,0:T(8,128)(2,1)S(1)}, u32[]{:S(2)}, u32[]{:S(2)}) collective-permute-start(bf16[2,192,256]{2,1,0:T(8,128)(2,1)} %get-tuple-element.112), channel_id=1, source_target_pairs={{0,2},{1,3},{2,0},{3,1},{4,6},{5,7},{6,4},{7,5},{8,10},{9,11},{10,... | collective-permute-start | bytes 589832 | tf_op jit(solution)/shard_map/ppermute | solution.py:357
  69.5 13.9 %collective-permute-start.25 = (bf16[2,192,256]{2,1,0:T(8,128)(2,1)}, bf16[2,192,256]{2,1,0:T(8,128)(2,1)S(1)}, u32[]{:S(2)}, u32[]{:S(2)}) collective-permute-start(bf16[2,192,256]{2,1,0:T(8,128)(2,1)} %get-tuple-element.113), channel_id=1, source_target_pairs={{0,6},{1,7},{2,4},{3,5},{4,2},{5,3},{6,0},{7,1},{8,14},{9,15},{10,... | collective-permute-start | bytes 589832 | tf_op jit(solution)/shard_map/ppermute | solution.py:357
  72.1 11.3 %collective-permute-start.26 = (bf16[2,192,256]{2,1,0:T(8,128)(2,1)}, bf16[2,192,256]{2,1,0:T(8,128)(2,1)S(1)}, u32[]{:S(2)}, u32[]{:S(2)}) collective-permute-start(bf16[2,192,256]{2,1,0:T(8,128)(2,1)} %get-tuple-element.114), channel_id=1, source_target_pairs={{0,8},{1,9},{2,10},{3,11},{4,12},{5,13},{6,14},{7,15},{8,0},{9,1},... | collective-permute-start | bytes 589832 | tf_op jit(solution)/shard_map/ppermute | solution.py:357
  79.0 6.0 %collective-permute-start.27 = (bf16[2,192,256]{2,1,0:T(8,128)(2,1)}, bf16[2,192,256]{2,1,0:T(8,128)(2,1)}, u32[]{:S(2)}, u32[]{:S(2)}) collective-permute-start(bf16[2,192,256]{2,1,0:T(8,128)(2,1)} %get-tuple-element.111.refs_8_), channel_id=1, source_target_pairs={{0,1},{1,0},{2,3},{3,2},{4,5},{5,4},{6,7},{7,6},{8,9},{9,8},{10,11... | collective-permute-start | bytes 589832 | tf_op jit(solution)/shard_map/ppermute | solution.py:361
  80.2 4.9 %collective-permute-start.20 = (bf16[2,192,256]{2,1,0:T(8,128)(2,1)}, bf16[2,192,256]{2,1,0:T(8,128)(2,1)S(1)}, u32[]{:S(2)}, u32[]{:S(2)}) collective-permute-start(bf16[2,192,256]{2,1,0:T(8,128)(2,1)} %collective-permute-done.16.refs_16_), channel_id=1, source_target_pairs={{0,1},{1,0},{2,3},{3,2},{4,5},{5,4},{6,7},{7,6},{8,9},{9,8},{10,11... | collective-permute-start | bytes 589832 | tf_op jit(solution)/shard_map/ppermute | solution.py:361
  81.9 3.6 %collective-permute-start.35 = (bf16[2,192,256]{2,1,0:T(8,128)(2,1)}, bf16[2,192,256]{2,1,0:T(8,128)(2,1)S(1)}, u32[]{:S(2)}, u32[]{:S(2)}) collective-permute-start(bf16[2,192,256]{2,1,0:T(8,128)(2,1)} %collective-permute-done.31.refs_17_), channel_id=1, source_target_pairs={{0,1},{1,0},{2,3},{3,2},{4,5},{5,4},{6,7},{7,6},{8,9},{9,8},{10,11... | collective-permute-start | bytes 589832 | tf_op jit(solution)/shard_map/ppermute | solution.py:361
  83.4 2.2 %collective-permute-start.36 = (bf16[2,192,256]{2,1,0:T(8,128)(2,1)}, bf16[2,192,256]{2,1,0:T(8,128)(2,1)S(1)}, u32[]{:S(2)}, u32[]{:S(2)}) collective-permute-start(bf16[2,192,256]{2,1,0:T(8,128)(2,1)} %collective-permute-done.32.refs_18_), channel_id=1, source_target_pairs={{0,1},{1,0},{2,3},{3,2},{4,5},{5,4},{6,7},{7,6},{8,9},{9,8},{10,11... | collective-permute-start | bytes 589832 | tf_op jit(solution)/shard_map/ppermute | solution.py:361
  83.5 2.8 %collective-permute-start.37 = (bf16[2,192,256]{2,1,0:T(8,128)(2,1)}, bf16[2,192,256]{2,1,0:T(8,128)(2,1)S(1)}, u32[]{:S(2)}, u32[]{:S(2)}) collective-permute-start(bf16[2,192,256]{2,1,0:T(8,128)(2,1)} %collective-permute-done.33.refs_19_), channel_id=1, source_target_pairs={{0,1},{1,0},{2,3},{3,2},{4,5},{5,4},{6,7},{7,6},{8,9},{9,8},{10,11... | collective-permute-start | bytes 589832 | tf_op jit(solution)/shard_map/ppermute | solution.py:361
  85.0 1.7 collective-permute-start.12
  85.1 1.7 collective-permute-start.13
  85.5 1.7 collective-permute-start.28
  85.6 1.9 collective-permute-start.29
  86.3 1.7 collective-permute-start.30
  86.6 16.1 %collective-permute-start.14 = (bf16[2,192,256]{2,1,0:T(8,128)(2,1)S(1)}, bf16[2,192,256]{2,1,0:T(8,128)(2,1)}, u32[]{:S(2)}, u32[]{:S(2)}) collective-permute-start(bf16[2,192,256]{2,1,0:T(8,128)(2,1)S(1)} %collective-permute-done.10.refs_10_), channel_id=1, source_target_pairs={{0,1},{1,0},{2,3},{3,2},{4,5},{5,4},{6,7},{7,6},{8,9},{9,8},{10,11... | collective-permute-start | bytes 589832 | tf_op jit(solution)/shard_map/ppermute | solution.py:361
  86.8 15.9 %collective-permute-start.15 = (bf16[2,192,256]{2,1,0:T(8,128)(2,1)}, bf16[2,192,256]{2,1,0:T(8,128)(2,1)}, u32[]{:S(2)}, u32[]{:S(2)}) collective-permute-start(bf16[2,192,256]{2,1,0:T(8,128)(2,1)} %collective-permute-done.11.refs_11_), channel_id=1, source_target_pairs={{0,1},{1,0},{2,3},{3,2},{4,5},{5,4},{6,7},{7,6},{8,9},{9,8},{10,11... | collective-permute-start | bytes 589832 | tf_op jit(solution)/shard_map/ppermute | solution.py:361
  87.3 15.5 %collective-permute-start.21 = (bf16[2,192,256]{2,1,0:T(8,128)(2,1)}, bf16[2,192,256]{2,1,0:T(8,128)(2,1)}, u32[]{:S(2)}, u32[]{:S(2)}) collective-permute-start(bf16[2,192,256]{2,1,0:T(8,128)(2,1)} %collective-permute-done.17.refs_17_), channel_id=1, source_target_pairs={{0,1},{1,0},{2,3},{3,2},{4,5},{5,4},{6,7},{7,6},{8,9},{9,8},{10,11... | collective-permute-start | bytes 589832 | tf_op jit(solution)/shard_map/ppermute | solution.py:361
  87.5 15.2 %collective-permute-start.22 = (bf16[2,192,256]{2,1,0:T(8,128)(2,1)}, bf16[2,192,256]{2,1,0:T(8,128)(2,1)}, u32[]{:S(2)}, u32[]{:S(2)}) collective-permute-start(bf16[2,192,256]{2,1,0:T(8,128)(2,1)} %collective-permute-done.18.refs_18_), channel_id=1, source_target_pairs={{0,1},{1,0},{2,3},{3,2},{4,5},{5,4},{6,7},{7,6},{8,9},{9,8},{10,11... | collective-permute-start | bytes 589832 | tf_op jit(solution)/shard_map/ppermute | solution.py:361
  88.8 13.9 %collective-permute-start.23 = (bf16[2,192,256]{2,1,0:T(8,128)(2,1)}, bf16[2,192,256]{2,1,0:T(8,128)(2,1)}, u32[]{:S(2)}, u32[]{:S(2)}) collective-permute-start(bf16[2,192,256]{2,1,0:T(8,128)(2,1)} %collective-permute-done.19.refs_19_), channel_id=1, source_target_pairs={{0,1},{1,0},{2,3},{3,2},{4,5},{5,4},{6,7},{7,6},{8,9},{9,8},{10,11... | collective-permute-start | bytes 589832 | tf_op jit(solution)/shard_map/ppermute | solution.py:361
  119.9 18.2 %collective-permute-start.45 = (bf16[4,640,1280]{2,1,0:T(8,128)(2,1)}, bf16[4,640,1280]{2,1,0:T(8,128)(2,1)}, u32[]{:S(2)}, u32[]{:S(2)}) collective-permute-start(bf16[4,640,1280]{2,1,0:T(8,128)(2,1)} %bitcast.15), channel_id=1, source_target_pairs={{0,1},{1,0},{2,3},{3,2},{4,5},{5,4},{6,7},{7,6},{8,9},{9,8},{10,11... | collective-permute-start | bytes 19660808 | tf_op jit(solution)/shard_map/ppermute | solution.py:361
  120.1 5.1 %collective-permute-start.38 = (bf16[240,256]{1,0:T(8,128)(2,1)}, bf16[240,256]{1,0:T(8,128)(2,1)S(1)}, u32[]{:S(2)}, u32[]{:S(2)}) collective-permute-start(bf16[240,256]{1,0:T(8,128)(2,1)} %get-tuple-element.128), channel_id=1, source_target_pairs={{0,2},{1,3},{2,0},{3,1},{4,6},{5,7},{6,4},{7,5},{8,10},{9,11},{10,... | collective-permute-start | bytes 368648 | tf_op jit(solution)/shard_map/ppermute | solution.py:357
  121.5 7.1 %collective-permute-start.39 = (bf16[240,256]{1,0:T(8,128)(2,1)}, bf16[240,256]{1,0:T(8,128)(2,1)S(1)}, u32[]{:S(2)}, u32[]{:S(2)}) collective-permute-start(bf16[240,256]{1,0:T(8,128)(2,1)} %get-tuple-element.129), channel_id=1, source_target_pairs={{0,4},{1,5},{2,6},{3,7},{4,0},{5,1},{6,2},{7,3},{8,12},{9,13},{10,... | collective-permute-start | bytes 368648 | tf_op jit(solution)/shard_map/ppermute | solution.py:357
  122.6 8.8 %collective-permute-start.40 = (bf16[240,256]{1,0:T(8,128)(2,1)}, bf16[240,256]{1,0:T(8,128)(2,1)}, u32[]{:S(2)}, u32[]{:S(2)}) collective-permute-start(bf16[240,256]{1,0:T(8,128)(2,1)} %get-tuple-element.130), channel_id=1, source_target_pairs={{0,6},{1,7},{2,4},{3,5},{4,2},{5,3},{6,0},{7,1},{8,14},{9,15},{10,... | collective-permute-start | bytes 368648 | tf_op jit(solution)/shard_map/ppermute | solution.py:357
  124.0 9.8 %collective-permute-start.41 = (bf16[240,256]{1,0:T(8,128)(2,1)}, bf16[240,256]{1,0:T(8,128)(2,1)}, u32[]{:S(2)}, u32[]{:S(2)}) collective-permute-start(bf16[240,256]{1,0:T(8,128)(2,1)} %get-tuple-element.131), channel_id=1, source_target_pairs={{0,8},{1,9},{2,10},{3,11},{4,12},{5,13},{6,14},{7,15},{8,0},{9,1},... | collective-permute-start | bytes 368648 | tf_op jit(solution)/shard_map/ppermute | solution.py:357
  125.2 12.8 %copy-start.1 = (bf16[240,256]{1,0:T(8,128)(2,1)}, bf16[240,256]{1,0:T(8,128)(2,1)S(1)}, u32[]{:S(2)}) copy-start(bf16[240,256]{1,0:T(8,128)(2,1)S(1)} %collective-permute-done.38.refs_1_) | copy-start | bytes 368644
  125.2 8.6 %collective-permute-start.42 = (bf16[240,256]{1,0:T(8,128)(2,1)}, bf16[240,256]{1,0:T(8,128)(2,1)}, u32[]{:S(2)}, u32[]{:S(2)}) collective-permute-start(bf16[240,256]{1,0:T(8,128)(2,1)} %get-tuple-element.132), channel_id=1, source_target_pairs={{0,10},{1,11},{2,8},{3,9},{4,14},{5,15},{6,12},{7,13},{8,2},{9,3},... | collective-permute-start | bytes 368648 | tf_op jit(solution)/shard_map/ppermute | solution.py:357
  128.7 6.4 %collective-permute-start.43 = (bf16[240,256]{1,0:T(8,128)(2,1)}, bf16[240,256]{1,0:T(8,128)(2,1)}, u32[]{:S(2)}, u32[]{:S(2)}) collective-permute-start(bf16[240,256]{1,0:T(8,128)(2,1)} %get-tuple-element.133), channel_id=1, source_target_pairs={{0,12},{1,13},{2,14},{3,15},{4,8},{5,9},{6,10},{7,11},{8,4},{9,5},... | collective-permute-start | bytes 368648 | tf_op jit(solution)/shard_map/ppermute | solution.py:357
  131.4 6.6 %collective-permute-start.44 = (bf16[240,256]{1,0:T(8,128)(2,1)}, bf16[240,256]{1,0:T(8,128)(2,1)}, u32[]{:S(2)}, u32[]{:S(2)}) collective-permute-start(bf16[240,256]{1,0:T(8,128)(2,1)} %get-tuple-element.134), channel_id=1, source_target_pairs={{0,14},{1,15},{2,12},{3,13},{4,10},{5,11},{6,8},{7,9},{8,6},{9,7},... | collective-permute-start | bytes 368648 | tf_op jit(solution)/shard_map/ppermute | solution.py:357
  133.8 12.0 %copy-start.4 = (s32[3]{0:T(128)S(1)}, s32[3]{0:T(128)}, u32[]{:S(2)}) copy-start(s32[3]{0:T(128)} %pad_add_fusion.meta) | copy-start | bytes 40
  153.8 43.4 %collective-permute-start.46 = (bf16[384,2560]{1,0:T(8,128)(2,1)}, bf16[384,2560]{1,0:T(8,128)(2,1)S(1)}, u32[]{:S(2)}, u32[]{:S(2)}) collective-permute-start(bf16[384,2560]{1,0:T(8,128)(2,1)} %project.3), channel_id=1, source_target_pairs={{0,16},{16,0},{1,17},{17,1},{2,18},{18,2},{3,19},{19,3},{4,20},{20... | collective-permute-start | bytes 5898248 | tf_op jit(solution)/shard_map/ppermute | solution.py:365
  (16 other events, 42.0 us)
Sparse Core Ops, SparseCore 0:
  10.6 70.9 all-gather.2

commit v2 on v1

v2 whole, which is shorter than its diff:
```python
import functools
import math

import jax
import jax.numpy as jnp
from jax import lax
from jax.experimental import pallas as pl
from jax.experimental.pallas import tpu as pltpu
from jax.sharding import PartitionSpec as P

HEAD_DIM = 128
GRID_H = 8
GRID_W = 16
CAP = 30
HD = 2560
SPAN = 96
ROWS = 192
HEADS = 10
FEATURES = HEADS * HEAD_DIM
CHIPS = 8
PART = 48
SLOT = ROWS + PART
TILE_Q = 384
TILE_K = 768
SCALE = 1.0 / math.sqrt(HEAD_DIM)
BF16 = jnp.bfloat16
F32 = jnp.float32
MIB = 2**20
SMEM = pl.BlockSpec(memory_space=pltpu.SMEM)


def params(mib):
    return pltpu.CompilerParams(vmem_limit_bytes=mib * MIB)


def cost(flops, moved):
    return pl.CostEstimate(flops=flops, bytes_accessed=moved, transcendentals=0)


def shape(*dims, kind=BF16):
    return jax.ShapeDtypeStruct(dims, kind)


def whole(member):
    return pl.BlockSpec(member.shape, lambda step: (0,) * len(member.shape))


def call(kernel, name, outs, operands, scratch, mib, estimate, scalars=0):
    return pl.pallas_call(
        kernel,
        grid=(1,),
        out_shape=outs,
        in_specs=[SMEM] * scalars + [whole(member) for member in operands[scalars:]],
        out_specs=jax.tree.map(whole, outs),
        scratch_shapes=scratch,
        compiler_params=params(mib),
        cost_estimate=estimate,
        name=name,
    )(*operands)


def dot(left, right):
    return lax.dot_general(left, right, (((1,), (0,)), ((), ())), preferred_element_type=F32)


def dot_rows(left, right):
    return lax.dot_general(left, right, (((1,), (1,)), ((), ())), preferred_element_type=F32)


def rope_tables(own_spans):
    positions = (
        own_spans[:, None] * SPAN + jnp.arange(SPAN, dtype=jnp.int32)[None, :]
    ).reshape(-1)
    pairs = HEAD_DIM // 2
    side = pairs // 3
    time = pairs - 2 * side
    time_freq = 10000.0 ** (-jnp.arange(time, dtype=F32) / time)
    side_freq = 10000.0 ** (-jnp.arange(side, dtype=F32) / side)
    freq = jnp.concatenate([time_freq, side_freq, side_freq])
    freq = jnp.broadcast_to(freq[:, None], (pairs, 2)).reshape(1, HEAD_DIM)
    pair = (jnp.arange(HEAD_DIM, dtype=jnp.int32) // 2)[None, :]
    place = jnp.where(
        pair < time,
        (positions // (GRID_H * GRID_W))[:, None],
        jnp.where(
            pair < time + side,
            (positions // GRID_W % GRID_H)[:, None],
            (positions % GRID_W)[:, None],
        ),
    ).astype(F32)
    angle = place * freq
    return jnp.cos(angle), jnp.sin(angle)


def prepare_kernel(q, qt, k, kt, v, vt, out, stats):
    for chip in range(CHIPS):
        for place, head in ((0, chip), (1, CHIPS + chip // 4)):
            columns = slice(head * HEAD_DIM, (head + 1) * HEAD_DIM)
            out[chip, place, :, :HEAD_DIM] = v[:, columns]
            out[chip, place, :, HEAD_DIM:] = vt[:, columns]
    lane = lax.broadcasted_iota(jnp.int32, (ROWS, HEAD_DIM), 1)
    total = jnp.zeros((ROWS, HEAD_DIM), F32)
    for place, (left, right) in enumerate(((q, q), (q, qt), (k, k), (k, kt))):
        product = left[...].astype(F32) * right[...].astype(F32)
        total = jnp.where(lane == place, jnp.sum(product, axis=1, keepdims=True), total)
    stats[...] = total


def prepare(*operands):
    return call(
        prepare_kernel,
        "prepare",
        [shape(CHIPS, 2, ROWS, 256), shape(ROWS, HEAD_DIM, kind=F32)],
        operands,
        [],
        60,
        cost(8 * ROWS * FEATURES, 6 * MIB),
    )


def norm_rope_kernel(q, qt, k, kt, mine, theirs, q_gain, k_gain, cosine, sine, out):
    stats = mine[...] + theirs[...]
    cos = cosine[...]
    even = lax.broadcasted_iota(jnp.int32, (ROWS, HEAD_DIM), 1) % 2 == 0
    sin_next = jnp.where(even, -sine[...], 0.0)
    sin_last = jnp.where(even, 0.0, sine[...])

    def rotated(x):
        after = pltpu.roll(x, HEAD_DIM - 1, 1)
        before = pltpu.roll(x, 1, 1)
        return (x * cos + (after * sin_next + before * sin_last)).astype(BF16)

    def of_head(raw_ref, tangent_ref, gain_ref, inverse, mixing, head):
        columns = slice(head * HEAD_DIM, (head + 1) * HEAD_DIM)
        raw = raw_ref[:, columns].astype(F32)
        tangent = tangent_ref[:, columns].astype(F32)
        gain = gain_ref[:, columns]
        normed = gain * raw * inverse
        normed_tangent = gain * (
            tangent * inverse - raw * mixing * inverse * inverse * inverse
        )
        return rotated(normed), rotated(normed_tangent)

    wide = (ROWS, HEAD_DIM)
    for first, raw_ref, tangent_ref, gain_ref in ((2, k, kt, k_gain), (0, q, qt, q_gain)):
        inverse = jnp.broadcast_to(lax.rsqrt(stats[:, first : first + 1] / HD + 1e-06), wide)
        mixing = jnp.broadcast_to(stats[:, first + 1 : first + 2] / HD, wide)
        for head in range(HEADS):
            turned = jnp.concatenate(
                of_head(raw_ref, tangent_ref, gain_ref, inverse, mixing, head), axis=1
            )
            low = 0 if first else 2 * ROWS
            if head < CHIPS:
                out[head, low : low + ROWS] = turned
                continue
            for column in range(4):
                chip = 4 * (head - CHIPS) + column
                if first:
                    out[chip, ROWS : 2 * ROWS] = turned
                else:
                    out[chip, 3 * ROWS :] = turned[column * PART : (column + 1) * PART]


def norm_rope(*operands):
    return call(
        norm_rope_kernel,
        "norm_rope",
        [shape(CHIPS, 2 * ROWS + SLOT, 256)],
        operands,
        [],
        60,
        cost(40 * ROWS * FEATURES, 5 * MIB),
    )[0]


def attend_kernel(mixed, mixed_other, v_in, v_other, out, keys, values, queries, results, sems):
    copies = []

    def copy(source, target):
        copies.append(pltpu.make_async_copy(source, target, sems.at[len(copies)]))
        copies[-1].start()

    main = CHIPS * ROWS
    for chip in range(CHIPS):
        copy(mixed.at[chip, 2 * ROWS : 3 * ROWS], queries.at[chip * ROWS : (chip + 1) * ROWS])
        low = main + chip * PART
        copy(mixed.at[chip, 3 * ROWS :], queries.at[low : low + PART])
    asked = len(copies)
    for place in range(2):
        for chunk in range(2 * CHIPS):
            rows = slice(chunk * ROWS, (chunk + 1) * ROWS)
            k_from, v_from = ((mixed, v_in), (mixed_other, v_other))[chunk // CHIPS]
            chip = chunk % CHIPS
            copy(k_from.at[chip, place * ROWS : (place + 1) * ROWS], keys.at[place, rows])
            copy(v_from.at[chip, place], values.at[place, rows])
    per_step = 2 * TILE_K // ROWS
    steps = 2 * CHIPS * ROWS // TILE_K

    def one_tile(start, size, place, wait):
        both = queries[pl.ds(start, size)]
        plain = both[:, :HEAD_DIM]
        crossed = jnp.concatenate([both[:, HEAD_DIM:], plain], axis=1)
        weighted = jnp.zeros((size, 256), F32)
        weighted_tangent = jnp.zeros((size, HEAD_DIM), F32)
        norm_lanes = jnp.zeros((size, HEAD_DIM), F32)
        tangent_lanes = jnp.zeros((size, HEAD_DIM), F32)
        for step in range(steps):
            if wait:
                low = asked + (place * steps + step) * per_step
                for member in copies[low : low + per_step]:
                    member.wait()
            rows = slice(step * TILE_K, (step + 1) * TILE_K)
            key_rows = keys[place, rows]
            value_rows = values[place, rows]
            scores = dot_rows(plain, key_rows[:, :HEAD_DIM])
            scores_tangent = dot_rows(crossed, key_rows) * SCALE
            squashed = jnp.tanh(scores * (SCALE / CAP))
            weights = jnp.exp2(squashed * (CAP * math.log2(math.e)))
            weights_tangent = weights * ((1.0 - squashed * squashed) * scores_tangent)
            for low in range(0, TILE_K, HEAD_DIM):
                norm_lanes = norm_lanes + weights[:, low : low + HEAD_DIM]
                tangent_lanes = tangent_lanes + weights_tangent[:, low : low + HEAD_DIM]
            weighted = weighted + dot(weights.astype(BF16), value_rows)
            weighted_tangent = weighted_tangent + dot(
                weights_tangent.astype(BF16), value_rows[:, :HEAD_DIM]
            )
        inverse = 1.0 / jnp.sum(norm_lanes, axis=1, keepdims=True)
        shift = jnp.sum(tangent_lanes, axis=1, keepdims=True) * inverse
        attention = weighted[:, :HEAD_DIM] * inverse
        attention_tangent = (
            weighted[:, HEAD_DIM:] + weighted_tangent
        ) * inverse - shift * attention
        outcome = jnp.concatenate([attention, attention_tangent], axis=1)
        results[pl.ds(start, size)] = outcome.astype(BF16)

    for member in copies[:asked]:
        member.wait()
    one_tile(0, TILE_Q, 0, True)

    def later(tile, carry):
        one_tile(pl.multiple_of(tile * TILE_Q, TILE_Q), TILE_Q, 0, False)
        return carry

    lax.fori_loop(1, main // TILE_Q, later, 0)
    one_tile(main, CHIPS * PART, 1, True)
    for group in range(2):
        for chip in range(CHIPS):
            out[group, chip, :ROWS] = results[chip * ROWS : (chip + 1) * ROWS]
            low = main + chip * PART
            out[group, chip, ROWS:] = results[low : low + PART]


def attend(*operands):
    anywhere = pl.BlockSpec(memory_space=pl.ANY)
    outs = [shape(2, CHIPS, SLOT, 256)]
    return pl.pallas_call(
        attend_kernel,
        grid=(1,),
        out_shape=outs,
        in_specs=[anywhere] * len(operands),
        out_specs=jax.tree.map(whole, outs),
        scratch_shapes=[
            pltpu.VMEM((2, 2 * CHIPS * ROWS, 256), BF16),
            pltpu.VMEM((2, 2 * CHIPS * ROWS, 256), BF16),
            pltpu.VMEM((CHIPS * SLOT, 256), BF16),
            pltpu.VMEM((CHIPS * SLOT, 256), BF16),
            pltpu.SemaphoreType.DMA((10 * CHIPS,)),
        ],
        compiler_params=params(60),
        cost_estimate=cost(8 * 256 * CHIPS * SLOT * 2 * CHIPS * ROWS, 14 * MIB),
        name="attend",
    )(*operands)[0]


def project_kernel(meta, parts, *refs):
    pieces = refs[:6]
    out, out_tangent, left = refs[6:]

    @pl.when(pl.program_id(0) == 0)
    def _():
        for group in range(2):
            first = HEADS * jnp.bitwise_xor(group, meta[2])
            start = HEADS - meta[1] * (HEADS // 2)

            def column(head, first=first, start=start):
                return first + (head + start) % HEADS

            for chip in range(CHIPS):
                part = parts.at[group, chip]
                for side in range(2):
                    lanes = slice(side * HEAD_DIM, (side + 1) * HEAD_DIM)
                    top = side * ROWS
                    left[column(chip), top : top + ROWS] = part[:ROWS, lanes]
                    low = top + chip % 4 * PART
                    left[column(CHIPS + chip // 4), low : low + PART] = part[ROWS:, lanes]

    rows = jnp.concatenate([left[head] for head in range(2 * HEADS)], axis=1)
    for low in range(0, out.shape[1], 256):
        right = jnp.concatenate([piece[0, :, low : low + 256] for piece in pieces], axis=0)
        result = dot(rows, right).astype(out.dtype)
        out[:, low : low + 256] = result[:ROWS]
        out_tangent[:, low : low + 256] = result[ROWS:]


def project(meta, parts, own, cross):
    quarter = FEATURES // 4
    wide = FEATURES
    count = FEATURES // wide

    def straight(step, meta):
        return (2 * meta[2] + step // count, 0, step % count)

    def mirrored(step, meta):
        return (3 - 2 * meta[2] - step // count, 0, step % count)

    half_spec = pl.BlockSpec((1, 2 * quarter, wide), straight)
    quarter_specs = [pl.BlockSpec((1, quarter, wide), place) for place in (straight, mirrored)]
    out = shape(ROWS, 2 * FEATURES)
    out_spec = pl.BlockSpec((ROWS, wide), lambda step, meta: (0, step))
    return pl.pallas_call(
        project_kernel,
        out_shape=[out, out],
        grid_spec=pltpu.PrefetchScalarGridSpec(
            num_scalar_prefetch=1,
            grid=(2 * count,),
            in_specs=[pl.BlockSpec(parts.shape, lambda step, meta: (0, 0, 0, 0))]
            + [half_spec] * 2
            + quarter_specs * 2,
            out_specs=[out_spec, out_spec],
            scratch_shapes=[pltpu.VMEM((2 * HEADS, 2 * ROWS, HEAD_DIM), BF16)],
        ),
        compiler_params=params(60),
        cost_estimate=cost(2 * 2 * ROWS * 2 * FEATURES * 2 * FEATURES, 18 * MIB),
        name="project",
    )(meta, parts, *own, *[member for member in cross for _ in range(2)])


HOME = [(clip, group) for clip in range(4) for group in range(2) if clip // 2 == group]
AWAY = [(clip, group) for clip in range(4) for group in range(2) if clip // 2 != group]
CORES = [[2 * chip + core for chip in range(CHIPS)] for core in range(2)]
GROUP_CORES = [
    [16 * group + 2 * chip + core for group in range(2) for chip in range(CHIPS)]
    for core in range(2)
]


def to_chips(array):
    return lax.all_to_all(array, "ctx", 0, 0, axis_index_groups=CORES, tiled=True)


def to_core(array):
    return lax.ppermute(array, "ctx", [(place, place ^ 1) for place in range(16)])


def after(arrays, event):
    return lax.optimization_barrier((arrays, event))[0]


def move(array, pairs):
    pairs = [(2 * a + b, 2 * c + d) for (a, b), (c, d) in pairs]
    return lax.ppermute(array, ("dp", "head"), pairs)


def to_group(array):
    return lax.ppermute(array, "head", [(0, 1), (1, 0)])


def on_device(
    query_input,
    key_input,
    value_input,
    query_tangent,
    key_tangent,
    value_tangent,
    query_gain,
    key_gain,
    out_weight,
    span_order,
):
    place = lax.axis_index("ctx")
    group = lax.axis_index("head")
    chip, core = place // 2, place % 2
    meta = jnp.stack([chip, core, group]).astype(jnp.int32)
    half = FEATURES // 2
    own_rows = lax.dynamic_slice_in_dim(out_weight, core * half, half, 0)
    own_weight = lax.all_gather(own_rows, "dp", axis=0)

    raw = [
        member[0]
        for member in (
            query_input,
            query_tangent,
            key_input,
            key_tangent,
            value_input,
            value_tangent,
        )
    ]
    value_out, stats = prepare(*raw)
    values = to_chips(value_out)
    stats_peer = to_group(stats)
    cosine, sine = rope_tables(lax.dynamic_slice_in_dim(span_order, 2 * place, 2))
    gains = (query_gain[None], key_gain[None])
    values, stats_peer, cosine, sine, gains = lax.optimization_barrier(
        (values, stats_peer, cosine, sine, gains)
    )
    values_other = to_core(values)
    quarter = half // 2
    home = lax.axis_index("dp") // 2 == group
    lower, upper = [
        after(lax.dynamic_slice_in_dim(out_weight, core * half + low, quarter, 0), values)
        for low in (0, quarter)
    ]
    near = move(lower, [((clip, own), (clip, 1 - own)) for clip, own in AWAY])
    far = move(upper, [((clip, own), (3 - clip, 1 - own)) for clip, own in AWAY])
    mixed_out = norm_rope(*raw[:4], stats, stats_peer, *gains, cosine, sine)
    mixed = to_chips(after(mixed_out, values_other))
    near, far = after((near, far), mixed)
    cross_weight = lax.all_gather(jnp.where(home, near, far), "dp", axis=0)
    mixed_other = to_core(mixed)
    own_other = to_core(after(own_weight, mixed_other))
    results = attend(mixed, mixed_other, values, values_other)
    parts = lax.all_to_all(
        results.reshape(2 * CHIPS, SLOT, 256),
        ("head", "ctx"),
        0,
        0,
        axis_index_groups=GROUP_CORES,
        tiled=True,
    )
    cross_other = to_core(after(cross_weight, parts))
    projected, tangent = project(
        meta,
        parts.reshape(2, CHIPS, SLOT, 256),
        (own_weight, own_other),
        (cross_weight, cross_other),
    )
    return (projected[None], tangent[None])


def solution(mesh):
    return jax.shard_map(
        on_device,
        mesh=mesh,
        in_specs=(
            P("dp", "ctx", "head"),
            P("dp", "ctx", "head"),
            P("dp", "ctx", "head"),
            P("dp", "ctx", "head"),
            P("dp", "ctx", "head"),
            P("dp", "ctx", "head"),
            P("head"),
            P("head"),
            P("head", "dp"),
            P(),
        ),
        out_specs=(P("dp", "ctx", "head"), P("dp", "ctx", "head")),
        check_vma=False,
    )
```

time: 211 us -> 191 us (0.905)
  blocking collectives: 0 us -> 34.8 us
  starting transfers between devices: 51.9 us -> 23.9 us
  waiting for transfers between devices: 75 us -> 62.5 us
  Pallas kernels: 54.5 us -> 43.1 us
    all_to_all x0 -> x2, waiting for transfers between devices: none -> 40.7 us  [to_chips(): lax.all_to_all(array, 'ctx', 0, 0, axis_index_groups=CORES, tiled=True)]
    all_to_all x0 -> x1, blocking collectives: none -> 34.8 us  [on_device(): lax.all_to_all(results.reshape(2 * CHIPS, SLOT, 256), ('head', 'ctx'), 0,...]
    ppermute x28 -> x2, starting transfers between devices: 36.7 us -> 1.99 us  [move(): return lax.ppermute(array, ('dp', 'head'), pairs)]
    ppermute x2 -> x1, waiting for transfers between devices: 42.1 us -> 12.1 us  [to_group(): return lax.ppermute(array, 'head', [(0, 1), (1, 0)])]
    pallas_call x4 -> x2, Pallas kernels: 39.3 us -> 9.39 us  [call(): pl.pallas_call(kernel, grid=(1,), out_shape=outs, in_specs=[SMEM] * scala...]
    ppermute x28 -> x2, waiting for transfers between devices: 32.6 us -> 4.57 us  [move(): return lax.ppermute(array, ('dp', 'head'), pairs)]
    pallas_call x2, Pallas kernels: 15.2 us -> 33.7 us  [the longest x1 22 us: attend(): pl.pallas_call(attend_kernel, grid=(1,), out_shape=outs, in_specs=[anywhe...]
    all_to_all x0 -> x2, starting transfers between devices: none -> 13.2 us  [to_chips(): lax.all_to_all(array, 'ctx', 0, 0, axis_index_groups=CORES, tiled=True)]
  transfers between devices with their start and end apart: 48 -> 11, of which waited for: 13 -> 5; matrix products, arithmetic and copies ran while one was open for 2% -> 3% of each run, Pallas kernels for 19% -> 17%
where the time goes in v2:
time: 191 us; the launch traced here: 189 us
  waiting for transfers between devices  62.5 us (33%)
  Pallas kernels  43.1 us (23%)
  blocking collectives  34.8 us (18%)
  starting transfers between devices  23.9 us (13%)
  between operations  14.2 us (7%)
  local copies, waits for them, and re-layouts  7.19 us (4%)
  other arithmetic  3.03 us (2%)
    all_to_all x2, waiting for transfers between devices, to_chips(): lax.all_to_all(array, 'ctx', 0, 0, axis_index_groups=CORES, tiled=True)  40.7 us
    all_to_all x1, blocking collectives, on_device(): lax.all_to_all(results.reshape(2 * CHIPS, SLOT, 256), ('head', 'ctx'), 0,...  34.8 us
    pallas_call x1, Pallas kernels, attend(): pl.pallas_call(attend_kernel, grid=(1,), out_shape=outs, in_specs=[anywhe...  22 us
    all_to_all x2, starting transfers between devices, to_chips(): lax.all_to_all(array, 'ctx', 0, 0, axis_index_groups=CORES, tiled=True)  13.2 us
    ppermute x1, waiting for transfers between devices, to_group(): return lax.ppermute(array, 'head', [(0, 1), (1, 0)])  12.1 us
    pallas_call x1, Pallas kernels, project(): pl.pallas_call(project_kernel, out_shape=[out, out], grid_spec=pltpu.Pref...  11.7 us
    pallas_call x2, Pallas kernels, call(): pl.pallas_call(kernel, grid=(1,), out_shape=outs, in_specs=[SMEM] * scala...  9.39 us
    ppermute x4, starting transfers between devices, to_core(): lax.ppermute(array, 'ctx', [(place, place ^ 1) for place in range(16)])  5.2 us
  transfers between devices with their start and end apart: 11, of which 5 were waited for; matrix products, arithmetic and copies ran while one was open for 3% of the time, Pallas kernels for 17%

profile of v2, /device:TPU:1, one launch (start us, length us, event | category | flops | bytes accessed | tf_op | source)
XLA Modules:
  0.0 188.7 jit_solution(17157680652289083353)
XLA Ops:
  7.2 0.0 all-gather.5.cloned.1.call-start
  7.2 2.7 %constant_dynamic-slice_fusion.2 = bf16[640,1280]{1,0:T(8,128)(2,1)} fusion(bf16[1280,1280]{1,0:T(8,128)(2,1)} %param.18, s32[]{:T(128)S(6)} %select_n.98), kind=kLoop, calls=%fused_computation.24 | loop fusion | bytes 3276804 | tf_op jit(solution)/shard_map/dynamic_slice | solution.py:385
  9.9 0.0 all-gather.5.cloned.1.call-update
  10.0 0.0 copy-start.6
  10.0 0.0 copy-start.4
  10.0 0.0 copy-start.5
  10.0 3.6 %prepare.1 = (bf16[8,2,192,256]{3,2,1,0:T(8,128)(2,1)}, f32[192,128]{1,0:T(8,128)}) custom-call(bf16[192,1280]{1,0:T(8,128)(2,1)} %bitcast.22, bf16[192,1280]{1,0:T(8,128)(2,1)} %bitcast.24, bf16[192,1280]{1,0:T(8,128)(2,1)} %bitcast.26, bf16[192,1280]{1,0:T(8,128)(2,1)} %bitcast.28, bf16[192,1280]{1,0:T(8,128)(2,1)} %bitcast.30, bf16[192,1280]{1,0:T(8,128)(2,1)} %bitcast.31), custom_call_target="tpu_custom_call" | custom-call | flops 1966080 | bytes 6291456 | tf_op jit(solution)/shard_map/prepare/pallas_call | solution.py:49
  13.6 0.0 copy-start.2
  13.6 6.5 %all-to-all-start = ((bf16[8,2,192,256]{3,2,1,0:T(8,128)(2,1)}), bf16[8,2,192,256]{3,2,1,0:T(8,128)(2,1)}, u32[]{:S(2)}, u32[]{:S(2)}) async-start(bf16[8,2,192,256]{3,2,1,0:T(8,128)(2,1)} %get-tuple-element.20), calls=%async_computation | async-start | bytes 3145728 | tf_op jit(solution)/shard_map/all_to_all | solution.py:348
  20.1 0.0 copy-done.2
  20.1 3.4 %collective-permute-start = (f32[192,128]{1,0:T(8,128)S(1)}, f32[192,128]{1,0:T(8,128)S(1)}, u32[]{:S(2)}, u32[]{:S(2)}) collective-permute-start(f32[192,128]{1,0:T(8,128)S(1)} %copy-done.2), channel_id=1, source_target_pairs={{0,16},{16,0},{1,17},{17,1},{2,18},{18,2},{3,19},{19,3},{4,20},{20... | collective-permute-start | bytes 294920 | tf_op jit(solution)/shard_map/ppermute | solution.py:365
  23.5 0.0 copy-done.6
  23.5 0.1 dynamic-slice_multiply_fusion
  23.6 0.1 iota_add_fusion
  23.7 0.1 add.89
  23.8 0.1 pad_maximum_fusion
  23.8 0.1 broadcast_in_dim.69
  23.9 0.2 mul.24
  24.1 1.2 fusion
  25.3 0.0 copy-done.4
  25.3 0.6 broadcast_in_dim.70.q_gain
  25.9 0.0 copy-done.5
  25.9 0.6 broadcast_in_dim.71.k_gain
  26.5 12.1 %collective-permute-done.theirs = f32[192,128]{1,0:T(8,128)S(1)} collective-permute-done((f32[192,128]{1,0:T(8,128)S(1)}, f32[192,128]{1,0:T(8,128)S(1)}, u32[]{:S(2)}, u32[]{:S(2)}) %collective-permute-start) | collective-permute-done | bytes 98336 | tf_op jit(solution)/shard_map/ppermute | solution.py:365
  38.6 0.0 copy-start.3
  38.6 3.1 %all-to-all-done.v_in = bf16[8,2,192,256]{3,2,1,0:T(8,128)(2,1)} async-done(((bf16[8,2,192,256]{3,2,1,0:T(8,128)(2,1)}), bf16[8,2,192,256]{3,2,1,0:T(8,128)(2,1)}, u32[]{:S(2)}, u32[]{:S(2)}) %all-to-all-start) | async-done | bytes 1572896 | tf_op jit(solution)/shard_map/all_to_all | solution.py:348
  41.6 0.8 collective-permute-start.1
  42.5 0.0 copy-done.3
  42.5 5.8 %norm_rope.1 = bf16[8,624,256]{2,1,0:T(8,128)(2,1)} custom-call(bf16[192,1280]{1,0:T(8,128)(2,1)} %bitcast.23, bf16[192,1280]{1,0:T(8,128)(2,1)} %bitcast.25, bf16[192,1280]{1,0:T(8,128)(2,1)} %bitcast.27, bf16[192,1280]{1,0:T(8,128)(2,1)} %bitcast.29, f32[192,128]{1,0:T(8,128)} %get-tuple-element.19.mine, f32[192,128]{1,0:T(8,128)} %copy-done.3, ...), custom_call_target="tpu_custom_call" | custom-call | flops 9830400 | bytes 5242880 | tf_op jit(solution)/shard_map/norm_rope/pallas_call | solution.py:49
  48.3 0.0 copy-start.1
  48.3 0.0 collective-permute-done.1.v_other
  48.3 6.7 %all-to-all-start.1 = ((bf16[8,624,256]{2,1,0:T(8,128)(2,1)}), bf16[8,624,256]{2,1,0:T(8,128)(2,1)}, u32[]{:S(2)}, u32[]{:S(2)}) async-start(bf16[8,624,256]{2,1,0:T(8,128)(2,1)} %norm_rope.1), calls=%async_computation.1 | async-start | bytes 5111808 | tf_op jit(solution)/shard_map/all_to_all | solution.py:348
  55.0 0.0 all-gather.7.cloned.1.call-start
  55.1 0.0 copy-done.1
  55.1 1.3 constant_dynamic-slice_fusion
  56.4 1.3 collective-permute-start.4
  57.7 0.7 collective-permute-start.5
  58.4 37.6 %all-to-all-done.1.mixed = bf16[8,624,256]{2,1,0:T(8,128)(2,1)} async-done(((bf16[8,624,256]{2,1,0:T(8,128)(2,1)}), bf16[8,624,256]{2,1,0:T(8,128)(2,1)}, u32[]{:S(2)}, u32[]{:S(2)}) %all-to-all-start.1) | async-done | bytes 2555936 | tf_op jit(solution)/shard_map/all_to_all | solution.py:348
  96.0 1.7 collective-permute-start.2
  97.6 4.6 %collective-permute-done.4 = bf16[320,1280]{1,0:T(8,128)(2,1)S(1)} collective-permute-done((bf16[320,1280]{1,0:T(8,128)(2,1)}, bf16[320,1280]{1,0:T(8,128)(2,1)S(1)}, u32[]{:S(2)}, u32[]{:S(2)}) %collective-permute-start.4) | collective-permute-done | bytes 819232 | tf_op jit(solution)/shard_map/ppermute | solution.py:361
  102.2 0.0 collective-permute-done.5
  102.2 1.0 broadcast_select_fusion
  103.2 0.0 all-gather.7.cloned.1.call-update
  103.2 0.0 collective-permute-done.2.mixed_other
  103.2 0.0 all-gather.5.cloned.1.call-done
  103.2 1.1 collective-permute-start.3
  104.4 22.0 %attend.1 = bf16[2,8,240,256]{3,2,1,0:T(8,128)(2,1)} custom-call(bf16[8,624,256]{2,1,0:T(8,128)(2,1)} %all-to-all-done.1.mixed, bf16[8,624,256]{2,1,0:T(8,128)(2,1)} %collective-permute-done.2.mixed_other, bf16[8,2,192,256]{3,2,1,0:T(8,128)(2,1)} %all-to-all-done.v_in, bf16[8,2,192,256]{3,2,1,0:T(8,128)(2,1)} %collective-permute-done.1.v_other), custom_call_target="tpu_custom_call" | custom-call | flops 12079595520 | bytes 14680064 | tf_op jit(solution)/shard_map/attend/pallas_call | solution.py:256
  126.4 34.8 %all_to_all.15 = bf16[16,240,256]{2,1,0:T(8,128)(2,1)} all-to-all(bf16[16,240,256]{2,1,0:T(8,128)(2,1)} %bitcast.21), channel_id=1, replica_groups={{0,2,4,6,8,10,12,14,16,18,20,22,24,26,28,30},{1,3,5,7,9,11,13,15,17,19,..., dimensions={0} | all-to-all | bytes 3932160 | tf_op jit(solution)/shard_map/all_to_all | solution.py:423
  161.2 0.0 all-gather.7.cloned.1.call-done
  161.2 1.6 collective-permute-start.6
  162.8 0.6 pad_add_fusion.meta
  163.4 5.1 %collective-permute-done.6.refs_4_.refs_5_ = bf16[4,320,1280]{2,1,0:T(8,128)(2,1)S(1)} collective-permute-done((bf16[4,320,1280]{2,1,0:T(8,128)(2,1)}, bf16[4,320,1280]{2,1,0:T(8,128)(2,1)S(1)}, u32[]{:S(2)}, u32[]{:S(2)}) %collective-permute-start.6) | collective-permute-done | bytes 3276832 | tf_op jit(solution)/shard_map/ppermute | solution.py:352
  168.5 0.0 copy-start
  168.5 0.0 collective-permute-done.3.refs_1_
  168.5 1.7 copy-done
  170.1 11.7 %project.1 = (bf16[192,2560]{1,0:T(8,128)(2,1)}, bf16[192,2560]{1,0:T(8,128)(2,1)}) custom-call(s32[3]{0:T(128)} %pad_add_fusion.meta, bf16[2,8,240,256]{3,2,1,0:T(8,128)(2,1)} %bitcast.18, bf16[4,640,1280]{2,1,0:T(8,128)(2,1)} %bitcast.20, bf16[4,640,1280]{2,1,0:T(8,128)(2,1)} %collective-permute-done.3.refs_1_, bf16[4,320,1280]{2,1,0:T(8,128)(2,1)} %bitcast.16, ...), custom_call_target="tpu_custom_call" | custom-call | flops 5033164800 | bytes 18874368 | tf_op jit(solution)/shard_map/project/pallas_call | solution.py:320
  (4 shorter events, 0.0 us)
Async XLA Ops:
  7.2 96.1 %all-gather.5.cloned.1.call-start = ((), (), s32[]{:S(2)}) async-start(), calls=%async_computation.3 | async-start | bytes 8192000 | tf_op jit(solution)/shard_map/all_gather | solution.py:386
  10.0 13.5 %copy-start.6 = (s32[32]{0:T(128)S(1)}, s32[32]{0:T(128)}, u32[]{:S(2)}) copy-start(s32[32]{0:T(128)} %param.19) | copy-start | bytes 388
  10.0 15.3 %copy-start.4 = (f32[1280]{0:T(1024)S(1)}, f32[1280]{0:T(1024)}, u32[]{:S(2)}) copy-start(f32[1280]{0:T(1024)} %param.16) | copy-start | bytes 15364
  10.0 15.9 %copy-start.5 = (f32[1280]{0:T(1024)S(1)}, f32[1280]{0:T(1024)}, u32[]{:S(2)}) copy-start(f32[1280]{0:T(1024)} %param.17) | copy-start | bytes 15364
  13.6 6.5 %copy-start.2 = (f32[192,128]{1,0:T(8,128)S(1)}, f32[192,128]{1,0:T(8,128)}, u32[]{:S(2)}) copy-start(f32[192,128]{1,0:T(8,128)} %get-tuple-element.19.mine) | copy-start | bytes 294916
  13.6 28.0 %all-to-all-start = ((bf16[8,2,192,256]{3,2,1,0:T(8,128)(2,1)}), bf16[8,2,192,256]{3,2,1,0:T(8,128)(2,1)}, u32[]{:S(2)}, u32[]{:S(2)}) async-start(bf16[8,2,192,256]{3,2,1,0:T(8,128)(2,1)} %get-tuple-element.20), calls=%async_computation | async-start | bytes 3145728 | tf_op jit(solution)/shard_map/all_to_all | solution.py:348
  20.1 18.4 %collective-permute-start = (f32[192,128]{1,0:T(8,128)S(1)}, f32[192,128]{1,0:T(8,128)S(1)}, u32[]{:S(2)}, u32[]{:S(2)}) collective-permute-start(f32[192,128]{1,0:T(8,128)S(1)} %copy-done.2), channel_id=1, source_target_pairs={{0,16},{16,0},{1,17},{17,1},{2,18},{18,2},{3,19},{19,3},{4,20},{20... | collective-permute-start | bytes 294920 | tf_op jit(solution)/shard_map/ppermute | solution.py:365
  38.6 3.9 %copy-start.3 = (f32[192,128]{1,0:T(8,128)}, f32[192,128]{1,0:T(8,128)S(1)}, u32[]{:S(2)}) copy-start(f32[192,128]{1,0:T(8,128)S(1)} %collective-permute-done.theirs) | copy-start | bytes 294916
  41.6 6.6 %collective-permute-start.1 = (bf16[8,2,192,256]{3,2,1,0:T(8,128)(2,1)}, bf16[8,2,192,256]{3,2,1,0:T(8,128)(2,1)}, u32[]{:S(2)}, u32[]{:S(2)}) collective-permute-start(bf16[8,2,192,256]{3,2,1,0:T(8,128)(2,1)} %all-to-all-done.v_in), channel_id=1, source_target_pairs={{0,1},{1,0},{2,3},{3,2},{4,5},{5,4},{6,7},{7,6},{8,9},{9,8},{10,11... | collective-permute-start | bytes 4718600 | tf_op jit(solution)/shard_map/ppermute | solution.py:352
  48.3 6.8 %copy-start.1 = (bf16[1280,1280]{1,0:T(8,128)(2,1)S(1)}, bf16[1280,1280]{1,0:T(8,128)(2,1)}, u32[]{:S(2)}) copy-start(bf16[1280,1280]{1,0:T(8,128)(2,1)} %param.18) | copy-start | bytes 9830404
  48.3 47.7 %all-to-all-start.1 = ((bf16[8,624,256]{2,1,0:T(8,128)(2,1)}), bf16[8,624,256]{2,1,0:T(8,128)(2,1)}, u32[]{:S(2)}, u32[]{:S(2)}) async-start(bf16[8,624,256]{2,1,0:T(8,128)(2,1)} %norm_rope.1), calls=%async_computation.1 | async-start | bytes 5111808 | tf_op jit(solution)/shard_map/all_to_all | solution.py:348
  55.0 106.2 %all-gather.7.cloned.1.call-start = ((), (), s32[]{:S(2)}) async-start(), calls=%async_computation.4 | async-start | bytes 4096000 | tf_op jit(solution)/shard_map/all_gather | solution.py:419
  56.4 45.8 %collective-permute-start.4 = (bf16[320,1280]{1,0:T(8,128)(2,1)}, bf16[320,1280]{1,0:T(8,128)(2,1)S(1)}, u32[]{:S(2)}, u32[]{:S(2)}) collective-permute-start(bf16[320,1280]{1,0:T(8,128)(2,1)} %get-tuple-element.29), channel_id=1, source_target_pairs={{16,0},{48,32},{64,80},{96,112},{17,1},{49,33},{65,81},{97,113},{1... | collective-permute-start | bytes 2457608 | tf_op jit(solution)/shard_map/ppermute | solution.py:361
  57.7 44.5 %collective-permute-start.5 = (bf16[320,1280]{1,0:T(8,128)(2,1)}, bf16[320,1280]{1,0:T(8,128)(2,1)S(1)}, u32[]{:S(2)}, u32[]{:S(2)}) collective-permute-start(bf16[320,1280]{1,0:T(8,128)(2,1)} %get-tuple-element.30), channel_id=1, source_target_pairs={{16,96},{48,64},{64,48},{96,16},{17,97},{49,65},{65,49},{97,17},{1... | collective-permute-start | bytes 2457608 | tf_op jit(solution)/shard_map/ppermute | solution.py:361
  96.0 7.2 %collective-permute-start.2 = (bf16[8,624,256]{2,1,0:T(8,128)(2,1)}, bf16[8,624,256]{2,1,0:T(8,128)(2,1)}, u32[]{:S(2)}, u32[]{:S(2)}) collective-permute-start(bf16[8,624,256]{2,1,0:T(8,128)(2,1)} %all-to-all-done.1.mixed), channel_id=1, source_target_pairs={{0,1},{1,0},{2,3},{3,2},{4,5},{5,4},{6,7},{7,6},{8,9},{9,8},{10,11... | collective-permute-start | bytes 7667720 | tf_op jit(solution)/shard_map/ppermute | solution.py:352
  103.2 65.2 %collective-permute-start.3 = (bf16[4,640,1280]{2,1,0:T(8,128)(2,1)}, bf16[4,640,1280]{2,1,0:T(8,128)(2,1)}, u32[]{:S(2)}, u32[]{:S(2)}) collective-permute-start(bf16[4,640,1280]{2,1,0:T(8,128)(2,1)} %bitcast.19), channel_id=1, source_target_pairs={{0,1},{1,0},{2,3},{3,2},{4,5},{5,4},{6,7},{7,6},{8,9},{9,8},{10,11... | collective-permute-start | bytes 19660808 | tf_op jit(solution)/shard_map/ppermute | solution.py:352
  161.2 7.3 %collective-permute-start.6 = (bf16[4,320,1280]{2,1,0:T(8,128)(2,1)}, bf16[4,320,1280]{2,1,0:T(8,128)(2,1)S(1)}, u32[]{:S(2)}, u32[]{:S(2)}) collective-permute-start(bf16[4,320,1280]{2,1,0:T(8,128)(2,1)} %bitcast.15), channel_id=1, source_target_pairs={{0,1},{1,0},{2,3},{3,2},{4,5},{5,4},{6,7},{7,6},{8,9},{9,8},{10,11... | collective-permute-start | bytes 9830408 | tf_op jit(solution)/shard_map/ppermute | solution.py:352
  168.5 1.7 copy-start
Sparse Core Ops, SparseCore 0:
  10.1 88.3 all-gather.4
  103.3 43.6 all-gather.6

commit v3 on v2

--- a/solution.py
+++ b/solution.py
@@ -21,7 +21,7 @@
 PART = 48
 SLOT = ROWS + PART
 TILE_Q = 384
-TILE_K = 768
+TILE_K = 256
 SCALE = 1.0 / math.sqrt(HEAD_DIM)
 BF16 = jnp.bfloat16
 F32 = jnp.float32
@@ -193,8 +193,9 @@
             chip = chunk % CHIPS
             copy(k_from.at[chip, place * ROWS : (place + 1) * ROWS], keys.at[place, rows])
             copy(v_from.at[chip, place], values.at[place, rows])
-    per_step = 2 * TILE_K // ROWS
     steps = 2 * CHIPS * ROWS // TILE_K
+    group = 3 * TILE_K
+    per_group = 2 * group // ROWS
 
     def one_tile(start, size, place, wait):
         both = queries[pl.ds(start, size)]
@@ -204,26 +205,37 @@
         weighted_tangent = jnp.zeros((size, HEAD_DIM), F32)
         norm_lanes = jnp.zeros((size, HEAD_DIM), F32)
         tangent_lanes = jnp.zeros((size, HEAD_DIM), F32)
-        for step in range(steps):
-            if wait:
-                low = asked + (place * steps + step) * per_step
-                for member in copies[low : low + per_step]:
+
+        def rows(step):
+            return slice(step * TILE_K, (step + 1) * TILE_K)
+
+        def score(step):
+            if wait and step % 3 == 0:
+                low = asked + (place * steps + step) // 3 * per_group
+                for member in copies[low : low + per_group]:
                     member.wait()
-            rows = slice(step * TILE_K, (step + 1) * TILE_K)
-            key_rows = keys[place, rows]
-            value_rows = values[place, rows]
-            scores = dot_rows(plain, key_rows[:, :HEAD_DIM])
-            scores_tangent = dot_rows(crossed, key_rows) * SCALE
-            squashed = jnp.tanh(scores * (SCALE / CAP))
-            weights = jnp.exp2(squashed * (CAP * math.log2(math.e)))
-            weights_tangent = weights * ((1.0 - squashed * squashed) * scores_tangent)
-            for low in range(0, TILE_K, HEAD_DIM):
-                norm_lanes = norm_lanes + weights[:, low : low + HEAD_DIM]
-                tangent_lanes = tangent_lanes + weights_tangent[:, low : low + HEAD_DIM]
-            weighted = weighted + dot(weights.astype(BF16), value_rows)
-            weighted_tangent = weighted_tangent + dot(
-                weights_tangent.astype(BF16), value_rows[:, :HEAD_DIM]
-            )
+            key_rows = keys[place, rows(step)]
+            return dot_rows(plain, key_rows[:, :HEAD_DIM]), dot_rows(crossed, key_rows)
+
+        ahead, behind = score(0), None
+        for step in range(steps + 1):
+            if step < steps:
+                scores, scores_tangent = ahead
+                if step + 1 < steps:
+                    ahead = score(step + 1)
+                squashed = jnp.tanh(scores * (SCALE / CAP))
+                weights = jnp.exp2(squashed * (CAP * math.log2(math.e)))
+                weights_tangent = weights * (
+                    (1.0 - squashed * squashed) * (scores_tangent * SCALE)
+                )
+                for low in range(0, TILE_K, HEAD_DIM):
+                    norm_lanes = norm_lanes + weights[:, low : low + HEAD_DIM]
+                    tangent_lanes = tangent_lanes + weights_tangent[:, low : low + HEAD_DIM]
+            if step > 0:
+                value_rows = values[place, rows(step - 1)]
+                weighted = weighted + dot(behind[0], value_rows)
+                weighted_tangent = weighted_tangent + dot(behind[1], value_rows[:, :HEAD_DIM])
+            behind = (weights.astype(BF16), weights_tangent.astype(BF16))
         inverse = 1.0 / jnp.sum(norm_lanes, axis=1, keepdims=True)
         shift = jnp.sum(tangent_lanes, axis=1, keepdims=True) * inverse
         attention = weighted[:, :HEAD_DIM] * inverse
@@ -272,67 +284,77 @@
     )(*operands)[0]
 
 
-def project_kernel(meta, parts, *refs):
-    pieces = refs[:6]
-    out, out_tangent, left = refs[6:]
+def project_kernel(last, meta, parts, *refs):
+    pieces, refs = refs[:4], refs[4:]
+    before, refs = (refs[0], refs[1:]) if last else (None, refs)
+    outs, left = refs[:-1], refs[-1]
 
     @pl.when(pl.program_id(0) == 0)
     def _():
-        for group in range(2):
-            first = HEADS * jnp.bitwise_xor(group, meta[2])
-            start = HEADS - meta[1] * (HEADS // 2)
-
-            def column(head, first=first, start=start):
-                return first + (head + start) % HEADS
-
-            for chip in range(CHIPS):
-                part = parts.at[group, chip]
-                for side in range(2):
-                    lanes = slice(side * HEAD_DIM, (side + 1) * HEAD_DIM)
-                    top = side * ROWS
-                    left[column(chip), top : top + ROWS] = part[:ROWS, lanes]
-                    low = top + chip % 4 * PART
-                    left[column(CHIPS + chip // 4), low : low + PART] = part[ROWS:, lanes]
-
-    rows = jnp.concatenate([left[head] for head in range(2 * HEADS)], axis=1)
-    for low in range(0, out.shape[1], 256):
-        right = jnp.concatenate([piece[0, :, low : low + 256] for piece in pieces], axis=0)
-        result = dot(rows, right).astype(out.dtype)
-        out[:, low : low + 256] = result[:ROWS]
-        out_tangent[:, low : low + 256] = result[ROWS:]
-
-
-def project(meta, parts, own, cross):
+        def column(head):
+            return (head + HEADS - meta[1] * (HEADS // 2)) % HEADS
+
+        for chip in range(CHIPS):
+            part = parts.at[0, chip]
+            for side in range(2):
+                lanes = slice(side * HEAD_DIM, (side + 1) * HEAD_DIM)
+                top = side * ROWS
+                left[column(chip), top : top + ROWS] = part[:ROWS, lanes]
+                low = top + chip % 4 * PART
+                left[column(CHIPS + chip // 4), low : low + PART] = part[ROWS:, lanes]
+
+    rows = jnp.concatenate([left[head] for head in range(HEADS)], axis=1)
+    for low in range(0, FEATURES, 256):
+        columns = slice(low, low + 256)
+        right = jnp.concatenate([piece[0, :, columns] for piece in pieces], axis=0)
+        result = dot(rows, right)
+        if last:
+            result = result + before[:, columns]
+            outs[0][:, columns] = result[:ROWS].astype(BF16)
+            outs[1][:, columns] = result[ROWS:].astype(BF16)
+        else:
+            outs[0][:, columns] = result
+
+
+def project(meta, parts, weights, before=None):
+    last = before is not None
     quarter = FEATURES // 4
-    wide = FEATURES
-    count = FEATURES // wide
 
     def straight(step, meta):
-        return (2 * meta[2] + step // count, 0, step % count)
+        return (2 * meta[2] + step, 0, 0)
 
     def mirrored(step, meta):
-        return (3 - 2 * meta[2] - step // count, 0, step % count)
-
-    half_spec = pl.BlockSpec((1, 2 * quarter, wide), straight)
-    quarter_specs = [pl.BlockSpec((1, quarter, wide), place) for place in (straight, mirrored)]
-    out = shape(ROWS, 2 * FEATURES)
-    out_spec = pl.BlockSpec((ROWS, wide), lambda step, meta: (0, step))
+        return (3 - 2 * meta[2] - step, 0, 0)
+
+    def of_group(step, meta):
+        return (1 - meta[2] if last else meta[2], 0, 0, 0)
+
+    def columns(rows):
+        return pl.BlockSpec((rows, FEATURES), lambda step, meta: (0, step))
+
+    specs = [pl.BlockSpec((1, CHIPS, SLOT, 256), of_group)]
+    specs += [pl.BlockSpec((1, quarter, FEATURES), at) for at in (straight, mirrored)] * 2
+    operands = [member for member in weights for _ in range(2)]
+    if last:
+        operands += [before]
+        specs += [columns(2 * ROWS)]
+        outs, out_specs = [shape(ROWS, 2 * FEATURES)] * 2, [columns(ROWS)] * 2
+    else:
+        outs, out_specs = [shape(2 * ROWS, 2 * FEATURES, kind=F32)], [columns(2 * ROWS)]
     return pl.pallas_call(
-        project_kernel,
-        out_shape=[out, out],
+        functools.partial(project_kernel, last),
+        out_shape=outs,
         grid_spec=pltpu.PrefetchScalarGridSpec(
             num_scalar_prefetch=1,
-            grid=(2 * count,),
-            in_specs=[pl.BlockSpec(parts.shape, lambda step, meta: (0, 0, 0, 0))]
-            + [half_spec] * 2
-            + quarter_specs * 2,
-            out_specs=[out_spec, out_spec],
-            scratch_shapes=[pltpu.VMEM((2 * HEADS, 2 * ROWS, HEAD_DIM), BF16)],
+            grid=(2,),
+            in_specs=specs,
+            out_specs=out_specs,
+            scratch_shapes=[pltpu.VMEM((HEADS, 2 * ROWS, HEAD_DIM), BF16)],
         ),
         compiler_params=params(60),
-        cost_estimate=cost(2 * 2 * ROWS * 2 * FEATURES * 2 * FEATURES, 18 * MIB),
+        cost_estimate=cost(2 * 2 * ROWS * FEATURES * 2 * FEATURES, 12 * MIB),
         name="project",
-    )(meta, parts, *own, *[member for member in cross for _ in range(2)])
+    )(meta, parts, *operands)
 
 
 HOME = [(clip, group) for clip in range(4) for group in range(2) if clip // 2 == group]
@@ -357,8 +379,13 @@
 
 
 def move(array, pairs):
-    pairs = [(2 * a + b, 2 * c + d) for (a, b), (c, d) in pairs]
-    return lax.ppermute(array, ("dp", "head"), pairs)
+    links = []
+    for (clip, group), (next_clip, next_group) in pairs:
+        flip = 8 * (group ^ next_group)
+        for place in range(16):
+            source = 32 * clip + 16 * group + place
+            links.append((source, 32 * next_clip + 16 * next_group + (place ^ flip)))
+    return lax.ppermute(array, ("dp", "head", "ctx"), links)
 
 
 def to_group(array):
@@ -381,10 +408,6 @@
     group = lax.axis_index("head")
     chip, core = place // 2, place % 2
     meta = jnp.stack([chip, core, group]).astype(jnp.int32)
-    half = FEATURES // 2
-    own_rows = lax.dynamic_slice_in_dim(out_weight, core * half, half, 0)
-    own_weight = lax.all_gather(own_rows, "dp", axis=0)
-
     raw = [
         member[0]
         for member in (
@@ -396,23 +419,27 @@
             value_tangent,
         )
     ]
+    quarter = FEATURES // 4
+    home = lax.axis_index("dp") // 2 == group
+    lower, upper = [
+        lax.dynamic_slice_in_dim(out_weight, (2 * core + part) * quarter, quarter, 0)
+        for part in range(2)
+    ]
+    second = move(upper, [((clip, own), (3 - clip, own)) for clip, own in HOME])
     value_out, stats = prepare(*raw)
     values = to_chips(value_out)
     stats_peer = to_group(stats)
+    second, stats_peer = lax.optimization_barrier((second, stats_peer))
     cosine, sine = rope_tables(lax.dynamic_slice_in_dim(span_order, 2 * place, 2))
     gains = (query_gain[None], key_gain[None])
     values, stats_peer, cosine, sine, gains = lax.optimization_barrier(
         (values, stats_peer, cosine, sine, gains)
     )
+    own_piece = jnp.where(home, lower, second)
+    own_weight = lax.all_gather(own_piece, "dp", axis=0)
     values_other = to_core(values)
-    quarter = half // 2
-    home = lax.axis_index("dp") // 2 == group
-    lower, upper = [
-        after(lax.dynamic_slice_in_dim(out_weight, core * half + low, quarter, 0), values)
-        for low in (0, quarter)
-    ]
-    near = move(lower, [((clip, own), (clip, 1 - own)) for clip, own in AWAY])
-    far = move(upper, [((clip, own), (3 - clip, 1 - own)) for clip, own in AWAY])
+    near = move(after(lower, values), [((clip, own), (clip, 1 - own)) for clip, own in AWAY])
+    far = move(after(upper, values), [((clip, own), (3 - clip, 1 - own)) for clip, own in AWAY])
     mixed_out = norm_rope(*raw[:4], stats, stats_peer, *gains, cosine, sine)
     mixed = to_chips(after(mixed_out, values_other))
     near, far = after((near, far), mixed)
@@ -429,12 +456,9 @@
         tiled=True,
     )
     cross_other = to_core(after(cross_weight, parts))
-    projected, tangent = project(
-        meta,
-        parts.reshape(2, CHIPS, SLOT, 256),
-        (own_weight, own_other),
-        (cross_weight, cross_other),
-    )
+    parts = parts.reshape(2, CHIPS, SLOT, 256)
+    own = project(meta, parts, (own_weight, own_other))[0]
+    projected, tangent = project(meta, parts, (cross_weight, cross_other), own)
     return (projected[None], tangent[None])
 
 

time: 191 us -> 180 us (0.942)
  blocking collectives: 34.8 us -> 0 us
  waiting for transfers between devices: 62.5 us -> 76.4 us
  starting transfers between devices: 23.9 us -> 34.1 us
  local copies, waits for them, and re-layouts: 7.19 us -> 2.73 us
  other arithmetic: 3.03 us -> 6.78 us
    all_to_all x1 -> x0, blocking collectives: 34.8 us -> none  [on_device(): lax.all_to_all(results.reshape(2 * CHIPS, SLOT, 256), ('head', 'ctx'), 0,...]
    all_to_all x0 -> x1, waiting for transfers between devices: none -> 29.1 us  [on_device(): lax.all_to_all(results.reshape(2 * CHIPS, SLOT, 256), ('head', 'ctx'), 0,...]
    all_to_all x0 -> x1, starting transfers between devices: none -> 12.7 us  [on_device(): lax.all_to_all(results.reshape(2 * CHIPS, SLOT, 256), ('head', 'ctx'), 0,...]
    ppermute x1, waiting for transfers between devices: 12.1 us -> 0.01 us  [to_group(): return lax.ppermute(array, 'head', [(0, 1), (1, 0)])]
    ppermute x2 -> x3, starting transfers between devices: 1.99 us -> 8.18 us  [move(): return lax.ppermute(array, ('dp', 'head', 'ctx'), links)]
    all_to_all x2, starting transfers between devices: 13.2 us -> 8.88 us  [to_chips(): lax.all_to_all(array, 'ctx', 0, 0, axis_index_groups=CORES, tiled=True)]
    pallas_call x1 -> x2, Pallas kernels: 11.7 us -> 15.6 us  [project(): pl.pallas_call(functools.partial(project_kernel, last), out_shape=outs, g...]
    all_to_all x2, waiting for transfers between devices: 40.7 us -> 37.6 us  [to_chips(): lax.all_to_all(array, 'ctx', 0, 0, axis_index_groups=CORES, tiled=True)]
  transfers between devices with their start and end apart: 11 -> 13, of which waited for: 5 -> 5; matrix products, arithmetic and copies ran while one was open for 3% -> 5% of each run, Pallas kernels for 17% -> 21%
where the time goes in v3:
time: 180 us; the launch traced here: 179 us
  waiting for transfers between devices  76.4 us (42%)
  Pallas kernels  44.8 us (25%)
  starting transfers between devices  34.1 us (19%)
  between operations  14.2 us (8%)
  other arithmetic  6.78 us (4%)
  local copies, waits for them, and re-layouts  2.73 us (2%)
    all_to_all x2, waiting for transfers between devices, to_chips(): lax.all_to_all(array, 'ctx', 0, 0, axis_index_groups=CORES, tiled=True)  37.6 us
    all_to_all x1, waiting for transfers between devices, on_device(): lax.all_to_all(results.reshape(2 * CHIPS, SLOT, 256), ('head', 'ctx'), 0,...  29.1 us
    pallas_call x1, Pallas kernels, attend(): pl.pallas_call(attend_kernel, grid=(1,), out_shape=outs, in_specs=[anywhe...  19.7 us
    pallas_call x2, Pallas kernels, project(): pl.pallas_call(functools.partial(project_kernel, last), out_shape=outs, g...  15.6 us
    all_to_all x1, starting transfers between devices, on_device(): lax.all_to_all(results.reshape(2 * CHIPS, SLOT, 256), ('head', 'ctx'), 0,...  12.7 us
    pallas_call x2, Pallas kernels, call(): pl.pallas_call(kernel, grid=(1,), out_shape=outs, in_specs=[SMEM] * scala...  9.44 us
    all_to_all x2, starting transfers between devices, to_chips(): lax.all_to_all(array, 'ctx', 0, 0, axis_index_groups=CORES, tiled=True)  8.88 us
    ppermute x3, starting transfers between devices, move(): return lax.ppermute(array, ('dp', 'head', 'ctx'), links)  8.18 us
  transfers between devices with their start and end apart: 13, of which 5 were waited for; matrix products, arithmetic and copies ran while one was open for 5% of the time, Pallas kernels for 21%

profile of v3, /device:TPU:1, one launch (start us, length us, event | category | flops | bytes accessed | tf_op | source)
XLA Modules:
  0.0 179.0 jit_solution(12461593463487257004)
XLA Ops:
  7.2 1.2 constant_dynamic-slice_fusion.1
  8.4 0.0 copy-start.6
  8.4 5.3 %collective-permute-start = (bf16[320,1280]{1,0:T(8,128)(2,1)S(1)}, bf16[320,1280]{1,0:T(8,128)(2,1)S(1)}, u32[]{:S(2)}, u32[]{:S(2)}) collective-permute-start(bf16[320,1280]{1,0:T(8,128)(2,1)S(1)} %constant_dynamic-slice_fusion.1), channel_id=1, source_target_pairs={{0,96},{1,97},{2,98},{3,99},{4,100},{5,101},{6,102},{7,103},{8,104... | collective-permute-start | bytes 2457608 | tf_op jit(solution)/shard_map/ppermute | solution.py:388
  13.7 3.6 %prepare.1 = (bf16[8,2,192,256]{3,2,1,0:T(8,128)(2,1)}, f32[192,128]{1,0:T(8,128)}) custom-call(bf16[192,1280]{1,0:T(8,128)(2,1)} %bitcast.24, bf16[192,1280]{1,0:T(8,128)(2,1)} %bitcast.26, bf16[192,1280]{1,0:T(8,128)(2,1)} %bitcast.28, bf16[192,1280]{1,0:T(8,128)(2,1)} %bitcast.30, bf16[192,1280]{1,0:T(8,128)(2,1)} %bitcast.32, bf16[192,1280]{1,0:T(8,128)(2,1)} %bitcast.33), custom_call_target="tpu_custom_call" | custom-call | flops 1966080 | bytes 6291456 | tf_op jit(solution)/shard_map/prepare/pallas_call | solution.py:49
  17.3 0.5 collective-permute-start.1
  17.7 0.0 copy-start.4
  17.7 0.0 copy-start.5
  17.7 5.2 %all-to-all-start = ((bf16[8,2,192,256]{3,2,1,0:T(8,128)(2,1)}), bf16[8,2,192,256]{3,2,1,0:T(8,128)(2,1)S(1)}, u32[]{:S(2)}, u32[]{:S(2)}) async-start(bf16[8,2,192,256]{3,2,1,0:T(8,128)(2,1)} %get-tuple-element.22), calls=%async_computation | async-start | bytes 3145728 | tf_op jit(solution)/shard_map/all_to_all | solution.py:370
  23.0 0.0 all-gather.7.cloned.1.call-start
  23.0 0.0 copy-done.6
  23.1 0.1 dynamic-slice_multiply_fusion
  23.1 0.1 iota_add_fusion
  23.2 0.0 collective-permute-done.1.theirs
  23.2 0.0 copy-start.3
  23.3 7.3 %collective-permute-done = bf16[320,1280]{1,0:T(8,128)(2,1)S(1)} collective-permute-done((bf16[320,1280]{1,0:T(8,128)(2,1)S(1)}, bf16[320,1280]{1,0:T(8,128)(2,1)S(1)}, u32[]{:S(2)}, u32[]{:S(2)}) %collective-permute-start) | collective-permute-done | bytes 819232 | tf_op jit(solution)/shard_map/ppermute | solution.py:388
  30.5 2.5 %broadcast_select_fusion = (bf16[320,1280]{1,0:T(8,128)(2,1)}, bf16[320,1280]{1,0:T(8,128)(2,1)}) fusion(bf16[320,1280]{1,0:T(8,128)(2,1)S(1)} %collective-permute-done, pred[]{:T(512)S(6)} %eq.8, bf16[1280,1280]{1,0:T(8,128)(2,1)} %param.18, s32[]{:T(128)S(6)} %select_n.104), kind=kLoop, calls=%fused_computation | loop fusion | flops 409600 | bytes 3276805 | tf_op jit(solution)/shard_map/jit(_where)/select_n | solution.py:438
  33.0 0.0 all-gather.7.cloned.1.call-update
  33.0 0.1 pad_maximum_fusion
  33.1 0.1 add.88
  33.2 0.1 broadcast_in_dim.69
  33.3 0.1 mul.31
  33.4 0.0 copy-done.4
  33.4 0.6 broadcast_in_dim.70.q_gain
  34.0 0.0 copy-done.5
  34.0 0.6 broadcast_in_dim.71.k_gain
  34.7 1.2 fusion
  35.8 8.6 %all-to-all-done.v_in = bf16[8,2,192,256]{3,2,1,0:T(8,128)(2,1)S(1)} async-done(((bf16[8,2,192,256]{3,2,1,0:T(8,128)(2,1)}), bf16[8,2,192,256]{3,2,1,0:T(8,128)(2,1)S(1)}, u32[]{:S(2)}, u32[]{:S(2)}) %all-to-all-start) | async-done | bytes 1572896 | tf_op jit(solution)/shard_map/all_to_all | solution.py:370
  44.4 0.0 copy-start.2
  44.4 0.9 collective-permute-start.2
  45.3 0.0 copy-done.3
  45.3 5.8 %norm_rope.1 = bf16[8,624,256]{2,1,0:T(8,128)(2,1)} custom-call(bf16[192,1280]{1,0:T(8,128)(2,1)} %bitcast.25, bf16[192,1280]{1,0:T(8,128)(2,1)} %bitcast.27, bf16[192,1280]{1,0:T(8,128)(2,1)} %bitcast.29, bf16[192,1280]{1,0:T(8,128)(2,1)} %bitcast.31, f32[192,128]{1,0:T(8,128)} %get-tuple-element.21.mine, f32[192,128]{1,0:T(8,128)} %copy-done.3, ...), custom_call_target="tpu_custom_call" | custom-call | flops 9830400 | bytes 5242880 | tf_op jit(solution)/shard_map/norm_rope/pallas_call | solution.py:49
  51.1 0.0 collective-permute-done.2.v_other
  51.1 0.0 copy-done.2
  51.1 3.6 %all-to-all-start.1 = ((bf16[8,624,256]{2,1,0:T(8,128)(2,1)}), bf16[8,624,256]{2,1,0:T(8,128)(2,1)S(1)}, u32[]{:S(2)}, u32[]{:S(2)}) async-start(bf16[8,624,256]{2,1,0:T(8,128)(2,1)} %norm_rope.1), calls=%async_computation.1 | async-start | bytes 5111808 | tf_op jit(solution)/shard_map/all_to_all | solution.py:370
  54.8 0.0 all-gather.5.cloned.1.call-start
  54.8 1.3 collective-permute-start.4
  56.1 1.6 collective-permute-start.5
  57.7 29.0 %all-to-all-done.1.mixed = bf16[8,624,256]{2,1,0:T(8,128)(2,1)S(1)} async-done(((bf16[8,624,256]{2,1,0:T(8,128)(2,1)}), bf16[8,624,256]{2,1,0:T(8,128)(2,1)S(1)}, u32[]{:S(2)}, u32[]{:S(2)}) %all-to-all-start.1) | async-done | bytes 2555936 | tf_op jit(solution)/shard_map/all_to_all | solution.py:370
  86.7 0.0 copy-start.1
  86.7 0.8 collective-permute-start.3
  87.5 0.0 collective-permute-done.4
  87.5 0.0 collective-permute-done.5
  87.5 2.2 %broadcast_select_fusion.1 = bf16[320,1280]{1,0:T(8,128)(2,1)} fusion(bf16[320,1280]{1,0:T(8,128)(2,1)} %collective-permute-done.4, bf16[320,1280]{1,0:T(8,128)(2,1)} %collective-permute-done.5, pred[]{:T(512)S(6)} %eq.8), kind=kLoop, calls=%fused_computation.1 | loop fusion | flops 409600 | bytes 2457601 | tf_op jit(solution)/shard_map/jit(_where)/select_n | solution.py:446
  89.7 0.0 all-gather.5.cloned.1.call-update
  89.7 2.4 %collective-permute-done.3.mixed_other = bf16[8,624,256]{2,1,0:T(8,128)(2,1)} collective-permute-done((bf16[8,624,256]{2,1,0:T(8,128)(2,1)S(1)}, bf16[8,624,256]{2,1,0:T(8,128)(2,1)}, u32[]{:S(2)}, u32[]{:S(2)}) %collective-permute-start.3) | collective-permute-done | bytes 2555936 | tf_op jit(solution)/shard_map/ppermute | solution.py:374
  92.1 0.0 copy-done.1
  92.1 19.7 %attend.1 = bf16[2,8,240,256]{3,2,1,0:T(8,128)(2,1)} custom-call(bf16[8,624,256]{2,1,0:T(8,128)(2,1)} %copy-done.1, bf16[8,624,256]{2,1,0:T(8,128)(2,1)} %collective-permute-done.3.mixed_other, bf16[8,2,192,256]{3,2,1,0:T(8,128)(2,1)} %copy-done.2, bf16[8,2,192,256]{3,2,1,0:T(8,128)(2,1)} %collective-permute-done.2.v_other), custom_call_target="tpu_custom_call" | custom-call | flops 12079595520 | bytes 14680064 | tf_op jit(solution)/shard_map/attend/pallas_call | solution.py:268
  111.8 12.7 %all-to-all-start.2 = ((bf16[16,240,256]{2,1,0:T(8,128)(2,1)}), bf16[16,240,256]{2,1,0:T(8,128)(2,1)S(1)}, u32[]{:S(2)}, u32[]{:S(2)}) async-start(bf16[16,240,256]{2,1,0:T(8,128)(2,1)} %bitcast.23), calls=%async_computation.2 | async-start | bytes 3932160 | tf_op jit(solution)/shard_map/all_to_all | solution.py:450
  124.5 0.0 all-gather.7.cloned.1.call-done
  124.5 0.7 collective-permute-start.7
  125.3 29.1 %all-to-all-done.2 = bf16[16,240,256]{2,1,0:T(8,128)(2,1)S(1)} async-done(((bf16[16,240,256]{2,1,0:T(8,128)(2,1)}), bf16[16,240,256]{2,1,0:T(8,128)(2,1)S(1)}, u32[]{:S(2)}, u32[]{:S(2)}) %all-to-all-start.2) | async-done | bytes 1966112 | tf_op jit(solution)/shard_map/all_to_all | solution.py:450
  154.4 0.0 copy-start
  154.4 0.0 all-gather.5.cloned.1.call-done
  154.4 1.5 collective-permute-start.6
  155.9 0.6 pad_add_fusion.meta
  156.5 0.0 collective-permute-done.7.refs_2_.refs_3_
  156.5 0.0 copy-done
  156.5 7.6 %project.2.refs_4_ = f32[384,2560]{1,0:T(8,128)} custom-call(s32[3]{0:T(128)} %pad_add_fusion.meta, bf16[2,8,240,256]{3,2,1,0:T(8,128)(2,1)} %bitcast.15, bf16[4,320,1280]{2,1,0:T(8,128)(2,1)} %bitcast.18, bf16[4,320,1280]{2,1,0:T(8,128)(2,1)} %bitcast.19, bf16[4,320,1280]{2,1,0:T(8,128)(2,1)} %collective-permute-done.7.refs_2_.refs_3_, ...), custom_call_target="tpu_custom_call" | custom-call | flops 2516582400 | bytes 12582912 | tf_op jit(solution)/shard_map/project/pallas_call | solution.py:344
  164.1 0.0 collective-permute-done.6.refs_2_.refs_3_
  164.1 8.0 %project.3 = (bf16[192,2560]{1,0:T(8,128)(2,1)}, bf16[192,2560]{1,0:T(8,128)(2,1)}) custom-call(s32[3]{0:T(128)} %pad_add_fusion.meta, bf16[2,8,240,256]{3,2,1,0:T(8,128)(2,1)} %bitcast.16, bf16[4,320,1280]{2,1,0:T(8,128)(2,1)} %bitcast.21, bf16[4,320,1280]{2,1,0:T(8,128)(2,1)} %bitcast.22, bf16[4,320,1280]{2,1,0:T(8,128)(2,1)} %collective-permute-done.6.refs_2_.refs_3_, ...), custom_call_target="tpu_custom_call" | custom-call | flops 2516582400 | bytes 12582912 | tf_op jit(solution)/shard_map/project/pallas_call | solution.py:344
  (4 shorter events, 0.0 us)
Async XLA Ops:
  8.4 14.7 %copy-start.6 = (s32[32]{0:T(128)S(1)}, s32[32]{0:T(128)}, u32[]{:S(2)}) copy-start(s32[32]{0:T(128)} %param.19) | copy-start | bytes 388
  8.4 22.1 %collective-permute-start = (bf16[320,1280]{1,0:T(8,128)(2,1)S(1)}, bf16[320,1280]{1,0:T(8,128)(2,1)S(1)}, u32[]{:S(2)}, u32[]{:S(2)}) collective-permute-start(bf16[320,1280]{1,0:T(8,128)(2,1)S(1)} %constant_dynamic-slice_fusion.1), channel_id=1, source_target_pairs={{0,96},{1,97},{2,98},{3,99},{4,100},{5,101},{6,102},{7,103},{8,104... | collective-permute-start | bytes 2457608 | tf_op jit(solution)/shard_map/ppermute | solution.py:388
  17.3 6.0 %collective-permute-start.1 = (f32[192,128]{1,0:T(8,128)}, f32[192,128]{1,0:T(8,128)S(1)}, u32[]{:S(2)}, u32[]{:S(2)}) collective-permute-start(f32[192,128]{1,0:T(8,128)} %get-tuple-element.21.mine), channel_id=1, source_target_pairs={{0,16},{16,0},{1,17},{17,1},{2,18},{18,2},{3,19},{19,3},{4,20},{20... | collective-permute-start | bytes 294920 | tf_op jit(solution)/shard_map/ppermute | solution.py:392
  17.7 15.7 %copy-start.4 = (f32[1280]{0:T(1024)S(1)}, f32[1280]{0:T(1024)}, u32[]{:S(2)}) copy-start(f32[1280]{0:T(1024)} %param.16) | copy-start | bytes 15364
  17.7 16.3 %copy-start.5 = (f32[1280]{0:T(1024)S(1)}, f32[1280]{0:T(1024)}, u32[]{:S(2)}) copy-start(f32[1280]{0:T(1024)} %param.17) | copy-start | bytes 15364
  17.7 26.7 %all-to-all-start = ((bf16[8,2,192,256]{3,2,1,0:T(8,128)(2,1)}), bf16[8,2,192,256]{3,2,1,0:T(8,128)(2,1)S(1)}, u32[]{:S(2)}, u32[]{:S(2)}) async-start(bf16[8,2,192,256]{3,2,1,0:T(8,128)(2,1)} %get-tuple-element.22), calls=%async_computation | async-start | bytes 3145728 | tf_op jit(solution)/shard_map/all_to_all | solution.py:370
  23.0 101.5 %all-gather.7.cloned.1.call-start = ((), (), s32[]{:S(2)}) async-start(), calls=%async_computation.4 | async-start | bytes 4096000 | tf_op jit(solution)/shard_map/all_gather | solution.py:439
  23.2 22.0 %copy-start.3 = (f32[192,128]{1,0:T(8,128)}, f32[192,128]{1,0:T(8,128)S(1)}, u32[]{:S(2)}) copy-start(f32[192,128]{1,0:T(8,128)S(1)} %collective-permute-done.1.theirs) | copy-start | bytes 294916
  44.4 6.7 %copy-start.2 = (bf16[8,2,192,256]{3,2,1,0:T(8,128)(2,1)}, bf16[8,2,192,256]{3,2,1,0:T(8,128)(2,1)S(1)}, u32[]{:S(2)}) copy-start(bf16[8,2,192,256]{3,2,1,0:T(8,128)(2,1)S(1)} %all-to-all-done.v_in) | copy-start | bytes 4718596
  44.4 6.7 %collective-permute-start.2 = (bf16[8,2,192,256]{3,2,1,0:T(8,128)(2,1)S(1)}, bf16[8,2,192,256]{3,2,1,0:T(8,128)(2,1)}, u32[]{:S(2)}, u32[]{:S(2)}) collective-permute-start(bf16[8,2,192,256]{3,2,1,0:T(8,128)(2,1)S(1)} %all-to-all-done.v_in), channel_id=1, source_target_pairs={{0,1},{1,0},{2,3},{3,2},{4,5},{5,4},{6,7},{7,6},{8,9},{9,8},{10,11... | collective-permute-start | bytes 4718600 | tf_op jit(solution)/shard_map/ppermute | solution.py:374
  51.1 35.6 %all-to-all-start.1 = ((bf16[8,624,256]{2,1,0:T(8,128)(2,1)}), bf16[8,624,256]{2,1,0:T(8,128)(2,1)S(1)}, u32[]{:S(2)}, u32[]{:S(2)}) async-start(bf16[8,624,256]{2,1,0:T(8,128)(2,1)} %norm_rope.1), calls=%async_computation.1 | async-start | bytes 5111808 | tf_op jit(solution)/shard_map/all_to_all | solution.py:370
  54.8 99.6 %all-gather.5.cloned.1.call-start = ((), (), s32[]{:S(2)}) async-start(), calls=%async_computation.3 | async-start | bytes 4096000 | tf_op jit(solution)/shard_map/all_gather | solution.py:446
  54.8 32.7 %collective-permute-start.4 = (bf16[320,1280]{1,0:T(8,128)(2,1)}, bf16[320,1280]{1,0:T(8,128)(2,1)}, u32[]{:S(2)}, u32[]{:S(2)}) collective-permute-start(bf16[320,1280]{1,0:T(8,128)(2,1)} %get-tuple-element.31), channel_id=1, source_target_pairs={{16,8},{17,9},{18,10},{19,11},{20,12},{21,13},{22,14},{23,15},{24,... | collective-permute-start | bytes 2457608 | tf_op jit(solution)/shard_map/ppermute | solution.py:388
  56.1 31.4 %collective-permute-start.5 = (bf16[320,1280]{1,0:T(8,128)(2,1)S(1)}, bf16[320,1280]{1,0:T(8,128)(2,1)}, u32[]{:S(2)}, u32[]{:S(2)}) collective-permute-start(bf16[320,1280]{1,0:T(8,128)(2,1)S(1)} %constant_dynamic-slice_fusion.1), channel_id=1, source_target_pairs={{16,104},{17,105},{18,106},{19,107},{20,108},{21,109},{22,110},{23... | collective-permute-start | bytes 2457608 | tf_op jit(solution)/shard_map/ppermute | solution.py:388
  86.7 5.4 %copy-start.1 = (bf16[8,624,256]{2,1,0:T(8,128)(2,1)}, bf16[8,624,256]{2,1,0:T(8,128)(2,1)S(1)}, u32[]{:S(2)}) copy-start(bf16[8,624,256]{2,1,0:T(8,128)(2,1)S(1)} %all-to-all-done.1.mixed) | copy-start | bytes 7667716
  86.7 5.4 %collective-permute-start.3 = (bf16[8,624,256]{2,1,0:T(8,128)(2,1)S(1)}, bf16[8,624,256]{2,1,0:T(8,128)(2,1)}, u32[]{:S(2)}, u32[]{:S(2)}) collective-permute-start(bf16[8,624,256]{2,1,0:T(8,128)(2,1)S(1)} %all-to-all-done.1.mixed), channel_id=1, source_target_pairs={{0,1},{1,0},{2,3},{3,2},{4,5},{5,4},{6,7},{7,6},{8,9},{9,8},{10,11... | collective-permute-start | bytes 7667720 | tf_op jit(solution)/shard_map/ppermute | solution.py:374
  111.8 42.5 %all-to-all-start.2 = ((bf16[16,240,256]{2,1,0:T(8,128)(2,1)}), bf16[16,240,256]{2,1,0:T(8,128)(2,1)S(1)}, u32[]{:S(2)}, u32[]{:S(2)}) async-start(bf16[16,240,256]{2,1,0:T(8,128)(2,1)} %bitcast.23), calls=%async_computation.2 | async-start | bytes 3932160 | tf_op jit(solution)/shard_map/all_to_all | solution.py:450
  124.5 32.0 %collective-permute-start.7 = (bf16[4,320,1280]{2,1,0:T(8,128)(2,1)}, bf16[4,320,1280]{2,1,0:T(8,128)(2,1)}, u32[]{:S(2)}, u32[]{:S(2)}) collective-permute-start(bf16[4,320,1280]{2,1,0:T(8,128)(2,1)} %bitcast.17), channel_id=1, source_target_pairs={{0,1},{1,0},{2,3},{3,2},{4,5},{5,4},{6,7},{7,6},{8,9},{9,8},{10,11... | collective-permute-start | bytes 9830408 | tf_op jit(solution)/shard_map/ppermute | solution.py:374
  154.4 2.1 %copy-start = (bf16[16,240,256]{2,1,0:T(8,128)(2,1)}, bf16[16,240,256]{2,1,0:T(8,128)(2,1)S(1)}, u32[]{:S(2)}) copy-start(bf16[16,240,256]{2,1,0:T(8,128)(2,1)S(1)} %all-to-all-done.2) | copy-start | bytes 5898244
  154.4 9.8 %collective-permute-start.6 = (bf16[4,320,1280]{2,1,0:T(8,128)(2,1)}, bf16[4,320,1280]{2,1,0:T(8,128)(2,1)}, u32[]{:S(2)}, u32[]{:S(2)}) collective-permute-start(bf16[4,320,1280]{2,1,0:T(8,128)(2,1)} %bitcast.20), channel_id=1, source_target_pairs={{0,1},{1,0},{2,3},{3,2},{4,5},{5,4},{6,7},{7,6},{8,9},{9,8},{10,11... | collective-permute-start | bytes 9830408 | tf_op jit(solution)/shard_map/ppermute | solution.py:374
Sparse Core Ops, SparseCore 0:
  33.2 50.9 all-gather.6
  89.8 45.5 all-gather.4

commit v4 on v3

--- a/solution.py
+++ b/solution.py
@@ -425,8 +425,8 @@
         lax.dynamic_slice_in_dim(out_weight, (2 * core + part) * quarter, quarter, 0)
         for part in range(2)
     ]
-    second = move(upper, [((clip, own), (3 - clip, own)) for clip, own in HOME])
     value_out, stats = prepare(*raw)
+    second = move(after(upper, stats), [((clip, own), (3 - clip, own)) for clip, own in HOME])
     values = to_chips(value_out)
     stats_peer = to_group(stats)
     second, stats_peer = lax.optimization_barrier((second, stats_peer))

time: 180 us -> 179 us (level)
  waiting for transfers between devices: 76.4 us -> 73.9 us
    ppermute x3, waiting for transfers between devices: 7.27 us -> 10.9 us  [move(): return lax.ppermute(array, ('dp', 'head', 'ctx'), links)]
    all_to_all x2, waiting for transfers between devices: 37.6 us -> 33.9 us  [to_chips(): lax.all_to_all(array, 'ctx', 0, 0, axis_index_groups=CORES, tiled=True)]
    all_to_all x1, waiting for transfers between devices: 29.1 us -> 26.7 us  [on_device(): lax.all_to_all(results.reshape(2 * CHIPS, SLOT, 256), ('head', 'ctx'), 0,...]
  transfers between devices with their start and end apart: 13 -> 13, of which waited for: 5 -> 5; matrix products, arithmetic and copies ran while one was open for 5% -> 5% of each run, Pallas kernels for 21% -> 19%
where the time goes in v4:
time: 179 us; the launch traced here: 178 us
  waiting for transfers between devices  73.9 us (41%)
  Pallas kernels  44.7 us (25%)
  starting transfers between devices  35.9 us (20%)
  between operations  14.2 us (8%)
  other arithmetic  6.78 us (4%)
  local copies, waits for them, and re-layouts  2.73 us (2%)
    all_to_all x2, waiting for transfers between devices, to_chips(): lax.all_to_all(array, 'ctx', 0, 0, axis_index_groups=CORES, tiled=True)  33.9 us
    all_to_all x1, waiting for transfers between devices, on_device(): lax.all_to_all(results.reshape(2 * CHIPS, SLOT, 256), ('head', 'ctx'), 0,...  26.7 us
    pallas_call x1, Pallas kernels, attend(): pl.pallas_call(attend_kernel, grid=(1,), out_shape=outs, in_specs=[anywhe...  19.7 us
    pallas_call x2, Pallas kernels, project(): pl.pallas_call(functools.partial(project_kernel, last), out_shape=outs, g...  15.6 us
    all_to_all x1, starting transfers between devices, on_device(): lax.all_to_all(results.reshape(2 * CHIPS, SLOT, 256), ('head', 'ctx'), 0,...  13.1 us
    ppermute x3, waiting for transfers between devices, move(): return lax.ppermute(array, ('dp', 'head', 'ctx'), links)  10.9 us
    pallas_call x2, Pallas kernels, call(): pl.pallas_call(kernel, grid=(1,), out_shape=outs, in_specs=[SMEM] * scala...  9.31 us
    all_to_all x2, starting transfers between devices, to_chips(): lax.all_to_all(array, 'ctx', 0, 0, axis_index_groups=CORES, tiled=True)  8.77 us
  transfers between devices with their start and end apart: 13, of which 5 were waited for; matrix products, arithmetic and copies ran while one was open for 5% of the time, Pallas kernels for 19%

profile of v4, /device:TPU:1, one launch (start us, length us, event | category | flops | bytes accessed | tf_op | source)
XLA Modules:
  0.0 178.2 jit_solution(6144508216940068805)
XLA Ops:
  7.2 1.2 constant_dynamic-slice_fusion.1
  8.4 0.0 copy-start.6
  8.4 3.6 %prepare.1 = (bf16[8,2,192,256]{3,2,1,0:T(8,128)(2,1)}, f32[192,128]{1,0:T(8,128)}) custom-call(bf16[192,1280]{1,0:T(8,128)(2,1)} %bitcast.24, bf16[192,1280]{1,0:T(8,128)(2,1)} %bitcast.26, bf16[192,1280]{1,0:T(8,128)(2,1)} %bitcast.28, bf16[192,1280]{1,0:T(8,128)(2,1)} %bitcast.30, bf16[192,1280]{1,0:T(8,128)(2,1)} %bitcast.32, bf16[192,1280]{1,0:T(8,128)(2,1)} %bitcast.33), custom_call_target="tpu_custom_call" | custom-call | flops 1966080 | bytes 6291456 | tf_op jit(solution)/shard_map/prepare/pallas_call | solution.py:49
  12.0 5.3 %collective-permute-start = (bf16[320,1280]{1,0:T(8,128)(2,1)S(1)}, bf16[320,1280]{1,0:T(8,128)(2,1)S(1)}, u32[]{:S(2)}, u32[]{:S(2)}) collective-permute-start(bf16[320,1280]{1,0:T(8,128)(2,1)S(1)} %constant_dynamic-slice_fusion.1), channel_id=1, source_target_pairs={{0,96},{1,97},{2,98},{3,99},{4,100},{5,101},{6,102},{7,103},{8,104... | collective-permute-start | bytes 2457608 | tf_op jit(solution)/shard_map/ppermute | solution.py:388
  17.3 0.5 collective-permute-start.1
  17.8 0.0 copy-start.4
  17.8 0.0 copy-start.5
  17.8 5.1 %all-to-all-start = ((bf16[8,2,192,256]{3,2,1,0:T(8,128)(2,1)}), bf16[8,2,192,256]{3,2,1,0:T(8,128)(2,1)S(1)}, u32[]{:S(2)}, u32[]{:S(2)}) async-start(bf16[8,2,192,256]{3,2,1,0:T(8,128)(2,1)} %get-tuple-element.23), calls=%async_computation | async-start | bytes 3145728 | tf_op jit(solution)/shard_map/all_to_all | solution.py:370
  22.9 0.0 all-gather.7.cloned.1.call-start
  23.0 0.0 copy-done.6
  23.0 0.1 dynamic-slice_multiply_fusion
  23.1 0.1 iota_add_fusion
  23.2 0.0 collective-permute-done.1.theirs
  23.2 0.0 copy-start.3
  23.2 10.9 %collective-permute-done = bf16[320,1280]{1,0:T(8,128)(2,1)S(1)} collective-permute-done((bf16[320,1280]{1,0:T(8,128)(2,1)S(1)}, bf16[320,1280]{1,0:T(8,128)(2,1)S(1)}, u32[]{:S(2)}, u32[]{:S(2)}) %collective-permute-start) | collective-permute-done | bytes 819232 | tf_op jit(solution)/shard_map/ppermute | solution.py:388
  34.1 2.5 %broadcast_select_fusion = (bf16[320,1280]{1,0:T(8,128)(2,1)}, bf16[320,1280]{1,0:T(8,128)(2,1)}) fusion(bf16[320,1280]{1,0:T(8,128)(2,1)S(1)} %collective-permute-done, pred[]{:T(512)S(6)} %eq.8, bf16[1280,1280]{1,0:T(8,128)(2,1)} %param.18, s32[]{:T(128)S(6)} %select_n.104), kind=kLoop, calls=%fused_computation | loop fusion | flops 409600 | bytes 3276805 | tf_op jit(solution)/shard_map/jit(_where)/select_n | solution.py:438
  36.6 0.0 all-gather.7.cloned.1.call-update
  36.6 0.1 pad_maximum_fusion
  36.7 0.1 add.88
  36.8 0.1 broadcast_in_dim.69
  36.9 0.1 mul.31
  37.0 0.0 copy-done.4
  37.0 0.6 broadcast_in_dim.70.q_gain
  37.6 0.0 copy-done.5
  37.6 0.6 broadcast_in_dim.71.k_gain
  38.3 1.2 fusion
  39.4 4.9 %all-to-all-done.v_in = bf16[8,2,192,256]{3,2,1,0:T(8,128)(2,1)S(1)} async-done(((bf16[8,2,192,256]{3,2,1,0:T(8,128)(2,1)}), bf16[8,2,192,256]{3,2,1,0:T(8,128)(2,1)S(1)}, u32[]{:S(2)}, u32[]{:S(2)}) %all-to-all-start) | async-done | bytes 1572896 | tf_op jit(solution)/shard_map/all_to_all | solution.py:370
  44.4 0.0 copy-start.2
  44.4 0.9 collective-permute-start.2
  45.2 0.0 copy-done.3
  45.2 5.7 %norm_rope.1 = bf16[8,624,256]{2,1,0:T(8,128)(2,1)} custom-call(bf16[192,1280]{1,0:T(8,128)(2,1)} %bitcast.25, bf16[192,1280]{1,0:T(8,128)(2,1)} %bitcast.27, bf16[192,1280]{1,0:T(8,128)(2,1)} %bitcast.29, bf16[192,1280]{1,0:T(8,128)(2,1)} %bitcast.31, f32[192,128]{1,0:T(8,128)} %get-tuple-element.22.mine, f32[192,128]{1,0:T(8,128)} %copy-done.3, ...), custom_call_target="tpu_custom_call" | custom-call | flops 9830400 | bytes 5242880 | tf_op jit(solution)/shard_map/norm_rope/pallas_call | solution.py:49
  50.9 0.0 collective-permute-done.2.v_other
  50.9 0.0 copy-done.2
  50.9 3.6 %all-to-all-start.1 = ((bf16[8,624,256]{2,1,0:T(8,128)(2,1)}), bf16[8,624,256]{2,1,0:T(8,128)(2,1)S(1)}, u32[]{:S(2)}, u32[]{:S(2)}) async-start(bf16[8,624,256]{2,1,0:T(8,128)(2,1)} %norm_rope.1), calls=%async_computation.1 | async-start | bytes 5111808 | tf_op jit(solution)/shard_map/all_to_all | solution.py:370
  54.6 0.0 all-gather.5.cloned.1.call-start
  54.6 1.3 collective-permute-start.4
  55.9 1.6 collective-permute-start.5
  57.5 29.0 %all-to-all-done.1.mixed = bf16[8,624,256]{2,1,0:T(8,128)(2,1)S(1)} async-done(((bf16[8,624,256]{2,1,0:T(8,128)(2,1)}), bf16[8,624,256]{2,1,0:T(8,128)(2,1)S(1)}, u32[]{:S(2)}, u32[]{:S(2)}) %all-to-all-start.1) | async-done | bytes 2555936 | tf_op jit(solution)/shard_map/all_to_all | solution.py:370
  86.5 0.0 copy-start.1
  86.5 0.8 collective-permute-start.3
  87.3 0.0 collective-permute-done.4
  87.3 0.0 collective-permute-done.5
  87.3 2.2 %broadcast_select_fusion.1 = bf16[320,1280]{1,0:T(8,128)(2,1)} fusion(bf16[320,1280]{1,0:T(8,128)(2,1)} %collective-permute-done.4, bf16[320,1280]{1,0:T(8,128)(2,1)} %collective-permute-done.5, pred[]{:T(512)S(6)} %eq.8), kind=kLoop, calls=%fused_computation.1 | loop fusion | flops 409600 | bytes 2457601 | tf_op jit(solution)/shard_map/jit(_where)/select_n | solution.py:446
  89.5 0.0 all-gather.5.cloned.1.call-update
  89.5 2.4 %collective-permute-done.3.mixed_other = bf16[8,624,256]{2,1,0:T(8,128)(2,1)} collective-permute-done((bf16[8,624,256]{2,1,0:T(8,128)(2,1)S(1)}, bf16[8,624,256]{2,1,0:T(8,128)(2,1)}, u32[]{:S(2)}, u32[]{:S(2)}) %collective-permute-start.3) | collective-permute-done | bytes 2555936 | tf_op jit(solution)/shard_map/ppermute | solution.py:374
  91.9 0.0 copy-done.1
  91.9 19.7 %attend.1 = bf16[2,8,240,256]{3,2,1,0:T(8,128)(2,1)} custom-call(bf16[8,624,256]{2,1,0:T(8,128)(2,1)} %copy-done.1, bf16[8,624,256]{2,1,0:T(8,128)(2,1)} %collective-permute-done.3.mixed_other, bf16[8,2,192,256]{3,2,1,0:T(8,128)(2,1)} %copy-done.2, bf16[8,2,192,256]{3,2,1,0:T(8,128)(2,1)} %collective-permute-done.2.v_other), custom_call_target="tpu_custom_call" | custom-call | flops 12079595520 | bytes 14680064 | tf_op jit(solution)/shard_map/attend/pallas_call | solution.py:268
  111.6 13.1 %all-to-all-start.2 = ((bf16[16,240,256]{2,1,0:T(8,128)(2,1)}), bf16[16,240,256]{2,1,0:T(8,128)(2,1)S(1)}, u32[]{:S(2)}, u32[]{:S(2)}) async-start(bf16[16,240,256]{2,1,0:T(8,128)(2,1)} %bitcast.23), calls=%async_computation.2 | async-start | bytes 3932160 | tf_op jit(solution)/shard_map/all_to_all | solution.py:450
  124.8 0.0 all-gather.7.cloned.1.call-done
  124.8 1.3 collective-permute-start.7
  126.1 26.7 %all-to-all-done.2 = bf16[16,240,256]{2,1,0:T(8,128)(2,1)S(1)} async-done(((bf16[16,240,256]{2,1,0:T(8,128)(2,1)}), bf16[16,240,256]{2,1,0:T(8,128)(2,1)S(1)}, u32[]{:S(2)}, u32[]{:S(2)}) %all-to-all-start.2) | async-done | bytes 1966112 | tf_op jit(solution)/shard_map/all_to_all | solution.py:450
  152.7 0.0 copy-start
  152.7 0.0 all-gather.5.cloned.1.call-done
  152.7 2.4 %collective-permute-start.6 = (bf16[4,320,1280]{2,1,0:T(8,128)(2,1)}, bf16[4,320,1280]{2,1,0:T(8,128)(2,1)}, u32[]{:S(2)}, u32[]{:S(2)}) collective-permute-start(bf16[4,320,1280]{2,1,0:T(8,128)(2,1)} %bitcast.20), channel_id=1, source_target_pairs={{0,1},{1,0},{2,3},{3,2},{4,5},{5,4},{6,7},{7,6},{8,9},{9,8},{10,11... | collective-permute-start | bytes 9830408 | tf_op jit(solution)/shard_map/ppermute | solution.py:374
  155.1 0.6 pad_add_fusion.meta
  155.7 0.0 collective-permute-done.7.refs_2_.refs_3_
  155.7 0.0 copy-done
  155.7 7.6 %project.2.refs_4_ = f32[384,2560]{1,0:T(8,128)} custom-call(s32[3]{0:T(128)} %pad_add_fusion.meta, bf16[2,8,240,256]{3,2,1,0:T(8,128)(2,1)} %bitcast.15, bf16[4,320,1280]{2,1,0:T(8,128)(2,1)} %bitcast.18, bf16[4,320,1280]{2,1,0:T(8,128)(2,1)} %bitcast.19, bf16[4,320,1280]{2,1,0:T(8,128)(2,1)} %collective-permute-done.7.refs_2_.refs_3_, ...), custom_call_target="tpu_custom_call" | custom-call | flops 2516582400 | bytes 12582912 | tf_op jit(solution)/shard_map/project/pallas_call | solution.py:344
  163.4 0.0 collective-permute-done.6.refs_2_.refs_3_
  163.4 8.0 %project.3 = (bf16[192,2560]{1,0:T(8,128)(2,1)}, bf16[192,2560]{1,0:T(8,128)(2,1)}) custom-call(s32[3]{0:T(128)} %pad_add_fusion.meta, bf16[2,8,240,256]{3,2,1,0:T(8,128)(2,1)} %bitcast.16, bf16[4,320,1280]{2,1,0:T(8,128)(2,1)} %bitcast.21, bf16[4,320,1280]{2,1,0:T(8,128)(2,1)} %bitcast.22, bf16[4,320,1280]{2,1,0:T(8,128)(2,1)} %collective-permute-done.6.refs_2_.refs_3_, ...), custom_call_target="tpu_custom_call" | custom-call | flops 2516582400 | bytes 12582912 | tf_op jit(solution)/shard_map/project/pallas_call | solution.py:344
  (4 shorter events, 0.0 us)
Async XLA Ops:
  8.4 14.6 %copy-start.6 = (s32[32]{0:T(128)S(1)}, s32[32]{0:T(128)}, u32[]{:S(2)}) copy-start(s32[32]{0:T(128)} %param.19) | copy-start | bytes 388
  12.0 22.1 %collective-permute-start = (bf16[320,1280]{1,0:T(8,128)(2,1)S(1)}, bf16[320,1280]{1,0:T(8,128)(2,1)S(1)}, u32[]{:S(2)}, u32[]{:S(2)}) collective-permute-start(bf16[320,1280]{1,0:T(8,128)(2,1)S(1)} %constant_dynamic-slice_fusion.1), channel_id=1, source_target_pairs={{0,96},{1,97},{2,98},{3,99},{4,100},{5,101},{6,102},{7,103},{8,104... | collective-permute-start | bytes 2457608 | tf_op jit(solution)/shard_map/ppermute | solution.py:388
  17.3 5.9 %collective-permute-start.1 = (f32[192,128]{1,0:T(8,128)}, f32[192,128]{1,0:T(8,128)S(1)}, u32[]{:S(2)}, u32[]{:S(2)}) collective-permute-start(f32[192,128]{1,0:T(8,128)} %get-tuple-element.22.mine), channel_id=1, source_target_pairs={{0,16},{16,0},{1,17},{17,1},{2,18},{18,2},{3,19},{19,3},{4,20},{20... | collective-permute-start | bytes 294920 | tf_op jit(solution)/shard_map/ppermute | solution.py:392
  17.8 19.2 %copy-start.4 = (f32[1280]{0:T(1024)S(1)}, f32[1280]{0:T(1024)}, u32[]{:S(2)}) copy-start(f32[1280]{0:T(1024)} %param.16) | copy-start | bytes 15364
  17.8 19.8 %copy-start.5 = (f32[1280]{0:T(1024)S(1)}, f32[1280]{0:T(1024)}, u32[]{:S(2)}) copy-start(f32[1280]{0:T(1024)} %param.17) | copy-start | bytes 15364
  17.8 26.6 %all-to-all-start = ((bf16[8,2,192,256]{3,2,1,0:T(8,128)(2,1)}), bf16[8,2,192,256]{3,2,1,0:T(8,128)(2,1)S(1)}, u32[]{:S(2)}, u32[]{:S(2)}) async-start(bf16[8,2,192,256]{3,2,1,0:T(8,128)(2,1)} %get-tuple-element.23), calls=%async_computation | async-start | bytes 3145728 | tf_op jit(solution)/shard_map/all_to_all | solution.py:370
  22.9 101.8 %all-gather.7.cloned.1.call-start = ((), (), s32[]{:S(2)}) async-start(), calls=%async_computation.4 | async-start | bytes 4096000 | tf_op jit(solution)/shard_map/all_gather | solution.py:439
  23.2 22.0 %copy-start.3 = (f32[192,128]{1,0:T(8,128)}, f32[192,128]{1,0:T(8,128)S(1)}, u32[]{:S(2)}) copy-start(f32[192,128]{1,0:T(8,128)S(1)} %collective-permute-done.1.theirs) | copy-start | bytes 294916
  44.4 6.6 %copy-start.2 = (bf16[8,2,192,256]{3,2,1,0:T(8,128)(2,1)}, bf16[8,2,192,256]{3,2,1,0:T(8,128)(2,1)S(1)}, u32[]{:S(2)}) copy-start(bf16[8,2,192,256]{3,2,1,0:T(8,128)(2,1)S(1)} %all-to-all-done.v_in) | copy-start | bytes 4718596
  44.4 6.6 %collective-permute-start.2 = (bf16[8,2,192,256]{3,2,1,0:T(8,128)(2,1)S(1)}, bf16[8,2,192,256]{3,2,1,0:T(8,128)(2,1)}, u32[]{:S(2)}, u32[]{:S(2)}) collective-permute-start(bf16[8,2,192,256]{3,2,1,0:T(8,128)(2,1)S(1)} %all-to-all-done.v_in), channel_id=1, source_target_pairs={{0,1},{1,0},{2,3},{3,2},{4,5},{5,4},{6,7},{7,6},{8,9},{9,8},{10,11... | collective-permute-start | bytes 4718600 | tf_op jit(solution)/shard_map/ppermute | solution.py:374
  50.9 35.6 %all-to-all-start.1 = ((bf16[8,624,256]{2,1,0:T(8,128)(2,1)}), bf16[8,624,256]{2,1,0:T(8,128)(2,1)S(1)}, u32[]{:S(2)}, u32[]{:S(2)}) async-start(bf16[8,624,256]{2,1,0:T(8,128)(2,1)} %norm_rope.1), calls=%async_computation.1 | async-start | bytes 5111808 | tf_op jit(solution)/shard_map/all_to_all | solution.py:370
  54.6 98.2 %all-gather.5.cloned.1.call-start = ((), (), s32[]{:S(2)}) async-start(), calls=%async_computation.3 | async-start | bytes 4096000 | tf_op jit(solution)/shard_map/all_gather | solution.py:446
  54.6 32.7 %collective-permute-start.4 = (bf16[320,1280]{1,0:T(8,128)(2,1)}, bf16[320,1280]{1,0:T(8,128)(2,1)}, u32[]{:S(2)}, u32[]{:S(2)}) collective-permute-start(bf16[320,1280]{1,0:T(8,128)(2,1)} %get-tuple-element.33), channel_id=1, source_target_pairs={{16,8},{17,9},{18,10},{19,11},{20,12},{21,13},{22,14},{23,15},{24,... | collective-permute-start | bytes 2457608 | tf_op jit(solution)/shard_map/ppermute | solution.py:388
  55.9 31.4 %collective-permute-start.5 = (bf16[320,1280]{1,0:T(8,128)(2,1)S(1)}, bf16[320,1280]{1,0:T(8,128)(2,1)}, u32[]{:S(2)}, u32[]{:S(2)}) collective-permute-start(bf16[320,1280]{1,0:T(8,128)(2,1)S(1)} %constant_dynamic-slice_fusion.1), channel_id=1, source_target_pairs={{16,104},{17,105},{18,106},{19,107},{20,108},{21,109},{22,110},{23... | collective-permute-start | bytes 2457608 | tf_op jit(solution)/shard_map/ppermute | solution.py:388
  86.5 5.4 %copy-start.1 = (bf16[8,624,256]{2,1,0:T(8,128)(2,1)}, bf16[8,624,256]{2,1,0:T(8,128)(2,1)S(1)}, u32[]{:S(2)}) copy-start(bf16[8,624,256]{2,1,0:T(8,128)(2,1)S(1)} %all-to-all-done.1.mixed) | copy-start | bytes 7667716
  86.5 5.4 %collective-permute-start.3 = (bf16[8,624,256]{2,1,0:T(8,128)(2,1)S(1)}, bf16[8,624,256]{2,1,0:T(8,128)(2,1)}, u32[]{:S(2)}, u32[]{:S(2)}) collective-permute-start(bf16[8,624,256]{2,1,0:T(8,128)(2,1)S(1)} %all-to-all-done.1.mixed), channel_id=1, source_target_pairs={{0,1},{1,0},{2,3},{3,2},{4,5},{5,4},{6,7},{7,6},{8,9},{9,8},{10,11... | collective-permute-start | bytes 7667720 | tf_op jit(solution)/shard_map/ppermute | solution.py:374
  111.6 41.1 %all-to-all-start.2 = ((bf16[16,240,256]{2,1,0:T(8,128)(2,1)}), bf16[16,240,256]{2,1,0:T(8,128)(2,1)S(1)}, u32[]{:S(2)}, u32[]{:S(2)}) async-start(bf16[16,240,256]{2,1,0:T(8,128)(2,1)} %bitcast.23), calls=%async_computation.2 | async-start | bytes 3932160 | tf_op jit(solution)/shard_map/all_to_all | solution.py:450
  124.8 30.9 %collective-permute-start.7 = (bf16[4,320,1280]{2,1,0:T(8,128)(2,1)}, bf16[4,320,1280]{2,1,0:T(8,128)(2,1)}, u32[]{:S(2)}, u32[]{:S(2)}) collective-permute-start(bf16[4,320,1280]{2,1,0:T(8,128)(2,1)} %bitcast.17), channel_id=1, source_target_pairs={{0,1},{1,0},{2,3},{3,2},{4,5},{5,4},{6,7},{7,6},{8,9},{9,8},{10,11... | collective-permute-start | bytes 9830408 | tf_op jit(solution)/shard_map/ppermute | solution.py:374
  152.7 3.0 %copy-start = (bf16[16,240,256]{2,1,0:T(8,128)(2,1)}, bf16[16,240,256]{2,1,0:T(8,128)(2,1)S(1)}, u32[]{:S(2)}) copy-start(bf16[16,240,256]{2,1,0:T(8,128)(2,1)S(1)} %all-to-all-done.2) | copy-start | bytes 5898244
  152.7 10.6 %collective-permute-start.6 = (bf16[4,320,1280]{2,1,0:T(8,128)(2,1)}, bf16[4,320,1280]{2,1,0:T(8,128)(2,1)}, u32[]{:S(2)}, u32[]{:S(2)}) collective-permute-start(bf16[4,320,1280]{2,1,0:T(8,128)(2,1)} %bitcast.20), channel_id=1, source_target_pairs={{0,1},{1,0},{2,3},{3,2},{4,5},{5,4},{6,7},{7,6},{8,9},{9,8},{10,11... | collective-permute-start | bytes 9830408 | tf_op jit(solution)/shard_map/ppermute | solution.py:374
Sparse Core Ops, SparseCore 0:
  36.8 54.6 all-gather.6
  93.7 44.7 all-gather.4

commit v5 on v4

--- a/solution.py
+++ b/solution.py
@@ -429,7 +429,7 @@
     second = move(after(upper, stats), [((clip, own), (3 - clip, own)) for clip, own in HOME])
     values = to_chips(value_out)
     stats_peer = to_group(stats)
-    second, stats_peer = lax.optimization_barrier((second, stats_peer))
+    second, stats_peer, meta = lax.optimization_barrier((second, stats_peer, meta))
     cosine, sine = rope_tables(lax.dynamic_slice_in_dim(span_order, 2 * place, 2))
     gains = (query_gain[None], key_gain[None])
     values, stats_peer, cosine, sine, gains = lax.optimization_barrier(
@@ -443,7 +443,7 @@
     mixed_out = norm_rope(*raw[:4], stats, stats_peer, *gains, cosine, sine)
     mixed = to_chips(after(mixed_out, values_other))
     near, far = after((near, far), mixed)
-    cross_weight = lax.all_gather(jnp.where(home, near, far), "dp", axis=0)
+    cross_weight = lax.all_gather(near + far, "dp", axis=0)
     mixed_other = to_core(mixed)
     own_other = to_core(after(own_weight, mixed_other))
     results = attend(mixed, mixed_other, values, values_other)

time: 179 us -> 179 us (level)
    add x0 -> x1, other arithmetic: none -> 2.54 us  [on_device(): cross_weight = lax.all_gather(near + far, 'dp', axis=0)]
    select_n x1 -> x0, other arithmetic: 2.19 us -> none  [on_device(): cross_weight = lax.all_gather(jnp.where(home, near, far), 'dp', axis=0)]
where the time goes in v5:
time: 179 us; the launch traced here: 178 us
  waiting for transfers between devices  73 us (41%)
  Pallas kernels  44.7 us (25%)
  starting transfers between devices  36.3 us (20%)
  between operations  14.2 us (8%)
  other arithmetic  7.14 us (4%)
  local copies, waits for them, and re-layouts  2.72 us (2%)
    all_to_all x2, waiting for transfers between devices, to_chips(): lax.all_to_all(array, 'ctx', 0, 0, axis_index_groups=CORES, tiled=True)  33.9 us
    all_to_all x1, waiting for transfers between devices, on_device(): lax.all_to_all(results.reshape(2 * CHIPS, SLOT, 256), ('head', 'ctx'), 0,...  26.7 us
    pallas_call x1, Pallas kernels, attend(): pl.pallas_call(attend_kernel, grid=(1,), out_shape=outs, in_specs=[anywhe...  19.7 us
    pallas_call x2, Pallas kernels, project(): pl.pallas_call(functools.partial(project_kernel, last), out_shape=outs, g...  15.6 us
    all_to_all x1, starting transfers between devices, on_device(): lax.all_to_all(results.reshape(2 * CHIPS, SLOT, 256), ('head', 'ctx'), 0,...  13.5 us
    ppermute x3, waiting for transfers between devices, move(): return lax.ppermute(array, ('dp', 'head', 'ctx'), links)  10.3 us
    pallas_call x2, Pallas kernels, call(): pl.pallas_call(kernel, grid=(1,), out_shape=outs, in_specs=[SMEM] * scala...  9.31 us
    all_to_all x2, starting transfers between devices, to_chips(): lax.all_to_all(array, 'ctx', 0, 0, axis_index_groups=CORES, tiled=True)  8.77 us
  transfers between devices with their start and end apart: 13, of which 5 were waited for; matrix products, arithmetic and copies ran while one was open for 5% of the time, Pallas kernels for 19%

profile of v5, /device:TPU:1, one launch (start us, length us, event | category | flops | bytes accessed | tf_op | source)
XLA Modules:
  0.0 178.0 jit_solution(4780366732379231024)
XLA Ops:
  7.2 1.2 constant_dynamic-slice_fusion.1
  8.4 0.0 copy-start.6
  8.4 3.6 %prepare.1 = (bf16[8,2,192,256]{3,2,1,0:T(8,128)(2,1)}, f32[192,128]{1,0:T(8,128)}) custom-call(bf16[192,1280]{1,0:T(8,128)(2,1)} %bitcast.24, bf16[192,1280]{1,0:T(8,128)(2,1)} %bitcast.26, bf16[192,1280]{1,0:T(8,128)(2,1)} %bitcast.28, bf16[192,1280]{1,0:T(8,128)(2,1)} %bitcast.30, bf16[192,1280]{1,0:T(8,128)(2,1)} %bitcast.32, bf16[192,1280]{1,0:T(8,128)(2,1)} %bitcast.33), custom_call_target="tpu_custom_call" | custom-call | flops 1966080 | bytes 6291456 | tf_op jit(solution)/shard_map/prepare/pallas_call | solution.py:49
  12.0 5.3 %collective-permute-start = (bf16[320,1280]{1,0:T(8,128)(2,1)S(1)}, bf16[320,1280]{1,0:T(8,128)(2,1)S(1)}, u32[]{:S(2)}, u32[]{:S(2)}) collective-permute-start(bf16[320,1280]{1,0:T(8,128)(2,1)S(1)} %constant_dynamic-slice_fusion.1), channel_id=1, source_target_pairs={{0,96},{1,97},{2,98},{3,99},{4,100},{5,101},{6,102},{7,103},{8,104... | collective-permute-start | bytes 2457608 | tf_op jit(solution)/shard_map/ppermute | solution.py:388
  17.3 0.5 collective-permute-start.1
  17.8 0.0 copy-start.4
  17.8 0.0 copy-start.5
  17.8 5.1 %all-to-all-start = ((bf16[8,2,192,256]{3,2,1,0:T(8,128)(2,1)}), bf16[8,2,192,256]{3,2,1,0:T(8,128)(2,1)S(1)}, u32[]{:S(2)}, u32[]{:S(2)}) async-start(bf16[8,2,192,256]{3,2,1,0:T(8,128)(2,1)} %get-tuple-element.26), calls=%async_computation | async-start | bytes 3145728 | tf_op jit(solution)/shard_map/all_to_all | solution.py:370
  22.9 0.0 all-gather.7.cloned.1.call-start
  23.0 0.0 copy-done.6
  23.0 0.1 dynamic-slice_multiply_fusion
  23.1 0.1 iota_add_fusion
  23.2 0.7 pad_add_fusion.meta
  23.8 0.0 collective-permute-done.1.theirs
  23.8 0.0 copy-start.3
  23.8 10.3 %collective-permute-done = bf16[320,1280]{1,0:T(8,128)(2,1)S(1)} collective-permute-done((bf16[320,1280]{1,0:T(8,128)(2,1)S(1)}, bf16[320,1280]{1,0:T(8,128)(2,1)S(1)}, u32[]{:S(2)}, u32[]{:S(2)}) %collective-permute-start) | collective-permute-done | bytes 819232 | tf_op jit(solution)/shard_map/ppermute | solution.py:388
  34.1 2.5 %broadcast_select_fusion = (bf16[320,1280]{1,0:T(8,128)(2,1)}, bf16[320,1280]{1,0:T(8,128)(2,1)}) fusion(bf16[320,1280]{1,0:T(8,128)(2,1)S(1)} %collective-permute-done, pred[]{:T(512)S(6)} %eq.8, bf16[1280,1280]{1,0:T(8,128)(2,1)} %param.18, s32[]{:T(128)S(6)} %select_n.98), kind=kLoop, calls=%fused_computation | loop fusion | flops 409600 | bytes 3276805 | tf_op jit(solution)/shard_map/jit(_where)/select_n | solution.py:438
  36.6 0.0 all-gather.7.cloned.1.call-update
  36.6 0.1 pad_maximum_fusion
  36.7 0.1 add.91
  36.8 0.1 broadcast_in_dim.69
  36.9 0.1 mul.31
  37.0 0.0 copy-done.4
  37.0 0.6 broadcast_in_dim.70.q_gain
  37.6 0.0 copy-done.5
  37.6 0.6 broadcast_in_dim.71.k_gain
  38.3 1.2 fusion
  39.4 4.9 %all-to-all-done.v_in = bf16[8,2,192,256]{3,2,1,0:T(8,128)(2,1)S(1)} async-done(((bf16[8,2,192,256]{3,2,1,0:T(8,128)(2,1)}), bf16[8,2,192,256]{3,2,1,0:T(8,128)(2,1)S(1)}, u32[]{:S(2)}, u32[]{:S(2)}) %all-to-all-start) | async-done | bytes 1572896 | tf_op jit(solution)/shard_map/all_to_all | solution.py:370
  44.4 0.0 copy-start.2
  44.4 0.9 collective-permute-start.2
  45.2 0.0 copy-done.3
  45.2 5.7 %norm_rope.1 = bf16[8,624,256]{2,1,0:T(8,128)(2,1)} custom-call(bf16[192,1280]{1,0:T(8,128)(2,1)} %bitcast.25, bf16[192,1280]{1,0:T(8,128)(2,1)} %bitcast.27, bf16[192,1280]{1,0:T(8,128)(2,1)} %bitcast.29, bf16[192,1280]{1,0:T(8,128)(2,1)} %bitcast.31, f32[192,128]{1,0:T(8,128)} %get-tuple-element.23.mine, f32[192,128]{1,0:T(8,128)} %copy-done.3, ...), custom_call_target="tpu_custom_call" | custom-call | flops 9830400 | bytes 5242880 | tf_op jit(solution)/shard_map/norm_rope/pallas_call | solution.py:49
  50.9 0.0 collective-permute-done.2.v_other
  50.9 0.0 copy-done.2
  50.9 3.6 %all-to-all-start.1 = ((bf16[8,624,256]{2,1,0:T(8,128)(2,1)}), bf16[8,624,256]{2,1,0:T(8,128)(2,1)S(1)}, u32[]{:S(2)}, u32[]{:S(2)}) async-start(bf16[8,624,256]{2,1,0:T(8,128)(2,1)} %norm_rope.1), calls=%async_computation.1 | async-start | bytes 5111808 | tf_op jit(solution)/shard_map/all_to_all | solution.py:370
  54.6 0.0 all-gather.5.cloned.1.call-start
  54.6 1.3 collective-permute-start.4
  55.9 1.6 collective-permute-start.5
  57.5 29.0 %all-to-all-done.1.mixed = bf16[8,624,256]{2,1,0:T(8,128)(2,1)S(1)} async-done(((bf16[8,624,256]{2,1,0:T(8,128)(2,1)}), bf16[8,624,256]{2,1,0:T(8,128)(2,1)S(1)}, u32[]{:S(2)}, u32[]{:S(2)}) %all-to-all-start.1) | async-done | bytes 2555936 | tf_op jit(solution)/shard_map/all_to_all | solution.py:370
  86.5 0.0 copy-start.1
  86.5 0.8 collective-permute-start.3
  87.3 0.0 collective-permute-done.4
  87.3 0.0 collective-permute-done.5
  87.3 2.5 %add.95 = bf16[320,1280]{1,0:T(8,128)(2,1)} add(bf16[320,1280]{1,0:T(8,128)(2,1)} %collective-permute-done.4, bf16[320,1280]{1,0:T(8,128)(2,1)} %collective-permute-done.5) | non-fusion elementwise | flops 409600 | bytes 2457600 | tf_op jit(solution)/shard_map/add | solution.py:446
  89.9 0.0 all-gather.5.cloned.1.call-update
  89.9 2.0 %collective-permute-done.3.mixed_other = bf16[8,624,256]{2,1,0:T(8,128)(2,1)} collective-permute-done((bf16[8,624,256]{2,1,0:T(8,128)(2,1)S(1)}, bf16[8,624,256]{2,1,0:T(8,128)(2,1)}, u32[]{:S(2)}, u32[]{:S(2)}) %collective-permute-start.3) | collective-permute-done | bytes 2555936 | tf_op jit(solution)/shard_map/ppermute | solution.py:374
  91.9 0.0 copy-done.1
  91.9 19.7 %attend.1 = bf16[2,8,240,256]{3,2,1,0:T(8,128)(2,1)} custom-call(bf16[8,624,256]{2,1,0:T(8,128)(2,1)} %copy-done.1, bf16[8,624,256]{2,1,0:T(8,128)(2,1)} %collective-permute-done.3.mixed_other, bf16[8,2,192,256]{3,2,1,0:T(8,128)(2,1)} %copy-done.2, bf16[8,2,192,256]{3,2,1,0:T(8,128)(2,1)} %collective-permute-done.2.v_other), custom_call_target="tpu_custom_call" | custom-call | flops 12079595520 | bytes 14680064 | tf_op jit(solution)/shard_map/attend/pallas_call | solution.py:268
  111.6 13.5 %all-to-all-start.2 = ((bf16[16,240,256]{2,1,0:T(8,128)(2,1)}), bf16[16,240,256]{2,1,0:T(8,128)(2,1)S(1)}, u32[]{:S(2)}, u32[]{:S(2)}) async-start(bf16[16,240,256]{2,1,0:T(8,128)(2,1)} %bitcast.23), calls=%async_computation.2 | async-start | bytes 3932160 | tf_op jit(solution)/shard_map/all_to_all | solution.py:450
  125.1 0.0 all-gather.7.cloned.1.call-done
  125.2 1.2 collective-permute-start.7
  126.4 26.7 %all-to-all-done.2 = bf16[16,240,256]{2,1,0:T(8,128)(2,1)S(1)} async-done(((bf16[16,240,256]{2,1,0:T(8,128)(2,1)}), bf16[16,240,256]{2,1,0:T(8,128)(2,1)S(1)}, u32[]{:S(2)}, u32[]{:S(2)}) %all-to-all-start.2) | async-done | bytes 1966112 | tf_op jit(solution)/shard_map/all_to_all | solution.py:450
  153.1 0.0 copy-start
  153.1 0.0 all-gather.5.cloned.1.call-done
  153.1 2.3 %collective-permute-start.6 = (bf16[4,320,1280]{2,1,0:T(8,128)(2,1)}, bf16[4,320,1280]{2,1,0:T(8,128)(2,1)}, u32[]{:S(2)}, u32[]{:S(2)}) collective-permute-start(bf16[4,320,1280]{2,1,0:T(8,128)(2,1)} %bitcast.20), channel_id=1, source_target_pairs={{0,1},{1,0},{2,3},{3,2},{4,5},{5,4},{6,7},{7,6},{8,9},{9,8},{10,11... | collective-permute-start | bytes 9830408 | tf_op jit(solution)/shard_map/ppermute | solution.py:374
  155.5 0.0 collective-permute-done.7.refs_2_.refs_3_
  155.5 0.0 copy-done
  155.5 7.6 %project.2.refs_4_ = f32[384,2560]{1,0:T(8,128)} custom-call(s32[3]{0:T(128)} %pad_add_fusion.meta, bf16[2,8,240,256]{3,2,1,0:T(8,128)(2,1)} %bitcast.15, bf16[4,320,1280]{2,1,0:T(8,128)(2,1)} %bitcast.18, bf16[4,320,1280]{2,1,0:T(8,128)(2,1)} %bitcast.19, bf16[4,320,1280]{2,1,0:T(8,128)(2,1)} %collective-permute-done.7.refs_2_.refs_3_, ...), custom_call_target="tpu_custom_call" | custom-call | flops 2516582400 | bytes 12582912 | tf_op jit(solution)/shard_map/project/pallas_call | solution.py:344
  163.1 0.0 collective-permute-done.6.refs_2_.refs_3_
  163.1 8.0 %project.3 = (bf16[192,2560]{1,0:T(8,128)(2,1)}, bf16[192,2560]{1,0:T(8,128)(2,1)}) custom-call(s32[3]{0:T(128)} %pad_add_fusion.meta, bf16[2,8,240,256]{3,2,1,0:T(8,128)(2,1)} %bitcast.16, bf16[4,320,1280]{2,1,0:T(8,128)(2,1)} %bitcast.21, bf16[4,320,1280]{2,1,0:T(8,128)(2,1)} %bitcast.22, bf16[4,320,1280]{2,1,0:T(8,128)(2,1)} %collective-permute-done.6.refs_2_.refs_3_, ...), custom_call_target="tpu_custom_call" | custom-call | flops 2516582400 | bytes 12582912 | tf_op jit(solution)/shard_map/project/pallas_call | solution.py:344
  (4 shorter events, 0.0 us)
Async XLA Ops:
  8.4 14.6 %copy-start.6 = (s32[32]{0:T(128)S(1)}, s32[32]{0:T(128)}, u32[]{:S(2)}) copy-start(s32[32]{0:T(128)} %param.19) | copy-start | bytes 388
  12.0 22.1 %collective-permute-start = (bf16[320,1280]{1,0:T(8,128)(2,1)S(1)}, bf16[320,1280]{1,0:T(8,128)(2,1)S(1)}, u32[]{:S(2)}, u32[]{:S(2)}) collective-permute-start(bf16[320,1280]{1,0:T(8,128)(2,1)S(1)} %constant_dynamic-slice_fusion.1), channel_id=1, source_target_pairs={{0,96},{1,97},{2,98},{3,99},{4,100},{5,101},{6,102},{7,103},{8,104... | collective-permute-start | bytes 2457608 | tf_op jit(solution)/shard_map/ppermute | solution.py:388
  17.3 6.6 %collective-permute-start.1 = (f32[192,128]{1,0:T(8,128)}, f32[192,128]{1,0:T(8,128)S(1)}, u32[]{:S(2)}, u32[]{:S(2)}) collective-permute-start(f32[192,128]{1,0:T(8,128)} %get-tuple-element.23.mine), channel_id=1, source_target_pairs={{0,16},{16,0},{1,17},{17,1},{2,18},{18,2},{3,19},{19,3},{4,20},{20... | collective-permute-start | bytes 294920 | tf_op jit(solution)/shard_map/ppermute | solution.py:392
  17.8 19.2 %copy-start.4 = (f32[1280]{0:T(1024)S(1)}, f32[1280]{0:T(1024)}, u32[]{:S(2)}) copy-start(f32[1280]{0:T(1024)} %param.16) | copy-start | bytes 15364
  17.8 19.8 %copy-start.5 = (f32[1280]{0:T(1024)S(1)}, f32[1280]{0:T(1024)}, u32[]{:S(2)}) copy-start(f32[1280]{0:T(1024)} %param.17) | copy-start | bytes 15364
  17.8 26.6 %all-to-all-start = ((bf16[8,2,192,256]{3,2,1,0:T(8,128)(2,1)}), bf16[8,2,192,256]{3,2,1,0:T(8,128)(2,1)S(1)}, u32[]{:S(2)}, u32[]{:S(2)}) async-start(bf16[8,2,192,256]{3,2,1,0:T(8,128)(2,1)} %get-tuple-element.26), calls=%async_computation | async-start | bytes 3145728 | tf_op jit(solution)/shard_map/all_to_all | solution.py:370
  22.9 102.2 %all-gather.7.cloned.1.call-start = ((), (), s32[]{:S(2)}) async-start(), calls=%async_computation.4 | async-start | bytes 4096000 | tf_op jit(solution)/shard_map/all_gather | solution.py:439
  23.8 21.4 %copy-start.3 = (f32[192,128]{1,0:T(8,128)}, f32[192,128]{1,0:T(8,128)S(1)}, u32[]{:S(2)}) copy-start(f32[192,128]{1,0:T(8,128)S(1)} %collective-permute-done.1.theirs) | copy-start | bytes 294916
  44.4 6.6 %copy-start.2 = (bf16[8,2,192,256]{3,2,1,0:T(8,128)(2,1)}, bf16[8,2,192,256]{3,2,1,0:T(8,128)(2,1)S(1)}, u32[]{:S(2)}) copy-start(bf16[8,2,192,256]{3,2,1,0:T(8,128)(2,1)S(1)} %all-to-all-done.v_in) | copy-start | bytes 4718596
  44.4 6.6 %collective-permute-start.2 = (bf16[8,2,192,256]{3,2,1,0:T(8,128)(2,1)S(1)}, bf16[8,2,192,256]{3,2,1,0:T(8,128)(2,1)}, u32[]{:S(2)}, u32[]{:S(2)}) collective-permute-start(bf16[8,2,192,256]{3,2,1,0:T(8,128)(2,1)S(1)} %all-to-all-done.v_in), channel_id=1, source_target_pairs={{0,1},{1,0},{2,3},{3,2},{4,5},{5,4},{6,7},{7,6},{8,9},{9,8},{10,11... | collective-permute-start | bytes 4718600 | tf_op jit(solution)/shard_map/ppermute | solution.py:374
  50.9 35.6 %all-to-all-start.1 = ((bf16[8,624,256]{2,1,0:T(8,128)(2,1)}), bf16[8,624,256]{2,1,0:T(8,128)(2,1)S(1)}, u32[]{:S(2)}, u32[]{:S(2)}) async-start(bf16[8,624,256]{2,1,0:T(8,128)(2,1)} %norm_rope.1), calls=%async_computation.1 | async-start | bytes 5111808 | tf_op jit(solution)/shard_map/all_to_all | solution.py:370
  54.6 98.6 %all-gather.5.cloned.1.call-start = ((), (), s32[]{:S(2)}) async-start(), calls=%async_computation.3 | async-start | bytes 4096000 | tf_op jit(solution)/shard_map/all_gather | solution.py:446
  54.6 32.7 %collective-permute-start.4 = (bf16[320,1280]{1,0:T(8,128)(2,1)}, bf16[320,1280]{1,0:T(8,128)(2,1)}, u32[]{:S(2)}, u32[]{:S(2)}) collective-permute-start(bf16[320,1280]{1,0:T(8,128)(2,1)} %get-tuple-element.35), channel_id=1, source_target_pairs={{16,8},{17,9},{18,10},{19,11},{20,12},{21,13},{22,14},{23,15},{24,... | collective-permute-start | bytes 2457608 | tf_op jit(solution)/shard_map/ppermute | solution.py:388
  55.9 31.4 %collective-permute-start.5 = (bf16[320,1280]{1,0:T(8,128)(2,1)S(1)}, bf16[320,1280]{1,0:T(8,128)(2,1)}, u32[]{:S(2)}, u32[]{:S(2)}) collective-permute-start(bf16[320,1280]{1,0:T(8,128)(2,1)S(1)} %constant_dynamic-slice_fusion.1), channel_id=1, source_target_pairs={{16,104},{17,105},{18,106},{19,107},{20,108},{21,109},{22,110},{23... | collective-permute-start | bytes 2457608 | tf_op jit(solution)/shard_map/ppermute | solution.py:388
  86.5 5.4 %copy-start.1 = (bf16[8,624,256]{2,1,0:T(8,128)(2,1)}, bf16[8,624,256]{2,1,0:T(8,128)(2,1)S(1)}, u32[]{:S(2)}) copy-start(bf16[8,624,256]{2,1,0:T(8,128)(2,1)S(1)} %all-to-all-done.1.mixed) | copy-start | bytes 7667716
  86.5 5.4 %collective-permute-start.3 = (bf16[8,624,256]{2,1,0:T(8,128)(2,1)S(1)}, bf16[8,624,256]{2,1,0:T(8,128)(2,1)}, u32[]{:S(2)}, u32[]{:S(2)}) collective-permute-start(bf16[8,624,256]{2,1,0:T(8,128)(2,1)S(1)} %all-to-all-done.1.mixed), channel_id=1, source_target_pairs={{0,1},{1,0},{2,3},{3,2},{4,5},{5,4},{6,7},{7,6},{8,9},{9,8},{10,11... | collective-permute-start | bytes 7667720 | tf_op jit(solution)/shard_map/ppermute | solution.py:374
  111.6 41.5 %all-to-all-start.2 = ((bf16[16,240,256]{2,1,0:T(8,128)(2,1)}), bf16[16,240,256]{2,1,0:T(8,128)(2,1)S(1)}, u32[]{:S(2)}, u32[]{:S(2)}) async-start(bf16[16,240,256]{2,1,0:T(8,128)(2,1)} %bitcast.23), calls=%async_computation.2 | async-start | bytes 3932160 | tf_op jit(solution)/shard_map/all_to_all | solution.py:450
  125.2 30.3 %collective-permute-start.7 = (bf16[4,320,1280]{2,1,0:T(8,128)(2,1)}, bf16[4,320,1280]{2,1,0:T(8,128)(2,1)}, u32[]{:S(2)}, u32[]{:S(2)}) collective-permute-start(bf16[4,320,1280]{2,1,0:T(8,128)(2,1)} %bitcast.17), channel_id=1, source_target_pairs={{0,1},{1,0},{2,3},{3,2},{4,5},{5,4},{6,7},{7,6},{8,9},{9,8},{10,11... | collective-permute-start | bytes 9830408 | tf_op jit(solution)/shard_map/ppermute | solution.py:374
  153.1 2.4 %copy-start = (bf16[16,240,256]{2,1,0:T(8,128)(2,1)}, bf16[16,240,256]{2,1,0:T(8,128)(2,1)S(1)}, u32[]{:S(2)}) copy-start(bf16[16,240,256]{2,1,0:T(8,128)(2,1)S(1)} %all-to-all-done.2) | copy-start | bytes 5898244
  153.1 10.0 %collective-permute-start.6 = (bf16[4,320,1280]{2,1,0:T(8,128)(2,1)}, bf16[4,320,1280]{2,1,0:T(8,128)(2,1)}, u32[]{:S(2)}, u32[]{:S(2)}) collective-permute-start(bf16[4,320,1280]{2,1,0:T(8,128)(2,1)} %bitcast.20), channel_id=1, source_target_pairs={{0,1},{1,0},{2,3},{3,2},{4,5},{5,4},{6,7},{7,6},{8,9},{9,8},{10,11... | collective-permute-start | bytes 9830408 | tf_op jit(solution)/shard_map/ppermute | solution.py:374
Sparse Core Ops, SparseCore 0:
  36.8 54.6 all-gather.6
  93.7 45.0 all-gather.4

commit v6 on v5

--- a/solution.py
+++ b/solution.py
@@ -351,7 +351,7 @@
             out_specs=out_specs,
             scratch_shapes=[pltpu.VMEM((HEADS, 2 * ROWS, HEAD_DIM), BF16)],
         ),
-        compiler_params=params(60),
+        compiler_params=params(63),
         cost_estimate=cost(2 * 2 * ROWS * FEATURES * 2 * FEATURES, 12 * MIB),
         name="project",
     )(meta, parts, *operands)

time: 179 us -> 179 us (level)
  no operation moved by 1% of the time
where the time goes in v6:
time: 179 us; the launch traced here: 178 us
  waiting for transfers between devices  73 us (41%)
  Pallas kernels  44.7 us (25%)
  starting transfers between devices  36.3 us (20%)
  between operations  14.2 us (8%)
  other arithmetic  7.16 us (4%)
  local copies, waits for them, and re-layouts  2.71 us (2%)
    all_to_all x2, waiting for transfers between devices, to_chips(): lax.all_to_all(array, 'ctx', 0, 0, axis_index_groups=CORES, tiled=True)  34 us
    all_to_all x1, waiting for transfers between devices, on_device(): lax.all_to_all(results.reshape(2 * CHIPS, SLOT, 256), ('head', 'ctx'), 0,...  26.7 us
    pallas_call x1, Pallas kernels, attend(): pl.pallas_call(attend_kernel, grid=(1,), out_shape=outs, in_specs=[anywhe...  19.7 us
    pallas_call x2, Pallas kernels, project(): pl.pallas_call(functools.partial(project_kernel, last), out_shape=outs, g...  15.6 us
    all_to_all x1, starting transfers between devices, on_device(): lax.all_to_all(results.reshape(2 * CHIPS, SLOT, 256), ('head', 'ctx'), 0,...  13.5 us
    ppermute x3, waiting for transfers between devices, move(): return lax.ppermute(array, ('dp', 'head', 'ctx'), links)  10.3 us
    pallas_call x2, Pallas kernels, call(): pl.pallas_call(kernel, grid=(1,), out_shape=outs, in_specs=[SMEM] * scala...  9.33 us
    all_to_all x2, starting transfers between devices, to_chips(): lax.all_to_all(array, 'ctx', 0, 0, axis_index_groups=CORES, tiled=True)  8.77 us
  transfers between devices with their start and end apart: 13, of which 5 were waited for; matrix products, arithmetic and copies ran while one was open for 5% of the time, Pallas kernels for 19%

profile of v6, /device:TPU:1, one launch (start us, length us, event | category | flops | bytes accessed | tf_op | source)
XLA Modules:
  0.0 178.0 jit_solution(17545083995884007603)
XLA Ops:
  7.2 1.2 constant_dynamic-slice_fusion.1
  8.4 0.0 copy-start.5
  8.4 3.6 %prepare.1 = (bf16[8,2,192,256]{3,2,1,0:T(8,128)(2,1)}, f32[192,128]{1,0:T(8,128)}) custom-call(bf16[192,1280]{1,0:T(8,128)(2,1)} %bitcast.22, bf16[192,1280]{1,0:T(8,128)(2,1)} %bitcast.24, bf16[192,1280]{1,0:T(8,128)(2,1)} %bitcast.26, bf16[192,1280]{1,0:T(8,128)(2,1)} %bitcast.28, bf16[192,1280]{1,0:T(8,128)(2,1)} %bitcast.30, bf16[192,1280]{1,0:T(8,128)(2,1)} %bitcast.31), custom_call_target="tpu_custom_call" | custom-call | flops 1966080 | bytes 6291456 | tf_op jit(solution)/shard_map/prepare/pallas_call | solution.py:49
  12.0 5.3 %collective-permute-start = (bf16[320,1280]{1,0:T(8,128)(2,1)S(1)}, bf16[320,1280]{1,0:T(8,128)(2,1)S(1)}, u32[]{:S(2)}, u32[]{:S(2)}) collective-permute-start(bf16[320,1280]{1,0:T(8,128)(2,1)S(1)} %constant_dynamic-slice_fusion.1), channel_id=1, source_target_pairs={{0,96},{1,97},{2,98},{3,99},{4,100},{5,101},{6,102},{7,103},{8,104... | collective-permute-start | bytes 2457608 | tf_op jit(solution)/shard_map/ppermute | solution.py:388
  17.2 0.5 collective-permute-start.1
  17.8 0.0 copy-start.3
  17.8 0.0 copy-start.4
  17.8 5.1 %all-to-all-start = ((bf16[8,2,192,256]{3,2,1,0:T(8,128)(2,1)}), bf16[8,2,192,256]{3,2,1,0:T(8,128)(2,1)S(1)}, u32[]{:S(2)}, u32[]{:S(2)}) async-start(bf16[8,2,192,256]{3,2,1,0:T(8,128)(2,1)} %get-tuple-element.26), calls=%async_computation | async-start | bytes 3145728 | tf_op jit(solution)/shard_map/all_to_all | solution.py:370
  22.9 0.0 all-gather.7.cloned.1.call-start
  23.0 0.0 copy-done.5
  23.0 0.1 dynamic-slice_multiply_fusion
  23.1 0.1 iota_add_fusion
  23.2 0.7 pad_add_fusion.meta
  23.8 0.0 collective-permute-done.1.theirs
  23.8 0.0 copy-start.2
  23.8 10.2 %collective-permute-done = bf16[320,1280]{1,0:T(8,128)(2,1)S(1)} collective-permute-done((bf16[320,1280]{1,0:T(8,128)(2,1)S(1)}, bf16[320,1280]{1,0:T(8,128)(2,1)S(1)}, u32[]{:S(2)}, u32[]{:S(2)}) %collective-permute-start) | collective-permute-done | bytes 819232 | tf_op jit(solution)/shard_map/ppermute | solution.py:388
  34.1 2.5 %broadcast_select_fusion = (bf16[320,1280]{1,0:T(8,128)(2,1)}, bf16[320,1280]{1,0:T(8,128)(2,1)}) fusion(bf16[320,1280]{1,0:T(8,128)(2,1)S(1)} %collective-permute-done, pred[]{:T(512)S(6)} %eq.8, bf16[1280,1280]{1,0:T(8,128)(2,1)} %param.18, s32[]{:T(128)S(6)} %select_n.98), kind=kLoop, calls=%fused_computation | loop fusion | flops 409600 | bytes 3276805 | tf_op jit(solution)/shard_map/jit(_where)/select_n | solution.py:438
  36.6 0.0 all-gather.7.cloned.1.call-update
  36.6 0.1 pad_maximum_fusion
  36.7 0.1 add.91
  36.8 0.1 broadcast_in_dim.69
  36.8 0.1 mul.31
  37.0 0.0 copy-done.3
  37.0 0.6 broadcast_in_dim.70.q_gain
  37.6 0.0 copy-done.4
  37.6 0.6 broadcast_in_dim.71.k_gain
  38.2 1.2 fusion
  39.4 4.9 %all-to-all-done.v_in = bf16[8,2,192,256]{3,2,1,0:T(8,128)(2,1)S(1)} async-done(((bf16[8,2,192,256]{3,2,1,0:T(8,128)(2,1)}), bf16[8,2,192,256]{3,2,1,0:T(8,128)(2,1)S(1)}, u32[]{:S(2)}, u32[]{:S(2)}) %all-to-all-start) | async-done | bytes 1572896 | tf_op jit(solution)/shard_map/all_to_all | solution.py:370
  44.3 0.0 copy-start.1
  44.3 0.9 collective-permute-start.2
  45.2 0.0 copy-done.2
  45.2 5.7 %norm_rope.1 = bf16[8,624,256]{2,1,0:T(8,128)(2,1)} custom-call(bf16[192,1280]{1,0:T(8,128)(2,1)} %bitcast.23, bf16[192,1280]{1,0:T(8,128)(2,1)} %bitcast.25, bf16[192,1280]{1,0:T(8,128)(2,1)} %bitcast.27, bf16[192,1280]{1,0:T(8,128)(2,1)} %bitcast.29, f32[192,128]{1,0:T(8,128)} %get-tuple-element.23.mine, f32[192,128]{1,0:T(8,128)} %copy-done.2, ...), custom_call_target="tpu_custom_call" | custom-call | flops 9830400 | bytes 5242880 | tf_op jit(solution)/shard_map/norm_rope/pallas_call | solution.py:49
  50.9 0.0 collective-permute-done.2.v_other
  50.9 0.0 copy-done.1
  50.9 3.6 %all-to-all-start.1 = ((bf16[8,624,256]{2,1,0:T(8,128)(2,1)}), bf16[8,624,256]{2,1,0:T(8,128)(2,1)S(1)}, u32[]{:S(2)}, u32[]{:S(2)}) async-start(bf16[8,624,256]{2,1,0:T(8,128)(2,1)} %norm_rope.1), calls=%async_computation.1 | async-start | bytes 5111808 | tf_op jit(solution)/shard_map/all_to_all | solution.py:370
  54.6 0.0 all-gather.5.cloned.1.call-start
  54.6 1.3 collective-permute-start.4
  55.9 1.6 collective-permute-start.5
  57.5 29.0 %all-to-all-done.1.mixed = bf16[8,624,256]{2,1,0:T(8,128)(2,1)S(1)} async-done(((bf16[8,624,256]{2,1,0:T(8,128)(2,1)}), bf16[8,624,256]{2,1,0:T(8,128)(2,1)S(1)}, u32[]{:S(2)}, u32[]{:S(2)}) %all-to-all-start.1) | async-done | bytes 2555936 | tf_op jit(solution)/shard_map/all_to_all | solution.py:370
  86.5 0.0 copy-start
  86.5 0.8 collective-permute-start.3
  87.3 0.0 collective-permute-done.4
  87.3 0.0 collective-permute-done.5
  87.3 2.5 %add.95 = bf16[320,1280]{1,0:T(8,128)(2,1)} add(bf16[320,1280]{1,0:T(8,128)(2,1)} %collective-permute-done.4, bf16[320,1280]{1,0:T(8,128)(2,1)} %collective-permute-done.5) | non-fusion elementwise | flops 409600 | bytes 2457600 | tf_op jit(solution)/shard_map/add | solution.py:446
  89.9 0.0 all-gather.5.cloned.1.call-update
  89.9 2.0 %collective-permute-done.3.mixed_other = bf16[8,624,256]{2,1,0:T(8,128)(2,1)} collective-permute-done((bf16[8,624,256]{2,1,0:T(8,128)(2,1)S(1)}, bf16[8,624,256]{2,1,0:T(8,128)(2,1)}, u32[]{:S(2)}, u32[]{:S(2)}) %collective-permute-start.3) | collective-permute-done | bytes 2555936 | tf_op jit(solution)/shard_map/ppermute | solution.py:374
  91.9 0.0 copy-done
  91.9 19.7 %attend.1 = bf16[2,8,240,256]{3,2,1,0:T(8,128)(2,1)} custom-call(bf16[8,624,256]{2,1,0:T(8,128)(2,1)} %copy-done, bf16[8,624,256]{2,1,0:T(8,128)(2,1)} %collective-permute-done.3.mixed_other, bf16[8,2,192,256]{3,2,1,0:T(8,128)(2,1)} %copy-done.1, bf16[8,2,192,256]{3,2,1,0:T(8,128)(2,1)} %collective-permute-done.2.v_other), custom_call_target="tpu_custom_call" | custom-call | flops 12079595520 | bytes 14680064 | tf_op jit(solution)/shard_map/attend/pallas_call | solution.py:268
  111.6 13.5 %all-to-all-start.2 = ((bf16[16,240,256]{2,1,0:T(8,128)(2,1)}), bf16[16,240,256]{2,1,0:T(8,128)(2,1)}, u32[]{:S(2)}, u32[]{:S(2)}) async-start(bf16[16,240,256]{2,1,0:T(8,128)(2,1)} %bitcast.21), calls=%async_computation.2 | async-start | bytes 3932160 | tf_op jit(solution)/shard_map/all_to_all | solution.py:450
  125.1 0.0 all-gather.7.cloned.1.call-done
  125.1 1.3 collective-permute-start.7
  126.4 26.7 %all-to-all-done.2 = bf16[16,240,256]{2,1,0:T(8,128)(2,1)} async-done(((bf16[16,240,256]{2,1,0:T(8,128)(2,1)}), bf16[16,240,256]{2,1,0:T(8,128)(2,1)}, u32[]{:S(2)}, u32[]{:S(2)}) %all-to-all-start.2) | async-done | bytes 1966112 | tf_op jit(solution)/shard_map/all_to_all | solution.py:450
  153.1 0.0 all-gather.5.cloned.1.call-done
  153.1 2.4 %collective-permute-start.6 = (bf16[4,320,1280]{2,1,0:T(8,128)(2,1)}, bf16[4,320,1280]{2,1,0:T(8,128)(2,1)}, u32[]{:S(2)}, u32[]{:S(2)}) collective-permute-start(bf16[4,320,1280]{2,1,0:T(8,128)(2,1)} %bitcast.18), channel_id=1, source_target_pairs={{0,1},{1,0},{2,3},{3,2},{4,5},{5,4},{6,7},{7,6},{8,9},{9,8},{10,11... | collective-permute-start | bytes 9830408 | tf_op jit(solution)/shard_map/ppermute | solution.py:374
  155.5 0.0 collective-permute-done.7.refs_2_.refs_3_
  155.5 7.6 %project.2.refs_4_ = f32[384,2560]{1,0:T(8,128)} custom-call(s32[3]{0:T(128)} %pad_add_fusion.meta, bf16[2,8,240,256]{3,2,1,0:T(8,128)(2,1)} %bitcast.10.parts, bf16[4,320,1280]{2,1,0:T(8,128)(2,1)} %bitcast.16, bf16[4,320,1280]{2,1,0:T(8,128)(2,1)} %bitcast.17, bf16[4,320,1280]{2,1,0:T(8,128)(2,1)} %collective-permute-done.7.refs_2_.refs_3_, ...), custom_call_target="tpu_custom_call" | custom-call | flops 2516582400 | bytes 12582912 | tf_op jit(solution)/shard_map/project/pallas_call | solution.py:344
  163.1 0.0 collective-permute-done.6.refs_2_.refs_3_
  163.1 8.0 %project.3 = (bf16[192,2560]{1,0:T(8,128)(2,1)}, bf16[192,2560]{1,0:T(8,128)(2,1)}) custom-call(s32[3]{0:T(128)} %pad_add_fusion.meta, bf16[2,8,240,256]{3,2,1,0:T(8,128)(2,1)} %bitcast.10.parts, bf16[4,320,1280]{2,1,0:T(8,128)(2,1)} %bitcast.19, bf16[4,320,1280]{2,1,0:T(8,128)(2,1)} %bitcast.20, ...), custom_call_target="tpu_custom_call" | custom-call | flops 2516582400 | bytes 12582912 | tf_op jit(solution)/shard_map/project/pallas_call | solution.py:344
  (4 shorter events, 0.0 us)
Async XLA Ops:
  8.4 14.6 %copy-start.5 = (s32[32]{0:T(128)S(1)}, s32[32]{0:T(128)}, u32[]{:S(2)}) copy-start(s32[32]{0:T(128)} %param.19) | copy-start | bytes 388
  12.0 22.1 %collective-permute-start = (bf16[320,1280]{1,0:T(8,128)(2,1)S(1)}, bf16[320,1280]{1,0:T(8,128)(2,1)S(1)}, u32[]{:S(2)}, u32[]{:S(2)}) collective-permute-start(bf16[320,1280]{1,0:T(8,128)(2,1)S(1)} %constant_dynamic-slice_fusion.1), channel_id=1, source_target_pairs={{0,96},{1,97},{2,98},{3,99},{4,100},{5,101},{6,102},{7,103},{8,104... | collective-permute-start | bytes 2457608 | tf_op jit(solution)/shard_map/ppermute | solution.py:388
  17.2 6.6 %collective-permute-start.1 = (f32[192,128]{1,0:T(8,128)}, f32[192,128]{1,0:T(8,128)S(1)}, u32[]{:S(2)}, u32[]{:S(2)}) collective-permute-start(f32[192,128]{1,0:T(8,128)} %get-tuple-element.23.mine), channel_id=1, source_target_pairs={{0,16},{16,0},{1,17},{17,1},{2,18},{18,2},{3,19},{19,3},{4,20},{20... | collective-permute-start | bytes 294920 | tf_op jit(solution)/shard_map/ppermute | solution.py:392
  17.8 19.2 %copy-start.3 = (f32[1280]{0:T(1024)S(1)}, f32[1280]{0:T(1024)}, u32[]{:S(2)}) copy-start(f32[1280]{0:T(1024)} %param.16) | copy-start | bytes 15364
  17.8 19.8 %copy-start.4 = (f32[1280]{0:T(1024)S(1)}, f32[1280]{0:T(1024)}, u32[]{:S(2)}) copy-start(f32[1280]{0:T(1024)} %param.17) | copy-start | bytes 15364
  17.8 26.6 %all-to-all-start = ((bf16[8,2,192,256]{3,2,1,0:T(8,128)(2,1)}), bf16[8,2,192,256]{3,2,1,0:T(8,128)(2,1)S(1)}, u32[]{:S(2)}, u32[]{:S(2)}) async-start(bf16[8,2,192,256]{3,2,1,0:T(8,128)(2,1)} %get-tuple-element.26), calls=%async_computation | async-start | bytes 3145728 | tf_op jit(solution)/shard_map/all_to_all | solution.py:370
  22.9 102.2 %all-gather.7.cloned.1.call-start = ((), (), s32[]{:S(2)}) async-start(), calls=%async_computation.4 | async-start | bytes 4096000 | tf_op jit(solution)/shard_map/all_gather | solution.py:439
  23.8 21.4 %copy-start.2 = (f32[192,128]{1,0:T(8,128)}, f32[192,128]{1,0:T(8,128)S(1)}, u32[]{:S(2)}) copy-start(f32[192,128]{1,0:T(8,128)S(1)} %collective-permute-done.1.theirs) | copy-start | bytes 294916
  44.3 6.6 %copy-start.1 = (bf16[8,2,192,256]{3,2,1,0:T(8,128)(2,1)}, bf16[8,2,192,256]{3,2,1,0:T(8,128)(2,1)S(1)}, u32[]{:S(2)}) copy-start(bf16[8,2,192,256]{3,2,1,0:T(8,128)(2,1)S(1)} %all-to-all-done.v_in) | copy-start | bytes 4718596
  44.3 6.6 %collective-permute-start.2 = (bf16[8,2,192,256]{3,2,1,0:T(8,128)(2,1)S(1)}, bf16[8,2,192,256]{3,2,1,0:T(8,128)(2,1)}, u32[]{:S(2)}, u32[]{:S(2)}) collective-permute-start(bf16[8,2,192,256]{3,2,1,0:T(8,128)(2,1)S(1)} %all-to-all-done.v_in), channel_id=1, source_target_pairs={{0,1},{1,0},{2,3},{3,2},{4,5},{5,4},{6,7},{7,6},{8,9},{9,8},{10,11... | collective-permute-start | bytes 4718600 | tf_op jit(solution)/shard_map/ppermute | solution.py:374
  50.9 35.6 %all-to-all-start.1 = ((bf16[8,624,256]{2,1,0:T(8,128)(2,1)}), bf16[8,624,256]{2,1,0:T(8,128)(2,1)S(1)}, u32[]{:S(2)}, u32[]{:S(2)}) async-start(bf16[8,624,256]{2,1,0:T(8,128)(2,1)} %norm_rope.1), calls=%async_computation.1 | async-start | bytes 5111808 | tf_op jit(solution)/shard_map/all_to_all | solution.py:370
  54.6 98.5 %all-gather.5.cloned.1.call-start = ((), (), s32[]{:S(2)}) async-start(), calls=%async_computation.3 | async-start | bytes 4096000 | tf_op jit(solution)/shard_map/all_gather | solution.py:446
  54.6 32.7 %collective-permute-start.4 = (bf16[320,1280]{1,0:T(8,128)(2,1)}, bf16[320,1280]{1,0:T(8,128)(2,1)}, u32[]{:S(2)}, u32[]{:S(2)}) collective-permute-start(bf16[320,1280]{1,0:T(8,128)(2,1)} %get-tuple-element.35), channel_id=1, source_target_pairs={{16,8},{17,9},{18,10},{19,11},{20,12},{21,13},{22,14},{23,15},{24,... | collective-permute-start | bytes 2457608 | tf_op jit(solution)/shard_map/ppermute | solution.py:388
  55.9 31.4 %collective-permute-start.5 = (bf16[320,1280]{1,0:T(8,128)(2,1)S(1)}, bf16[320,1280]{1,0:T(8,128)(2,1)}, u32[]{:S(2)}, u32[]{:S(2)}) collective-permute-start(bf16[320,1280]{1,0:T(8,128)(2,1)S(1)} %constant_dynamic-slice_fusion.1), channel_id=1, source_target_pairs={{16,104},{17,105},{18,106},{19,107},{20,108},{21,109},{22,110},{23... | collective-permute-start | bytes 2457608 | tf_op jit(solution)/shard_map/ppermute | solution.py:388
  86.5 5.4 %copy-start = (bf16[8,624,256]{2,1,0:T(8,128)(2,1)}, bf16[8,624,256]{2,1,0:T(8,128)(2,1)S(1)}, u32[]{:S(2)}) copy-start(bf16[8,624,256]{2,1,0:T(8,128)(2,1)S(1)} %all-to-all-done.1.mixed) | copy-start | bytes 7667716
  86.5 5.4 %collective-permute-start.3 = (bf16[8,624,256]{2,1,0:T(8,128)(2,1)S(1)}, bf16[8,624,256]{2,1,0:T(8,128)(2,1)}, u32[]{:S(2)}, u32[]{:S(2)}) collective-permute-start(bf16[8,624,256]{2,1,0:T(8,128)(2,1)S(1)} %all-to-all-done.1.mixed), channel_id=1, source_target_pairs={{0,1},{1,0},{2,3},{3,2},{4,5},{5,4},{6,7},{7,6},{8,9},{9,8},{10,11... | collective-permute-start | bytes 7667720 | tf_op jit(solution)/shard_map/ppermute | solution.py:374
  111.6 41.5 %all-to-all-start.2 = ((bf16[16,240,256]{2,1,0:T(8,128)(2,1)}), bf16[16,240,256]{2,1,0:T(8,128)(2,1)}, u32[]{:S(2)}, u32[]{:S(2)}) async-start(bf16[16,240,256]{2,1,0:T(8,128)(2,1)} %bitcast.21), calls=%async_computation.2 | async-start | bytes 3932160 | tf_op jit(solution)/shard_map/all_to_all | solution.py:450
  125.1 30.3 %collective-permute-start.7 = (bf16[4,320,1280]{2,1,0:T(8,128)(2,1)}, bf16[4,320,1280]{2,1,0:T(8,128)(2,1)}, u32[]{:S(2)}, u32[]{:S(2)}) collective-permute-start(bf16[4,320,1280]{2,1,0:T(8,128)(2,1)} %bitcast.15), channel_id=1, source_target_pairs={{0,1},{1,0},{2,3},{3,2},{4,5},{5,4},{6,7},{7,6},{8,9},{9,8},{10,11... | collective-permute-start | bytes 9830408 | tf_op jit(solution)/shard_map/ppermute | solution.py:374
  153.1 10.0 %collective-permute-start.6 = (bf16[4,320,1280]{2,1,0:T(8,128)(2,1)}, bf16[4,320,1280]{2,1,0:T(8,128)(2,1)}, u32[]{:S(2)}, u32[]{:S(2)}) collective-permute-start(bf16[4,320,1280]{2,1,0:T(8,128)(2,1)} %bitcast.18), channel_id=1, source_target_pairs={{0,1},{1,0},{2,3},{3,2},{4,5},{5,4},{6,7},{7,6},{8,9},{9,8},{10,11... | collective-permute-start | bytes 9830408 | tf_op jit(solution)/shard_map/ppermute | solution.py:374
Sparse Core Ops, SparseCore 0:
  36.7 54.5 all-gather.6
  93.6 45.1 all-gather.4
